TPU v7x, 512 devices: a whole 4x4x16 slice. The times are simulated.
512 devices in a mesh: lat: 16 (over z_lo, y), lon: 32 (over z_hi, x, core).
Axes of the slice: x: 4, y: 4, z: 16 (z_hi: 4, z_lo: 4; z = z_hi * 4 + z_lo), core: 2. Of those that a mesh axis runs over, the one named last changes fastest.
Arguments:
- tracers: float32 [2, 24, 512, 4096], P(None, None, 'lat', 'lon'), may hold values from -6 to 6
- velocity: float32 [2, 24, 512, 4096], P(None, None, 'lat', 'lon'), may hold values from -6 to 6
- diffusivity: float32 [512, 4096], P('lat', 'lon'), may hold values from 0.05 to 5
- ocean_levels: int32 [512, 4096], P('lat', 'lon'), may hold values from 0 to 24, as said below
- surface_height: float32 [512, 4096], P('lat', 'lon'), may hold values from -6 to 6
- transport: float32 [2, 512, 4096], P(None, 'lat', 'lon'), may hold values from -6 to 6
- atm_flux: float32 [16, 4, 16384], P('lat', None, 'lon'), may hold values from -6 to 6
- send_rows: int32 [16, 32, 32, 64], P('lat', 'lon'), may hold values from 0 to 511
- src_owner: int32 [4, 512, 4096], P(None, 'lat', 'lon'), may hold values from 0 to 31
- src_slot: int32 [4, 512, 4096], P(None, 'lat', 'lon'), may hold values from 0 to 63
- xgrid_weights: float32 [4, 512, 4096], P(None, 'lat', 'lon'), may hold values from 0.1 to 1
- xgrid_count: int32 [512, 4096], P('lat', 'lon'), may hold values from 1 to 4
Outputs:
- tracers_out: float32 [2, 24, 512, 4096], P(None, None, 'lat', 'lon')
- height_out: float32 [512, 4096], P('lat', 'lon')
- transport_out: float32 [2, 512, 4096], P(None, 'lat', 'lon')
Inputs may be any that keep to these rules, and one draw needn't show every extreme that they name: `ocean_levels`: 0 marks a land column.
All inputs are finite; a program needn't handle non-finite values.
Results may differ from a plain program's by a relative error of at most 0.0001.
Values sent between devices are 32-bit elements; how exact they have to be, the bound alone decides.
No kernel may reach another device: no remote copies, remote signals or barrier semaphores. Data moves between devices by JAX's collectives and lax.ppermute only.
A program may use at most 64 MiB of HBM per device.

v0:
```python
import jax
import jax.numpy as jnp
from jax import lax
from jax.sharding import PartitionSpec as P

SUBSTEPS = 6


adv_rate = 0.1
heat_gain = 0.5
salt_gain = 0.5
wave_div = 0.5
wave_grad = 0.8
fresh_gain = 0.2
wind_gain = 0.2


def partner(shard, axis, bit):
    return lax.ppermute(shard, axis, [(i, i ^ 1 << bit) for i in range(lax.axis_size(axis))])


def with_halo(shard, sides, width, wrap):
    for axis, dim in sides:
        count, length = (lax.axis_size(axis), shard.shape[dim])
        up = [(i, (i + 1) % count) for i in range(count if wrap else count - 1)]
        down = [(j, i) for i, j in up]
        last = lax.slice_in_dim(shard, length - width, length, axis=dim)
        leading = lax.slice_in_dim(shard, 0, width, axis=dim)
        before = lax.ppermute(last, axis, up)
        after = lax.ppermute(leading, axis, down)
        shard = jnp.concatenate([before, shard, after], axis=dim)
    return shard


def shifted(shard, axis, by):
    count = lax.axis_size(axis)
    return lax.ppermute(shard, axis, [(i, (i + by) % count) for i in range(count)])


def passed_along(value, axis, steps):
    count = lax.axis_size(axis)
    leading, last = (max(0, -steps), min(count, count - steps))
    return lax.ppermute(value, axis, [(source, source + steps) for source in range(leading, last)])


def ocean_wetness(ocean_levels, depth_count):
    layer_ids = jnp.arange(depth_count, dtype=jnp.int32)[:, None, None]
    return (layer_ids < ocean_levels[None]).astype(jnp.float32)


def vertical_solve(forced, diffusivity, wetness):
    depth_count = forced.shape[1]
    couple = [diffusivity * wetness[layer + 1] for layer in range(depth_count - 1)]
    zero_plane = jnp.zeros_like(diffusivity)
    uppers = []
    rights = []
    for layer in range(depth_count):
        below_k = couple[layer] if layer < depth_count - 1 else zero_plane
        above_k = couple[layer - 1] if layer > 0 else zero_plane
        diag_val = 1.0 + above_k + below_k
        if layer == 0:
            pivot = diag_val
            right_val = forced[:, 0] / pivot
        else:
            pivot = diag_val + above_k * uppers[-1]
            right_val = (forced[:, layer] + above_k * rights[-1]) / pivot
        uppers.append(-below_k / pivot)
        rights.append(right_val)
    solved = [rights[-1]]
    for layer in range(depth_count - 2, -1, -1):
        solved.append(rights[layer] - uppers[layer] * solved[-1])
    return jnp.stack(solved[::-1], axis=1)


def unpack_stack(part, depth_count):
    values = part[: 2 * depth_count].reshape((2, depth_count) + part.shape[1:])
    layer_f = jnp.arange(depth_count, dtype=jnp.float32).reshape(
        (depth_count,) + (1,) * (part.ndim - 1)
    )
    wet_part = (layer_f < part[2 * depth_count][None]).astype(jnp.float32)
    return (values, wet_part)


def face_flux(speed, first_vals, first_wet, second_vals, second_wet):
    return speed * ((first_vals + second_vals) * 0.5) * (first_wet * second_wet)


def bit_order():
    count = lax.axis_size("lon").bit_length() - 1
    return list(range(count))


def fold_tracer(top_row):
    moved = top_row
    for bit_pos in bit_order():
        moved = partner(moved, "lon", bit_pos)
    return moved[:, ::-1]


def fold_height(top_row):
    moved = top_row
    for bit_pos in bit_order():
        moved = partner(moved, "lon", bit_pos)
    return moved[:, ::-1]


def gather_fluxes(atm_flux, send_rows, src_owner, src_slot, xgrid_weights, xgrid_count):
    atm_local = atm_flux[0]
    flux_count = atm_local.shape[0]
    rows_here = send_rows[0, 0]
    slot_count = rows_here.shape[1]
    picked = jnp.take(atm_local.T, rows_here, axis=0)
    packed = picked.reshape(rows_here.shape[0], slot_count * flux_count)
    received = lax.all_to_all(packed, "lon", split_axis=0, concat_axis=0, tiled=True)
    table = received.reshape(-1, flux_count).T
    picks = src_owner * slot_count + src_slot
    values = jnp.take(table, picks, axis=1)
    entry_ids = jnp.arange(src_owner.shape[0], dtype=jnp.int32)[:, None, None]
    used = (entry_ids < xgrid_count[None]).astype(jnp.float32) * xgrid_weights
    return jnp.sum(values * used[None], axis=1)


def per_device(
    tracers,
    velocity,
    diffusivity,
    ocean_levels,
    surface_height,
    transport,
    atm_flux,
    send_rows,
    src_owner,
    src_slot,
    xgrid_weights,
    xgrid_count,
):
    depth_count = tracers.shape[1]
    grid_rows = tracers.shape[2]
    grid_cols = tracers.shape[3]
    wetness = ocean_wetness(ocean_levels, depth_count)
    fluxes = gather_fluxes(atm_flux, send_rows, src_owner, src_slot, xgrid_weights, xgrid_count)
    top_lat = lax.axis_index("lat") == lax.axis_size("lat") - 1
    level_f = ocean_levels.astype(jnp.float32)
    stack = jnp.concatenate(
        [tracers.reshape(2 * depth_count, grid_rows, grid_cols), level_f[None]], axis=0
    )
    folded = fold_tracer(stack[:, -1, :])
    row_ext = with_halo(stack, (("lat", 1),), 1, False)
    col_ext = with_halo(stack, (("lon", 2),), 1, True)
    north_rim = jnp.where(top_lat, folded, row_ext[:, -1, :])
    east_stack = jnp.concatenate([stack[:, :, 1:], col_ext[:, :, -1:]], axis=2)
    north_stack = jnp.concatenate([stack[:, 1:, :], north_rim[:, None, :]], axis=1)
    west_stack = jnp.concatenate([col_ext[:, :, :1], stack[:, :, :-1]], axis=2)
    south_stack = jnp.concatenate([row_ext[:, :1, :], stack[:, :-1, :]], axis=1)
    west_speed = shifted(velocity[0, :, :, -1], "lon", 1)
    south_speed = passed_along(velocity[1, :, -1, :], "lat", 1)
    u_west = jnp.concatenate([west_speed[:, :, None], velocity[0, :, :, :-1]], axis=2)
    v_south = jnp.concatenate([south_speed[:, None, :], velocity[1, :, :-1, :]], axis=1)
    east_vals, east_wet = unpack_stack(east_stack, depth_count)
    north_vals, north_wet = unpack_stack(north_stack, depth_count)
    west_vals, west_wet = unpack_stack(west_stack, depth_count)
    south_vals, south_wet = unpack_stack(south_stack, depth_count)
    east_flux = face_flux(velocity[0], tracers, wetness, east_vals, east_wet)
    north_flux = face_flux(velocity[1], tracers, wetness, north_vals, north_wet)
    west_flux = face_flux(u_west, west_vals, west_wet, tracers, wetness)
    south_flux = face_flux(v_south, south_vals, south_wet, tracers, wetness)
    advected = tracers - adv_rate * (east_flux - west_flux + (north_flux - south_flux))
    surface = jnp.stack([heat_gain * fluxes[0], -salt_gain * fluxes[1]]) * wetness[0]
    forced = advected.at[:, 0].add(surface)
    tracers_out = vertical_solve(forced, diffusivity, wetness)
    ocean_top = wetness[0]
    depth_frac = level_f / depth_count
    height = surface_height
    east_tr = transport[0]
    north_tr = transport[1]
    for substep in range(SUBSTEPS):
        west_edge = shifted(east_tr[:, -1], "lon", 1)
        south_edge = passed_along(north_tr[-1, :], "lat", 1)
        west_tr = jnp.concatenate([west_edge[:, None], east_tr[:, :-1]], axis=1)
        south_tr = jnp.concatenate([south_edge[None], north_tr[:-1]], axis=0)
        spread = east_tr - west_tr + (north_tr - south_tr)
        height = (height - wave_div * spread + fresh_gain * fluxes[1]) * ocean_top
        east_edge = shifted(height[:, 0], "lon", -1)
        north_edge = passed_along(height[0, :], "lat", -1)
        north_edge = jnp.where(top_lat, fold_height(height[-1:, :])[0], north_edge)
        east_h = jnp.concatenate([height[:, 1:], east_edge[:, None]], axis=1)
        north_h = jnp.concatenate([height[1:], north_edge[None]], axis=0)
        east_tr = (
            east_tr - wave_grad * depth_frac * (east_h - height) + wind_gain * fluxes[2]
        ) * ocean_top
        north_tr = (
            north_tr - wave_grad * depth_frac * (north_h - height) + wind_gain * fluxes[3]
        ) * ocean_top
    return (tracers_out, height, jnp.stack([east_tr, north_tr]))


def solution(mesh):
    return jax.shard_map(
        per_device,
        mesh=mesh,
        in_specs=(
            P(None, None, "lat", "lon"),
            P(None, None, "lat", "lon"),
            P("lat", "lon"),
            P("lat", "lon"),
            P("lat", "lon"),
            P(None, "lat", "lon"),
            P("lat", None, "lon"),
            P("lat", "lon", None, None),
            P(None, "lat", "lon"),
            P(None, "lat", "lon"),
            P(None, "lat", "lon"),
            P("lat", "lon"),
        ),
        out_specs=(P(None, None, "lat", "lon"), P("lat", "lon"), P(None, "lat", "lon")),
        check_vma=False,
    )
```

profile of v0, /device:TPU:32, one launch (start us, length us, event | category | flops | bytes accessed | tf_op | source)
XLA Modules:
  0.0 480.7 jit_solution(14374161670248361056)
XLA Ops:
  3.0 5.5 %gather_fusion = f32[2048,4]{1,0:T(8,128)S(1)} fusion(f32[512,4]{1,0:T(8,128)S(1)} %bitcast.302, s32[2048]{0:T(1024)S(1)} %broadcast_clamp_fusion.1), kind=kCustom, calls=%fused_computation | custom fusion | bytes 73728 | tf_op jit(solution)/shard_map/jit(_take)/gather | solution.py:112
  10.0 17.0 %all-to-all-start = ((f32[32,1,256]{2,1,0:T(1,128)}), f32[32,1,256]{2,1,0:T(1,128)S(1)}, u32[]{:S(2)}, u32[]{:S(2)}) async-start(f32[32,1,256]{2,1,0:T(1,128)} %copy.181), calls=%async_computation | async-start | bytes 65536 | tf_op jit(solution)/shard_map/all_to_all | solution.py:114
  45.0 54.4 %gather_fusion.1 = f32[16384,4]{1,0:T(8,128)} fusion(f32[4,2048]{0,1:T(8,128)S(1)} %bitcast.310, s32[16384]{0:T(1024)S(1)} %broadcast_clamp_fusion), kind=kCustom, calls=%fused_computation.1 | custom fusion | bytes 589824 | tf_op jit(solution)/shard_map/jit(_take)/gather | solution.py:117
  99.4 7.0 %multiply_reduce_fusion = f32[32,128,4]{2,1,0:T(8,128)S(1)} fusion(f32[4,32,128,4]{3,2,1,0:T(8,128)} %bitcast.311, f32[4,32,128]{2,1,0:T(8,128)S(1)} %fusion.15, pred[4,32,128]{2,1,0:T(8,128)(4,1)S(1)} %get-tuple-element.99), kind=kLoop, calls=%fused_computation.2 | loop fusion | flops 180224 | bytes 409600 | tf_op jit(solution)/shard_map/reduce_sum | solution.py:120
  106.4 5.0 %fusion = (f32[32,128]{1,0:T(8,128)S(1)}, f32[32,128]{1,0:T(8,128)S(1)}, f32[32,128]{1,0:T(8,128)S(1)}, f32[32,128]{1,0:T(8,128)}, f32[32,128]{1,0:T(8,128)}) fusion(f32[4,32,128]{0,2,1:T(8,128)S(1)} %bitcast.303), kind=kLoop, calls=%fused_computation.11 | loop fusion | flops 20480 | bytes 147456 | tf_op jit(solution)/shard_map/mul | solution.py:192
  120.0 8.1 %collective-permute-start.17 = (f32[1,128]{1,0:T(1,128)S(1)}, f32[1,128]{1,0:T(1,128)S(1)}, u32[]{:S(2)}, u32[]{:S(2)}) collective-permute-start(f32[1,128]{1,0:T(1,128)S(1)} %collective-permute-done.16), channel_id=1, source_target_pairs={{0,4},{1,5},{2,6},{3,7},{4,0},{5,1},{6,2},{7,3},{8,12},{9,13},{10,... | collective-permute-start | bytes 1544 | tf_op jit(solution)/shard_map/ppermute | solution.py:19
  129.6 7.3 %collective-permute-start.18 = (f32[1,128]{1,0:T(1,128)S(1)}, f32[1,128]{1,0:T(1,128)S(1)}, u32[]{:S(2)}, u32[]{:S(2)}) collective-permute-start(f32[1,128]{1,0:T(1,128)S(1)} %collective-permute-done.17), channel_id=1, source_target_pairs={{0,8},{1,9},{2,10},{3,11},{4,12},{5,13},{6,14},{7,15},{8,0},{9,1},... | collective-permute-start | bytes 1544 | tf_op jit(solution)/shard_map/ppermute | solution.py:19
  138.5 4.5 collective-permute-start.20
  142.9 5.4 %collective-permute-start.19 = (f32[1,128]{1,0:T(1,128)S(1)}, f32[1,128]{1,0:T(1,128)S(1)}, u32[]{:S(2)}, u32[]{:S(2)}) collective-permute-start(f32[1,128]{1,0:T(1,128)S(1)} %collective-permute-done.18), channel_id=1, source_target_pairs={{0,16},{1,17},{2,18},{3,19},{4,20},{5,21},{6,22},{7,23},{8,24},{9,... | collective-permute-start | bytes 1544 | tf_op jit(solution)/shard_map/ppermute | solution.py:19
  148.4 4.6 collective-permute-start.13
  165.2 6.8 %collective-permute-done.14 = f32[32]{0:T(128)S(1)} collective-permute-done((f32[32]{0:T(128)S(1)}, f32[32]{0:T(128)S(1)}, u32[]{:S(2)}, u32[]{:S(2)}) %collective-permute-start.14) | collective-permute-done | bytes 160 | tf_op jit(solution)/shard_map/ppermute | solution.py:37
  183.0 7.2 %collective-permute-start = (f32[49,32,1]{0,1,2:T(8,128)S(1)}, f32[49,32,1]{0,1,2:T(8,128)S(1)}, u32[]{:S(2)}, u32[]{:S(2)}) collective-permute-start(f32[49,32,1]{0,1,2:T(8,128)S(1)} %copy.169), channel_id=1, source_target_pairs={{1,0},{2,1},{3,2},{4,3},{5,4},{6,5},{7,6},{8,7},{9,8},{10,9},{11,1... | collective-permute-start | bytes 18824 | tf_op jit(solution)/shard_map/ppermute | solution.py:30
  210.2 6.0 %collective-permute-start.29 = (f32[128]{0:T(128)S(1)}, f32[128]{0:T(128)S(1)}, u32[]{:S(2)}, u32[]{:S(2)}) collective-permute-start(f32[128]{0:T(128)S(1)} %get-tuple-element.165), channel_id=1, source_target_pairs={{32,0},{64,32},{96,64},{128,96},{160,128},{192,160},{224,192},{256... | collective-permute-start | bytes 1544 | tf_op jit(solution)/shard_map/ppermute | solution.py:43
  216.3 9.0 %collective-permute-start.28 = (f32[1,128]{1,0:T(1,128)S(1)}, f32[1,128]{1,0:T(1,128)S(1)}, u32[]{:S(2)}, u32[]{:S(2)}) collective-permute-start(f32[1,128]{1,0:T(1,128)S(1)} %collective-permute-done.27), channel_id=1, source_target_pairs={{0,16},{1,17},{2,18},{3,19},{4,20},{5,21},{6,22},{7,23},{8,24},{9,... | collective-permute-start | bytes 1544 | tf_op jit(solution)/shard_map/ppermute | solution.py:19
  241.1 6.1 %collective-permute-done.23 = f32[32]{0:T(128)S(1)} collective-permute-done((f32[32]{0:T(128)S(1)}, f32[32]{0:T(128)S(1)}, u32[]{:S(2)}, u32[]{:S(2)}) %collective-permute-start.23) | collective-permute-done | bytes 160 | tf_op jit(solution)/shard_map/ppermute | solution.py:37
  262.3 5.4 %collective-permute-start.35 = (f32[1,128]{1,0:T(1,128)S(1)}, f32[1,128]{1,0:T(1,128)S(1)}, u32[]{:S(2)}, u32[]{:S(2)}) collective-permute-start(f32[1,128]{1,0:T(1,128)S(1)} %collective-permute-done.34), channel_id=1, source_target_pairs={{0,4},{1,5},{2,6},{3,7},{4,0},{5,1},{6,2},{7,3},{8,12},{9,13},{10,... | collective-permute-start | bytes 1544 | tf_op jit(solution)/shard_map/ppermute | solution.py:19
  273.0 5.5 %collective-permute-start.36 = (f32[1,128]{1,0:T(1,128)S(1)}, f32[1,128]{1,0:T(1,128)S(1)}, u32[]{:S(2)}, u32[]{:S(2)}) collective-permute-start(f32[1,128]{1,0:T(1,128)S(1)} %collective-permute-done.35), channel_id=1, source_target_pairs={{0,8},{1,9},{2,10},{3,11},{4,12},{5,13},{6,14},{7,15},{8,0},{9,1},... | collective-permute-start | bytes 1544 | tf_op jit(solution)/shard_map/ppermute | solution.py:19
  279.1 6.8 %collective-permute-start.7 = (f32[49,128]{1,0:T(8,128)S(1)}, f32[49,128]{1,0:T(8,128)S(1)}, u32[]{:S(2)}, u32[]{:S(2)}) collective-permute-start(f32[49,128]{1,0:T(8,128)S(1)} %collective-permute-done.6), channel_id=1, source_target_pairs={{0,16},{1,17},{2,18},{3,19},{4,20},{5,21},{6,22},{7,23},{8,24},{9,... | collective-permute-start | bytes 75272 | tf_op jit(solution)/shard_map/ppermute | solution.py:19
  286.0 6.0 %collective-permute-start.38 = (f32[128]{0:T(128)S(1)}, f32[128]{0:T(128)S(1)}, u32[]{:S(2)}, u32[]{:S(2)}) collective-permute-start(f32[128]{0:T(128)S(1)} %get-tuple-element.163), channel_id=1, source_target_pairs={{32,0},{64,32},{96,64},{128,96},{160,128},{192,160},{224,192},{256... | collective-permute-start | bytes 1544 | tf_op jit(solution)/shard_map/ppermute | solution.py:43
  292.0 7.7 %collective-permute-start.37 = (f32[1,128]{1,0:T(1,128)S(1)}, f32[1,128]{1,0:T(1,128)S(1)}, u32[]{:S(2)}, u32[]{:S(2)}) collective-permute-start(f32[1,128]{1,0:T(1,128)S(1)} %collective-permute-done.36), channel_id=1, source_target_pairs={{0,16},{1,17},{2,18},{3,19},{4,20},{5,21},{6,22},{7,23},{8,24},{9,... | collective-permute-start | bytes 1544 | tf_op jit(solution)/shard_map/ppermute | solution.py:19
  311.1 8.9 %collective-permute-done.32 = f32[32]{0:T(128)S(1)} collective-permute-done((f32[32]{0:T(128)S(1)}, f32[32]{0:T(128)S(1)}, u32[]{:S(2)}, u32[]{:S(2)}) %collective-permute-start.32) | collective-permute-done | bytes 160 | tf_op jit(solution)/shard_map/ppermute | solution.py:37
  340.8 6.0 %collective-permute-start.47 = (f32[128]{0:T(128)}, f32[128]{0:T(128)S(1)}, u32[]{:S(2)}, u32[]{:S(2)}) collective-permute-start(f32[128]{0:T(128)} %get-tuple-element.161), channel_id=1, source_target_pairs={{32,0},{64,32},{96,64},{128,96},{160,128},{192,160},{224,192},{256... | collective-permute-start | bytes 1544 | tf_op jit(solution)/shard_map/ppermute | solution.py:43
  346.9 8.1 %collective-permute-start.46 = (f32[1,128]{1,0:T(1,128)}, f32[1,128]{1,0:T(1,128)S(1)}, u32[]{:S(2)}, u32[]{:S(2)}) collective-permute-start(f32[1,128]{1,0:T(1,128)} %collective-permute-done.45), channel_id=1, source_target_pairs={{0,16},{1,17},{2,18},{3,19},{4,20},{5,21},{6,22},{7,23},{8,24},{9,... | collective-permute-start | bytes 1544 | tf_op jit(solution)/shard_map/ppermute | solution.py:19
  371.3 5.4 %collective-permute-done.41 = f32[32]{0:T(128)S(1)} collective-permute-done((f32[32]{0:T(128)S(1)}, f32[32]{0:T(128)S(1)}, u32[]{:S(2)}, u32[]{:S(2)}) %collective-permute-start.41) | collective-permute-done | bytes 160 | tf_op jit(solution)/shard_map/ppermute | solution.py:37
  394.3 5.5 %collective-permute-start.54 = (f32[1,128]{1,0:T(1,128)S(1)}, f32[1,128]{1,0:T(1,128)S(1)}, u32[]{:S(2)}, u32[]{:S(2)}) collective-permute-start(f32[1,128]{1,0:T(1,128)S(1)} %collective-permute-done.53), channel_id=1, source_target_pairs={{0,8},{1,9},{2,10},{3,11},{4,12},{5,13},{6,14},{7,15},{8,0},{9,1},... | collective-permute-start | bytes 1544 | tf_op jit(solution)/shard_map/ppermute | solution.py:19
  400.5 6.0 %collective-permute-start.56 = (f32[128]{0:T(128)S(1)}, f32[128]{0:T(128)S(1)}, u32[]{:S(2)}, u32[]{:S(2)}) collective-permute-start(f32[128]{0:T(128)S(1)} %get-tuple-element.159), channel_id=1, source_target_pairs={{32,0},{64,32},{96,64},{128,96},{160,128},{192,160},{224,192},{256... | collective-permute-start | bytes 1544 | tf_op jit(solution)/shard_map/ppermute | solution.py:43
  406.6 7.7 %collective-permute-start.55 = (f32[1,128]{1,0:T(1,128)S(1)}, f32[1,128]{1,0:T(1,128)S(1)}, u32[]{:S(2)}, u32[]{:S(2)}) collective-permute-start(f32[1,128]{1,0:T(1,128)S(1)} %collective-permute-done.54), channel_id=1, source_target_pairs={{0,16},{1,17},{2,18},{3,19},{4,20},{5,21},{6,22},{7,23},{8,24},{9,... | collective-permute-start | bytes 1544 | tf_op jit(solution)/shard_map/ppermute | solution.py:19
  426.5 8.2 %collective-permute-done.50 = f32[32]{0:T(128)S(1)} collective-permute-done((f32[32]{0:T(128)S(1)}, f32[32]{0:T(128)S(1)}, u32[]{:S(2)}, u32[]{:S(2)}) %collective-permute-start.50) | collective-permute-done | bytes 160 | tf_op jit(solution)/shard_map/ppermute | solution.py:37
  445.9 5.0 %collective-permute-done.61 = f32[1,128]{1,0:T(1,128)S(1)} collective-permute-done((f32[1,128]{1,0:T(1,128)S(1)}, f32[1,128]{1,0:T(1,128)S(1)}, u32[]{:S(2)}, u32[]{:S(2)}) %collective-permute-start.61) | collective-permute-done | bytes 544 | tf_op jit(solution)/shard_map/ppermute | solution.py:19
  457.7 6.0 %collective-permute-start.64 = (f32[128]{0:T(128)S(1)}, f32[128]{0:T(128)S(1)}, u32[]{:S(2)}, u32[]{:S(2)}) collective-permute-start(f32[128]{0:T(128)S(1)} %get-tuple-element.157), channel_id=1, source_target_pairs={{32,0},{64,32},{96,64},{128,96},{160,128},{192,160},{224,192},{256... | collective-permute-start | bytes 1544 | tf_op jit(solution)/shard_map/ppermute | solution.py:43
  463.7 7.3 %collective-permute-start.63 = (f32[1,128]{1,0:T(1,128)S(1)}, f32[1,128]{1,0:T(1,128)S(1)}, u32[]{:S(2)}, u32[]{:S(2)}) collective-permute-start(f32[1,128]{1,0:T(1,128)S(1)} %collective-permute-done.62), channel_id=1, source_target_pairs={{0,16},{1,17},{2,18},{3,19},{4,20},{5,21},{6,22},{7,23},{8,24},{9,... | collective-permute-start | bytes 1544 | tf_op jit(solution)/shard_map/ppermute | solution.py:19
  471.2 6.7 %collective-permute-done.63 = f32[1,128]{1,0:T(1,128)S(1)} collective-permute-done((f32[1,128]{1,0:T(1,128)S(1)}, f32[1,128]{1,0:T(1,128)S(1)}, u32[]{:S(2)}, u32[]{:S(2)}) %collective-permute-start.63) | collective-permute-done | bytes 544 | tf_op jit(solution)/shard_map/ppermute | solution.py:19
  (432 shorter events, 211.9 us)
Async XLA Ops:
  10.0 33.8 %all-to-all-start = ((f32[32,1,256]{2,1,0:T(1,128)}), f32[32,1,256]{2,1,0:T(1,128)S(1)}, u32[]{:S(2)}, u32[]{:S(2)}) async-start(f32[32,1,256]{2,1,0:T(1,128)} %copy.181), calls=%async_computation | async-start | bytes 65536 | tf_op jit(solution)/shard_map/all_to_all | solution.py:114
  27.3 16.5 %collective-permute-start.11 = (f32[32]{0:T(128)S(1)}, f32[32]{0:T(128)S(1)}, u32[]{:S(2)}, u32[]{:S(2)}) collective-permute-start(f32[32]{0:T(128)S(1)} %slice_reduce_fusion.11), channel_id=1, source_target_pairs={{0,1},{1,2},{2,3},{3,4},{4,5},{5,6},{6,7},{7,8},{8,9},{9,10},{10,1... | collective-permute-start | bytes 392 | tf_op jit(solution)/shard_map/ppermute | solution.py:37
  29.5 82.0 %collective-permute-start.12 = (f32[128]{0:T(128)S(1)}, f32[128]{0:T(128)S(1)}, u32[]{:S(2)}, u32[]{:S(2)}) collective-permute-start(f32[128]{0:T(128)S(1)} %slice_bitcast_fusion.39), channel_id=1, source_target_pairs={{0,32},{32,64},{64,96},{96,128},{128,160},{160,192},{192,224},{224... | collective-permute-start | bytes 1544 | tf_op jit(solution)/shard_map/ppermute | solution.py:43
  33.7 234.0 %collective-permute-start.9 = (f32[49,1,128]{2,1,0:T(1,128)}, f32[49,1,128]{2,1,0:T(1,128)}, u32[]{:S(2)}, u32[]{:S(2)}) collective-permute-start(f32[49,1,128]{2,1,0:T(1,128)} %get-tuple-element.106), channel_id=1, source_target_pairs={{0,32},{32,64},{64,96},{96,128},{128,160},{160,192},{192,224},{224... | collective-permute-start | bytes 75272 | tf_op jit(solution)/shard_map/ppermute | solution.py:29
  38.0 215.4 %collective-permute-start.3 = (f32[49,128]{1,0:T(8,128)S(1)}, f32[49,128]{1,0:T(8,128)}, u32[]{:S(2)}, u32[]{:S(2)}) collective-permute-start(f32[49,128]{1,0:T(8,128)S(1)} %bitcast.332), channel_id=1, source_target_pairs={{0,1},{1,0},{2,3},{3,2},{4,5},{5,4},{6,7},{7,6},{8,9},{9,8},{10,11... | collective-permute-start | bytes 75272 | tf_op jit(solution)/shard_map/ppermute | solution.py:19
  129.6 13.4 %collective-permute-start.18 = (f32[1,128]{1,0:T(1,128)S(1)}, f32[1,128]{1,0:T(1,128)S(1)}, u32[]{:S(2)}, u32[]{:S(2)}) collective-permute-start(f32[1,128]{1,0:T(1,128)S(1)} %collective-permute-done.17), channel_id=1, source_target_pairs={{0,8},{1,9},{2,10},{3,11},{4,12},{5,13},{6,14},{7,15},{8,0},{9,1},... | collective-permute-start | bytes 1544 | tf_op jit(solution)/shard_map/ppermute | solution.py:19
  138.5 18.7 %collective-permute-start.20 = (f32[128]{0:T(128)S(1)}, f32[128]{0:T(128)S(1)}, u32[]{:S(2)}, u32[]{:S(2)}) collective-permute-start(f32[128]{0:T(128)S(1)} %get-tuple-element.167), channel_id=1, source_target_pairs={{32,0},{64,32},{96,64},{128,96},{160,128},{192,160},{224,192},{256... | collective-permute-start | bytes 1544 | tf_op jit(solution)/shard_map/ppermute | solution.py:43
  142.9 14.1 %collective-permute-start.19 = (f32[1,128]{1,0:T(1,128)S(1)}, f32[1,128]{1,0:T(1,128)S(1)}, u32[]{:S(2)}, u32[]{:S(2)}) collective-permute-start(f32[1,128]{1,0:T(1,128)S(1)} %collective-permute-done.18), channel_id=1, source_target_pairs={{0,16},{1,17},{2,18},{3,19},{4,20},{5,21},{6,22},{7,23},{8,24},{9,... | collective-permute-start | bytes 1544 | tf_op jit(solution)/shard_map/ppermute | solution.py:19
  154.3 41.0 %collective-permute-start.1 = (f32[49,32,1]{0,1,2:T(8,128)S(1)}, f32[49,32,1]{0,1,2:T(8,128)S(1)}, u32[]{:S(2)}, u32[]{:S(2)}) collective-permute-start(f32[49,32,1]{0,1,2:T(8,128)S(1)} %copy.171), channel_id=1, source_target_pairs={{0,1},{1,2},{2,3},{3,4},{4,5},{5,6},{6,7},{7,8},{8,9},{9,10},{10,1... | collective-permute-start | bytes 18824 | tf_op jit(solution)/shard_map/ppermute | solution.py:29
  158.6 15.5 %collective-permute-start.21 = (f32[128]{0:T(128)S(1)}, f32[128]{0:T(128)S(1)}, u32[]{:S(2)}, u32[]{:S(2)}) collective-permute-start(f32[128]{0:T(128)S(1)} %slice_bitcast_fusion.37), channel_id=1, source_target_pairs={{0,32},{32,64},{64,96},{96,128},{128,160},{160,192},{192,224},{224... | collective-permute-start | bytes 1544 | tf_op jit(solution)/shard_map/ppermute | solution.py:43
  175.4 15.9 %collective-permute-start.24 = (f32[1,128]{1,0:T(1,128)S(1)}, f32[1,128]{1,0:T(1,128)S(1)}, u32[]{:S(2)}, u32[]{:S(2)}) collective-permute-start(f32[1,128]{1,0:T(1,128)S(1)} %get-tuple-element.164), channel_id=1, source_target_pairs={{0,1},{1,0},{2,3},{3,2},{4,5},{5,4},{6,7},{7,6},{8,9},{9,8},{10,11... | collective-permute-start | bytes 1544 | tf_op jit(solution)/shard_map/ppermute | solution.py:19
  183.0 18.1 %collective-permute-start = (f32[49,32,1]{0,1,2:T(8,128)S(1)}, f32[49,32,1]{0,1,2:T(8,128)S(1)}, u32[]{:S(2)}, u32[]{:S(2)}) collective-permute-start(f32[49,32,1]{0,1,2:T(8,128)S(1)} %copy.169), channel_id=1, source_target_pairs={{1,0},{2,1},{3,2},{4,3},{5,4},{6,5},{7,6},{8,7},{9,8},{10,9},{11,1... | collective-permute-start | bytes 18824 | tf_op jit(solution)/shard_map/ppermute | solution.py:30
  203.8 12.4 %collective-permute-start.27 = (f32[1,128]{1,0:T(1,128)S(1)}, f32[1,128]{1,0:T(1,128)S(1)}, u32[]{:S(2)}, u32[]{:S(2)}) collective-permute-start(f32[1,128]{1,0:T(1,128)S(1)} %collective-permute-done.26), channel_id=1, source_target_pairs={{0,8},{1,9},{2,10},{3,11},{4,12},{5,13},{6,14},{7,15},{8,0},{9,1},... | collective-permute-start | bytes 1544 | tf_op jit(solution)/shard_map/ppermute | solution.py:19
  210.2 20.5 %collective-permute-start.29 = (f32[128]{0:T(128)S(1)}, f32[128]{0:T(128)S(1)}, u32[]{:S(2)}, u32[]{:S(2)}) collective-permute-start(f32[128]{0:T(128)S(1)} %get-tuple-element.165), channel_id=1, source_target_pairs={{32,0},{64,32},{96,64},{128,96},{160,128},{192,160},{224,192},{256... | collective-permute-start | bytes 1544 | tf_op jit(solution)/shard_map/ppermute | solution.py:43
  216.3 14.3 %collective-permute-start.28 = (f32[1,128]{1,0:T(1,128)S(1)}, f32[1,128]{1,0:T(1,128)S(1)}, u32[]{:S(2)}, u32[]{:S(2)}) collective-permute-start(f32[1,128]{1,0:T(1,128)S(1)} %collective-permute-done.27), channel_id=1, source_target_pairs={{0,16},{1,17},{2,18},{3,19},{4,20},{5,21},{6,22},{7,23},{8,24},{9,... | collective-permute-start | bytes 1544 | tf_op jit(solution)/shard_map/ppermute | solution.py:19
  228.6 94.7 %collective-permute-start.8 = (f32[49,1,128]{2,0,1:T(8,128)}, f32[49,1,128]{2,0,1:T(8,128)}, u32[]{:S(2)}, u32[]{:S(2)}) collective-permute-start(f32[49,1,128]{2,0,1:T(8,128)} %copy.196), channel_id=1, source_target_pairs={{32,0},{64,32},{96,64},{128,96},{160,128},{192,160},{224,192},{256... | collective-permute-start | bytes 75272 | tf_op jit(solution)/shard_map/ppermute | solution.py:30
  232.2 17.0 %collective-permute-start.30 = (f32[128]{0:T(128)S(1)}, f32[128]{0:T(128)S(1)}, u32[]{:S(2)}, u32[]{:S(2)}) collective-permute-start(f32[128]{0:T(128)S(1)} %slice_bitcast_fusion.35), channel_id=1, source_target_pairs={{0,32},{32,64},{64,96},{96,128},{128,160},{160,192},{192,224},{224... | collective-permute-start | bytes 1544 | tf_op jit(solution)/shard_map/ppermute | solution.py:43
  273.0 19.0 %collective-permute-start.36 = (f32[1,128]{1,0:T(1,128)S(1)}, f32[1,128]{1,0:T(1,128)S(1)}, u32[]{:S(2)}, u32[]{:S(2)}) collective-permute-start(f32[1,128]{1,0:T(1,128)S(1)} %collective-permute-done.35), channel_id=1, source_target_pairs={{0,8},{1,9},{2,10},{3,11},{4,12},{5,13},{6,14},{7,15},{8,0},{9,1},... | collective-permute-start | bytes 1544 | tf_op jit(solution)/shard_map/ppermute | solution.py:19
  279.1 31.9 %collective-permute-start.7 = (f32[49,128]{1,0:T(8,128)S(1)}, f32[49,128]{1,0:T(8,128)S(1)}, u32[]{:S(2)}, u32[]{:S(2)}) collective-permute-start(f32[49,128]{1,0:T(8,128)S(1)} %collective-permute-done.6), channel_id=1, source_target_pairs={{0,16},{1,17},{2,18},{3,19},{4,20},{5,21},{6,22},{7,23},{8,24},{9,... | collective-permute-start | bytes 75272 | tf_op jit(solution)/shard_map/ppermute | solution.py:19
  286.0 20.3 %collective-permute-start.38 = (f32[128]{0:T(128)S(1)}, f32[128]{0:T(128)S(1)}, u32[]{:S(2)}, u32[]{:S(2)}) collective-permute-start(f32[128]{0:T(128)S(1)} %get-tuple-element.163), channel_id=1, source_target_pairs={{32,0},{64,32},{96,64},{128,96},{160,128},{192,160},{224,192},{256... | collective-permute-start | bytes 1544 | tf_op jit(solution)/shard_map/ppermute | solution.py:43
  292.0 14.1 %collective-permute-start.37 = (f32[1,128]{1,0:T(1,128)S(1)}, f32[1,128]{1,0:T(1,128)S(1)}, u32[]{:S(2)}, u32[]{:S(2)}) collective-permute-start(f32[1,128]{1,0:T(1,128)S(1)} %collective-permute-done.36), channel_id=1, source_target_pairs={{0,16},{1,17},{2,18},{3,19},{4,20},{5,21},{6,22},{7,23},{8,24},{9,... | collective-permute-start | bytes 1544 | tf_op jit(solution)/shard_map/ppermute | solution.py:19
  307.0 13.1 %collective-permute-start.39 = (f32[128]{0:T(128)S(1)}, f32[128]{0:T(128)S(1)}, u32[]{:S(2)}, u32[]{:S(2)}) collective-permute-start(f32[128]{0:T(128)S(1)} %slice_bitcast_fusion.33), channel_id=1, source_target_pairs={{0,32},{32,64},{64,96},{96,128},{128,160},{160,192},{192,224},{224... | collective-permute-start | bytes 1544 | tf_op jit(solution)/shard_map/ppermute | solution.py:43
  340.8 20.5 %collective-permute-start.47 = (f32[128]{0:T(128)}, f32[128]{0:T(128)S(1)}, u32[]{:S(2)}, u32[]{:S(2)}) collective-permute-start(f32[128]{0:T(128)} %get-tuple-element.161), channel_id=1, source_target_pairs={{32,0},{64,32},{96,64},{128,96},{160,128},{192,160},{224,192},{256... | collective-permute-start | bytes 1544 | tf_op jit(solution)/shard_map/ppermute | solution.py:43
  346.9 14.4 %collective-permute-start.46 = (f32[1,128]{1,0:T(1,128)}, f32[1,128]{1,0:T(1,128)S(1)}, u32[]{:S(2)}, u32[]{:S(2)}) collective-permute-start(f32[1,128]{1,0:T(1,128)} %collective-permute-done.45), channel_id=1, source_target_pairs={{0,16},{1,17},{2,18},{3,19},{4,20},{5,21},{6,22},{7,23},{8,24},{9,... | collective-permute-start | bytes 1544 | tf_op jit(solution)/shard_map/ppermute | solution.py:19
  363.4 14.6 %collective-permute-start.48 = (f32[128]{0:T(128)}, f32[128]{0:T(128)}, u32[]{:S(2)}, u32[]{:S(2)}) collective-permute-start(f32[128]{0:T(128)} %slice_bitcast_fusion.31), channel_id=1, source_target_pairs={{0,32},{32,64},{64,96},{96,128},{128,160},{160,192},{192,224},{224... | collective-permute-start | bytes 1544 | tf_op jit(solution)/shard_map/ppermute | solution.py:43
  400.5 20.3 %collective-permute-start.56 = (f32[128]{0:T(128)S(1)}, f32[128]{0:T(128)S(1)}, u32[]{:S(2)}, u32[]{:S(2)}) collective-permute-start(f32[128]{0:T(128)S(1)} %get-tuple-element.159), channel_id=1, source_target_pairs={{32,0},{64,32},{96,64},{128,96},{160,128},{192,160},{224,192},{256... | collective-permute-start | bytes 1544 | tf_op jit(solution)/shard_map/ppermute | solution.py:43
  406.6 14.1 %collective-permute-start.55 = (f32[1,128]{1,0:T(1,128)S(1)}, f32[1,128]{1,0:T(1,128)S(1)}, u32[]{:S(2)}, u32[]{:S(2)}) collective-permute-start(f32[1,128]{1,0:T(1,128)S(1)} %collective-permute-done.54), channel_id=1, source_target_pairs={{0,16},{1,17},{2,18},{3,19},{4,20},{5,21},{6,22},{7,23},{8,24},{9,... | collective-permute-start | bytes 1544 | tf_op jit(solution)/shard_map/ppermute | solution.py:19
  421.7 13.1 %collective-permute-start.57 = (f32[128]{0:T(128)S(1)}, f32[128]{0:T(128)S(1)}, u32[]{:S(2)}, u32[]{:S(2)}) collective-permute-start(f32[128]{0:T(128)S(1)} %slice_bitcast_fusion.29), channel_id=1, source_target_pairs={{0,32},{32,64},{64,96},{96,128},{128,160},{160,192},{192,224},{224... | collective-permute-start | bytes 1544 | tf_op jit(solution)/shard_map/ppermute | solution.py:43
  450.9 12.8 %collective-permute-start.62 = (f32[1,128]{1,0:T(1,128)S(1)}, f32[1,128]{1,0:T(1,128)S(1)}, u32[]{:S(2)}, u32[]{:S(2)}) collective-permute-start(f32[1,128]{1,0:T(1,128)S(1)} %collective-permute-done.61), channel_id=1, source_target_pairs={{0,8},{1,9},{2,10},{3,11},{4,12},{5,13},{6,14},{7,15},{8,0},{9,1},... | collective-permute-start | bytes 1544 | tf_op jit(solution)/shard_map/ppermute | solution.py:19
  454.9 16.2 %collective-permute-start.58 = (f32[32]{0:T(128)S(1)}, f32[32]{0:T(128)S(1)}, u32[]{:S(2)}, u32[]{:S(2)}) collective-permute-start(f32[32]{0:T(128)S(1)} %slice_reduce_fusion), channel_id=1, source_target_pairs={{0,31},{1,0},{2,1},{3,2},{4,3},{5,4},{6,5},{7,6},{8,7},{9,8},{10,9... | collective-permute-start | bytes 392 | tf_op jit(solution)/shard_map/ppermute | solution.py:37
  457.7 20.3 %collective-permute-start.64 = (f32[128]{0:T(128)S(1)}, f32[128]{0:T(128)S(1)}, u32[]{:S(2)}, u32[]{:S(2)}) collective-permute-start(f32[128]{0:T(128)S(1)} %get-tuple-element.157), channel_id=1, source_target_pairs={{32,0},{64,32},{96,64},{128,96},{160,128},{192,160},{224,192},{256... | collective-permute-start | bytes 1544 | tf_op jit(solution)/shard_map/ppermute | solution.py:43
  463.7 14.1 %collective-permute-start.63 = (f32[1,128]{1,0:T(1,128)S(1)}, f32[1,128]{1,0:T(1,128)S(1)}, u32[]{:S(2)}, u32[]{:S(2)}) collective-permute-start(f32[1,128]{1,0:T(1,128)S(1)} %collective-permute-done.62), channel_id=1, source_target_pairs={{0,16},{1,17},{2,18},{3,19},{4,20},{5,21},{6,22},{7,23},{8,24},{9,... | collective-permute-start | bytes 1544 | tf_op jit(solution)/shard_map/ppermute | solution.py:19
  (118 other events, 6023.4 us)
where the time goes:
time: 485 us; the launch traced here: 481 us
  starting transfers between devices  256 us (53%)
  waiting for transfers between devices  87 us (18%)
  local copies, waits for them, and re-layouts  84.3 us (17%)
  other arithmetic  50.9 us (10%)
    ppermute x35, starting transfers between devices, partner(): lax.ppermute(shard, axis, [(i, i ^ 1 << bit) for i in range(lax.axis_size...  141 us
    gather x1, local copies, waits for them, and re-layouts, gather_fluxes(): values = jnp.take(table, picks, axis=1)  54.4 us
    ppermute x13, starting transfers between devices, passed_along(): lax.ppermute(value, axis, [(source, source + steps) for source in range(l...  52.4 us
    ppermute x13, waiting for transfers between devices, shifted(): lax.ppermute(shard, axis, [(i, (i + by) % count) for i in range(count)])  43.7 us
    ppermute x35, waiting for transfers between devices, partner(): lax.ppermute(shard, axis, [(i, i ^ 1 << bit) for i in range(lax.axis_size...  43.3 us
    ppermute x13, starting transfers between devices, shifted(): lax.ppermute(shard, axis, [(i, (i + by) % count) for i in range(count)])  30.1 us
    all_to_all x1, starting transfers between devices, gather_fluxes(): lax.all_to_all(packed, 'lon', split_axis=0, concat_axis=0, tiled=True)  17 us
  transfers between devices with their start and end apart: 66, of which 29 were waited for; matrix products, arithmetic and copies ran while one was open for 25% of the time, Pallas kernels for 0%

commit v1 on v0

v1 whole, which is shorter than its diff:
```python
import jax
import jax.numpy as jnp
from jax import lax
from jax.experimental import pallas as pl
from jax.experimental.pallas import tpu as pltpu
from jax.sharding import PartitionSpec as P

SUBSTEPS = 6
HALO = 8
FIELDS = 7
HEIGHT, EAST, NORTH, LEVELS, FRESH, WIND_E, WIND_N = range(FIELDS)
ROW_T = FIELDS * HALO
WEST_T = FIELDS * HALO + 1
EAST_T = FIELDS * HALO

adv_rate = 0.1
heat_gain = 0.5
salt_gain = 0.5
wave_div = 0.5
wave_grad = 0.8
fresh_gain = 0.2
wind_gain = 0.2

F32 = jnp.float32


def lanes(shape):
    return lax.broadcasted_iota(jnp.int32, shape, len(shape) - 1)


def rows_of(shape):
    return lax.broadcasted_iota(jnp.int32, shape, len(shape) - 2)


def turn(x, by, axis):
    size = x.shape[axis]
    by = by % size
    return x if by == 0 else pltpu.roll(x, by, axis)


def is_even(axis):
    return lax.rem(lax.axis_index(axis), 2) == 0


def is_top():
    return lax.axis_index("lat") == lax.axis_size("lat") - 1


def pick_kernel(atm_ref, rows_ref, out_ref):
    rows = rows_ref[0, 0]
    both = jnp.concatenate([rows, rows], axis=1)
    lane = both & 127
    part = both >> 7
    low = lanes(both.shape) < 64
    for pair in range(2):
        acc = None
        for k in range(atm_ref.shape[2] // 128):
            got = []
            for f in (2 * pair, 2 * pair + 1):
                row = jnp.broadcast_to(atm_ref[0, f : f + 1, k * 128 : (k + 1) * 128], both.shape)
                got.append(jnp.take_along_axis(row, lane, axis=1))
            value = jnp.where(low, got[0], got[1])
            acc = value if k == 0 else jnp.where(part == k, value, acc)
        out_ref[:, 0, pair * 128 : (pair + 1) * 128] = acc


def remap_kernel(
    table_ref, owner_ref, slot_ref, weight_ref, count_ref, level_ref, height_ref, transport_ref,
    t_low_ref, t_high_ref, v_high_ref, flux_ref, first_ref, second_ref, t_south_ref, tab, pack,
):
    received = table_ref[:, 0, :]
    half = received.shape[0] // 2
    low = lanes((half, 128)) < 64
    for pair in range(2):
        part = received[:, pair * 128 : (pair + 1) * 128]
        lo, hi = part[:half], part[half:]
        tab[2 * pair] = jnp.where(low, lo, turn(hi, 64, 1))
        tab[2 * pair + 1] = jnp.where(low, turn(lo, 64, 1), hi)
    count = count_ref[...]
    total = [jnp.zeros(count.shape, F32) for _ in range(4)]
    for k in range(owner_ref.shape[0]):
        owner = owner_ref[k]
        lane = slot_ref[k] + 64 * (owner >= half).astype(jnp.int32)
        row = jnp.where(owner >= half, owner - half, owner)
        acc = [None] * 4
        for r in range(half):
            here = row == r
            for f in range(4):
                source = jnp.broadcast_to(tab[f, r : r + 1, :], lane.shape)
                value = jnp.take_along_axis(source, lane, axis=1)
                acc[f] = value if r == 0 else jnp.where(here, value, acc[f])
        used = jnp.where(count > k, weight_ref[k], 0.0)
        total = [t + a * used for t, a in zip(total, acc)]
    for f in range(4):
        flux_ref[f] = total[f]

    even = is_even("lat")
    top = height_ref.shape[0] - HALO
    level_f = level_ref[...].astype(F32)
    for side, out in ((top, pack.at[0]), (0, pack.at[1])):
        rows = slice(side, side + HALO)
        out[HEIGHT * HALO : HEIGHT * HALO + HALO] = height_ref[rows]
        out[EAST * HALO : EAST * HALO + HALO] = transport_ref[0, rows]
        out[NORTH * HALO : NORTH * HALO + HALO] = transport_ref[1, rows]
        out[LEVELS * HALO : LEVELS * HALO + HALO] = level_f[rows]
        for i, f in ((FRESH, 1), (WIND_E, 2), (WIND_N, 3)):
            out[i * HALO : i * HALO + HALO] = total[f][rows]
    depth = t_low_ref.shape[1]
    for c in range(2):
        for l in range(depth):
            at = ROW_T + c * depth + l
            pack[0, at : at + 1] = t_high_ref[c, l, HALO - 1 : HALO]
            pack[1, at : at + 1] = t_low_ref[c, l, 0:1]
    for l in range(depth):
        at = ROW_T + 2 * depth + l
        pack[0, at : at + 1] = v_high_ref[0, l, HALO - 1 : HALO]
    pack[1, ROW_T + 2 * depth :] = jnp.zeros((depth, 128), F32)
    north_going, south_going = pack[0], pack[1]
    first_ref[...] = jnp.where(even, north_going, south_going)
    second_ref[...] = jnp.where(even, south_going, north_going)
    t_south_ref[...] = south_going[ROW_T : ROW_T + 2 * depth]


def column_kernel(t_ref, u_ref, level_ref, diff_ref, west_ref, east_ref, inv_ref):
    depth = t_ref.shape[1]
    shape = t_ref.shape[2:]
    lane = lanes(shape)
    west = jnp.zeros(shape, F32)
    east = jnp.zeros(shape, F32)
    for c in range(2):
        for l in range(depth):
            f = c * depth + l
            moved = turn(t_ref[c, l], WEST_T + f, 1)
            west = jnp.where(lane == WEST_T + f, moved, west)
            east = jnp.where(lane == EAST_T + f, moved, east)
    for l in range(depth):
        at = EAST_T + 2 * depth + l
        east = jnp.where(lane == at, turn(u_ref[0, l], at + 1, 1), east)
    west_ref[...] = west
    east_ref[...] = east
    level = level_ref[...]
    diff = diff_ref[...]
    above = jnp.zeros(shape, F32)
    inv = None
    for l in range(depth):
        below = jnp.where(level > l + 1, diff, 0.0) if l < depth - 1 else jnp.zeros(shape, F32)
        pivot = 1.0 + above + below
        if l > 0:
            pivot = pivot - above * above * inv
        inv = 1.0 / pivot
        inv_ref[l] = inv
        above = below


def edge_kernel(
    first_ref, second_ref, height_ref, transport_ref, level_ref, flux_ref, west_ref, east_ref,
    one_ref, two_ref, north_ref, south_ref,
):
    even = is_even("lat")
    a, b = first_ref[...], second_ref[...]
    north = jnp.where(even, a, b)
    south_ref[...] = jnp.where(even, b, a)
    south = south_ref[...]
    mirrored = jnp.take_along_axis(north, 127 - lanes(north.shape), axis=1)
    north = jnp.where(is_top(), mirrored, north)
    north_ref[...] = north
    own = (
        height_ref[...],
        transport_ref[0],
        transport_ref[1],
        level_ref[...].astype(F32),
        flux_ref[1],
        flux_ref[2],
        flux_ref[3],
    )
    pad = jnp.zeros((HALO, 128), F32)
    west = jnp.concatenate([pad, west_ref[...], pad], axis=0)
    east = jnp.concatenate([pad, east_ref[...], pad], axis=0)
    lane = lanes(west.shape)
    for i in range(FIELDS):
        rows = slice(i * HALO, (i + 1) * HALO)
        whole = jnp.concatenate([south[rows], own[i], north[rows]], axis=0)
        here = (lane >= i * HALO) & (lane < (i + 1) * HALO)
        west = jnp.where(here, turn(whole, i * HALO, 1), west)
        east = jnp.where(here, turn(whole, (i + 1) * HALO, 1), east)
    even = is_even("lon")
    one_ref[...] = jnp.where(even, east, west)
    two_ref[...] = jnp.where(even, west, east)


def step_kernel(
    one_ref, two_ref, north_ref, south_ref, height_ref, transport_ref, level_ref, flux_ref,
    west_ref, t_south_ref, inv_ref, diff_ref, t_ref, v_ref,
    t_out, height_out, transport_out, south_flux,
):
    top = is_top()
    even = is_even("lon")
    one, two = one_ref[...], two_ref[...]
    from_east = jnp.where(even, one, two)
    from_west = jnp.where(even, two, one)
    north, south = north_ref[...], south_ref[...]
    level = level_ref[...]
    level_f = level.astype(F32)
    rows, cols = level.shape
    lane = lanes(from_east.shape)
    own = (
        height_ref[...], transport_ref[0], transport_ref[1], level_f,
        flux_ref[1], flux_ref[2], flux_ref[3],
    )
    ext = []
    for i in range(FIELDS):
        at = slice(i * HALO, (i + 1) * HALO)
        whole = jnp.concatenate([south[at], own[i], north[at]], axis=0)
        rim = jnp.where(
            lane < HALO,
            turn(from_east, -i * HALO, 1),
            jnp.where(lane >= cols - HALO, turn(from_west, cols - (i + 1) * HALO, 1), 0.0),
        )
        ext.append(jnp.concatenate([whole, rim], axis=1))

    depth = t_ref.shape[1]

    def coefficients(f):
        wet = (f[LEVELS] > 0.0).astype(F32)
        return (
            wet,
            wave_grad * (f[LEVELS] / depth),
            fresh_gain * f[FRESH] * wet,
            wind_gain * f[WIND_E] * wet,
            wind_gain * f[WIND_N] * wet,
        )

    mine = [x for x in ext]
    fold = [x[HALO + rows :] for x in ext]
    wet, grad, fresh, wind_e, wind_n = coefficients(mine)
    p_wet, p_grad, p_fresh, p_wind_e, p_wind_n = coefficients(fold)
    h, e, n = mine[HEIGHT], mine[EAST], mine[NORTH]
    p_h, p_e, p_n = fold[HEIGHT], fold[EAST], fold[NORTH]
    row = rows_of(h.shape)
    last = HALO + rows - 1
    across = (row == last) & top
    p_last = rows_of(p_h.shape) == HALO - 1
    for _ in range(SUBSTEPS):
        h = (h - wave_div * ((e - turn(e, 1, 1)) + (n - turn(n, 1, 0)))) * wet + fresh
        p_h = (p_h - wave_div * ((p_e - turn(p_e, -1, 1)) + (p_n - turn(p_n, 1, 0)))) * p_wet + p_fresh
        h_n = jnp.where(across, jnp.broadcast_to(p_h[HALO - 1 :], h.shape), turn(h, -1, 0))
        p_h_n = jnp.where(p_last, jnp.broadcast_to(h[last : last + 1], p_h.shape), turn(p_h, -1, 0))
        e = (e - grad * (turn(h, -1, 1) - h)) * wet + wind_e
        n = (n - grad * (h_n - h)) * wet + wind_n
        p_e = (p_e - p_grad * (turn(p_h, 1, 1) - p_h)) * p_wet + p_wind_e
        p_n = (p_n - p_grad * (p_h_n - p_h)) * p_wet + p_wind_n
    inside = slice(HALO, HALO + rows)
    height_out[...] = h[inside, :cols]
    transport_out[0] = e[inside, :cols]
    transport_out[1] = n[inside, :cols]

    ext_level = ext[LEVELS]
    level_e = turn(ext_level, -1, 1)[inside, :cols]
    level_w = turn(ext_level, 1, 1)[inside, :cols]
    first = LEVELS * HALO
    level_n_row = jnp.where(top, north[first + HALO - 1 : first + HALO], north[first : first + 1])
    level_s_row = south[first + HALO - 1 : first + HALO]
    shape = (rows, cols)
    lane = lanes(shape)
    row = rows_of(shape)
    level_n = jnp.where(row == rows - 1, jnp.broadcast_to(level_n_row, shape), turn(level_f, -1, 0))
    face_e = jnp.minimum(level_f, level_e)
    face_n = jnp.minimum(level_f, level_n)
    face_s = jnp.minimum(level_f[0:1], level_s_row)
    t_w = from_west[inside]
    t_0 = turn(west_ref[...], EAST_T - WEST_T, 1)
    start_u = EAST_T + 2 * depth
    u_w = jnp.where(lane < EAST_T + depth, turn(t_w, EAST_T - start_u, 1), turn(t_w, EAST_T + depth - start_u, 1))
    layer = jnp.where(lane < EAST_T + depth, lane - EAST_T, lane - EAST_T - depth).astype(F32)
    face_w = jnp.broadcast_to(jnp.minimum(level_f, level_w)[:, 0:1], shape)
    west_flux = jnp.where(layer < face_w, u_w * ((t_w + t_0) * 0.5), 0.0)
    t_e = from_east[inside]
    for c in range(2):
        planes = slice(ROW_T + c * depth, ROW_T + (c + 1) * depth)
        flux = south[ROW_T + 2 * depth : ROW_T + 3 * depth] * (
            (south[planes] + t_south_ref[c * depth : (c + 1) * depth]) * 0.5
        )
        deep = rows_of(flux.shape).astype(F32) < face_s
        south_flux[c * depth : (c + 1) * depth] = jnp.where(deep, flux, 0.0)

    diff = diff_ref[...]
    wet_0 = (level > 0).astype(F32)
    source = (heat_gain * flux_ref[0] * wet_0, -salt_gain * flux_ref[1] * wet_0)
    right = [None, None]
    for l in range(depth):
        mask_e = face_e > l
        mask_n = face_n > l
        u_l, v_l = v_ref[0, l], v_ref[1, l]
        above = jnp.where(level > l, diff, 0.0)
        inv = inv_ref[l]
        for c in range(2):
            f = c * depth + l
            t = t_ref[c, l]
            east = jnp.where(lane == cols - 1, turn(t_e, cols - 1 - (WEST_T + f), 1), turn(t, -1, 1))
            flux_e = jnp.where(mask_e, u_l * ((t + east) * 0.5), 0.0)
            flux_w = jnp.where(lane == 0, turn(west_flux, -(EAST_T + f), 1), turn(flux_e, 1, 1))
            north_row = jnp.broadcast_to(north_ref[ROW_T + f : ROW_T + f + 1], shape)
            up = jnp.where(row == rows - 1, north_row, turn(t, -1, 0))
            flux_n = jnp.where(mask_n, v_l * ((t + up) * 0.5), 0.0)
            south_row = jnp.broadcast_to(south_flux[f : f + 1], shape)
            flux_s = jnp.where(row == 0, south_row, turn(flux_n, 1, 0))
            forced = t - adv_rate * ((flux_e - flux_w) + (flux_n - flux_s))
            if l == 0:
                forced = forced + source[c]
                right[c] = forced * inv
            else:
                right[c] = (forced + above * right[c]) * inv
            t_out[c, l] = right[c]
    for l in range(depth - 2, -1, -1):
        below = jnp.where(level > l + 1, diff, 0.0) * inv_ref[l]
        for c in range(2):
            right[c] = t_out[c, l] + below * right[c]
            t_out[c, l] = right[c]


def vmem(count):
    return [pl.BlockSpec(memory_space=pltpu.VMEM)] * count


def params():
    return pltpu.CompilerParams(vmem_limit_bytes=48 * 1024 * 1024)


def shape_of(*shape):
    return jax.ShapeDtypeStruct(shape, F32)


def lat_pairs(n_lat, n_lon):
    def at(i, j):
        return i * n_lon + j

    first, second = [], []
    for j in range(n_lon):
        for i in range(0, n_lat, 2):
            first += [(at(i, j), at(i + 1, j)), (at(i + 1, j), at(i, j))]
        for i in range(1, n_lat - 1, 2):
            second += [(at(i, j), at(i + 1, j)), (at(i + 1, j), at(i, j))]
        second.append((at(n_lat - 1, j), at(n_lat - 1, n_lon - 1 - j)))
    return first, second


def lon_pairs(n_lon):
    first, second = [], []
    for j in range(0, n_lon, 2):
        first += [(j, j + 1), (j + 1, j)]
        k, m = j + 1, (j + 2) % n_lon
        second += [(k, m), (m, k)]
    return first, second


def per_device(
    tracers,
    velocity,
    diffusivity,
    ocean_levels,
    surface_height,
    transport,
    atm_flux,
    send_rows,
    src_owner,
    src_slot,
    xgrid_weights,
    xgrid_count,
):
    n_lat, n_lon = lax.axis_size("lat"), lax.axis_size("lon")
    depth, rows, cols = tracers.shape[1:]
    slots = send_rows.shape[3]
    picked = pl.pallas_call(
        pick_kernel,
        out_shape=shape_of(n_lon, 1, 4 * slots),
        in_specs=vmem(2),
        out_specs=vmem(1)[0],
        compiler_params=params(),
        name="pick",
    )(atm_flux, send_rows)
    table = lax.all_to_all(picked, "lon", split_axis=0, concat_axis=0, tiled=True)

    eight = lambda pick: pl.BlockSpec((2, depth, HALO, cols), lambda i, p=pick: (0, 0, p, 0))
    last = rows // HALO - 1
    lat_rows = ROW_T + 3 * depth
    flux, first, second, t_south = pl.pallas_call(
        remap_kernel,
        grid=(1,),
        out_shape=(
            shape_of(4, rows, cols),
            shape_of(lat_rows, cols),
            shape_of(lat_rows, cols),
            shape_of(2 * depth, cols),
        ),
        in_specs=vmem(8)
        + [
            eight(0),
            eight(last),
            pl.BlockSpec((1, depth, HALO, cols), lambda i: (1, 0, last, 0)),
        ],
        out_specs=vmem(4),
        scratch_shapes=[
            pltpu.VMEM((4, n_lon // 2, 128), F32),
            pltpu.VMEM((2, lat_rows, cols), F32),
        ],
        compiler_params=params(),
        name="remap",
    )(
        table, src_owner, src_slot, xgrid_weights, xgrid_count, ocean_levels, surface_height, transport,
        tracers, tracers, velocity,
    )
    pairs = lat_pairs(n_lat, n_lon)
    first = lax.ppermute(first, ("lat", "lon"), pairs[0])
    second = lax.ppermute(second, ("lat", "lon"), pairs[1])

    west, east, inv = pl.pallas_call(
        column_kernel,
        grid=(1,),
        out_shape=(shape_of(rows, cols), shape_of(rows, cols), shape_of(depth, rows, cols)),
        in_specs=[
            pl.BlockSpec((2, depth, rows, cols), lambda i: (0, 0, 0, 0)),
            pl.BlockSpec((1, depth, rows, cols), lambda i: (0, 0, 0, 0)),
        ]
        + vmem(2),
        out_specs=vmem(3),
        compiler_params=params(),
        cost_estimate=pl.CostEstimate(flops=2000000, bytes_accessed=2000000, transcendentals=0),
        name="columns",
    )(tracers, velocity, ocean_levels, diffusivity)

    one, two, north, south = pl.pallas_call(
        edge_kernel,
        out_shape=(
            shape_of(rows + 2 * HALO, cols),
            shape_of(rows + 2 * HALO, cols),
            shape_of(lat_rows, cols),
            shape_of(lat_rows, cols),
        ),
        in_specs=vmem(8),
        out_specs=vmem(4),
        compiler_params=params(),
        name="edges",
    )(first, second, surface_height, transport, ocean_levels, flux, west, east)
    pairs = lon_pairs(n_lon)
    one = lax.ppermute(one, "lon", pairs[0])
    two = lax.ppermute(two, "lon", pairs[1])

    return pl.pallas_call(
        step_kernel,
        out_shape=(shape_of(2, depth, rows, cols), shape_of(rows, cols), shape_of(2, rows, cols)),
        in_specs=vmem(14),
        out_specs=tuple(vmem(3)),
        scratch_shapes=[pltpu.VMEM((2 * depth, cols), F32)],
        compiler_params=params(),
        name="step",
    )(
        one, two, north, south, surface_height, transport, ocean_levels, flux,
        west, t_south, inv, diffusivity, tracers, velocity,
    )


def solution(mesh):
    return jax.shard_map(
        per_device,
        mesh=mesh,
        in_specs=(
            P(None, None, "lat", "lon"),
            P(None, None, "lat", "lon"),
            P("lat", "lon"),
            P("lat", "lon"),
            P("lat", "lon"),
            P(None, "lat", "lon"),
            P("lat", None, "lon"),
            P("lat", "lon", None, None),
            P(None, "lat", "lon"),
            P(None, "lat", "lon"),
            P(None, "lat", "lon"),
            P("lat", "lon"),
        ),
        out_specs=(P(None, None, "lat", "lon"), P("lat", "lon"), P(None, "lat", "lon")),
        check_vma=False,
    )
```

time: 485 us -> 73.7 us (0.15)
  the two profiles are of different devices: /device:TPU:32 before, /device:TPU:120 now
where the time goes in v1:
time: 73.7 us; the launch traced here: 73.2 us
  blocking collectives  29.8 us (40%)
  waiting for transfers between devices  17.3 us (23%)
  starting transfers between devices  10.4 us (14%)
  Pallas kernels  8.65 us (12%)
  local copies, waits for them, and re-layouts  6.22 us (8%)
  between operations  0.78 us (1%)
    all_to_all x1, blocking collectives, per_device(): lax.all_to_all(picked, 'lon', split_axis=0, concat_axis=0, tiled=True)  29.8 us
    ppermute x1, waiting for transfers between devices, per_device(): second = lax.ppermute(second, ('lat', 'lon'), pairs[1])  8.79 us
    ppermute x1, waiting for transfers between devices, per_device(): two = lax.ppermute(two, 'lon', pairs[1])  7.99 us
    unnamed x28, local copies, waits for them, and re-layouts  6.22 us
    pallas_call x1, Pallas kernels, per_device(): pl.pallas_call(step_kernel, out_shape=(shape_of(2, depth, rows, cols), sh...  4.63 us
    ppermute x1, starting transfers between devices, per_device(): two = lax.ppermute(two, 'lon', pairs[1])  3.16 us
    pallas_call x1, Pallas kernels, per_device(): pl.pallas_call(remap_kernel, grid=(1,), out_shape=(shape_of(4, rows, cols...  3.14 us
    ppermute x1, starting transfers between devices, per_device(): first = lax.ppermute(first, ('lat', 'lon'), pairs[0])  2.65 us
  transfers between devices with their start and end apart: 4, of which 3 were waited for; matrix products, arithmetic and copies ran while one was open for 0% of the time, Pallas kernels for 1%

profile of v1, /device:TPU:120, one launch (start us, length us, event | category | flops | bytes accessed | tf_op | source)
XLA Modules:
  0.0 73.2 jit_solution(118919418953408514)
XLA Ops:
  0.6 0.0 copy-start.12
  0.6 0.7 copy-done.12
  1.4 0.7 copy-done.13
  2.0 0.3 pick.1
  2.4 0.0 copy-start.4
  2.4 0.0 copy-start.5
  2.4 0.0 copy-start.6
  2.4 29.8 %all_to_all.5.table_ref = f32[32,1,256]{2,1,0:T(1,128)S(1)} all-to-all(f32[32,1,256]{2,1,0:T(1,128)S(1)} %pick.1), channel_id=1, replica_groups=mesh['lat'=16,'lon'=32] {'lon'}, dimensions={0} | all-to-all | bytes 65536 | tf_op jit(solution)/shard_map/all_to_all | solution.py:381
  32.2 0.0 copy-done.11
  32.2 0.0 copy-done.4
  32.2 0.0 copy-done.5
  32.2 0.0 copy-done.6
  32.2 0.0 copy-start
  32.2 1.1 %copy-done = f32[2,24,32,128]{3,2,1,0:T(8,128)S(1)} copy-done((f32[2,24,32,128]{3,2,1,0:T(8,128)S(1)}, f32[2,24,32,128]{3,2,1,0:T(8,128)}, u32[]{:S(2)}) %copy-start) | copy-done | bytes 786456
  33.4 1.1 %copy-done.2 = f32[2,24,32,128]{3,2,1,0:T(8,128)S(1)} copy-done((f32[2,24,32,128]{3,2,1,0:T(8,128)S(1)}, f32[2,24,32,128]{3,2,1,0:T(8,128)}, u32[]{:S(2)}) %copy-start.2) | copy-done | bytes 786456
  34.5 0.8 %copy-done.8 = s32[4,32,128]{2,1,0:T(8,128)S(1)} copy-done((s32[4,32,128]{2,1,0:T(8,128)S(1)}, s32[4,32,128]{2,1,0:T(8,128)}, u32[]{:S(2)}) %copy-start.8) | copy-done | bytes 65560
  35.3 0.8 %copy-done.9 = s32[4,32,128]{2,1,0:T(8,128)S(1)} copy-done((s32[4,32,128]{2,1,0:T(8,128)S(1)}, s32[4,32,128]{2,1,0:T(8,128)}, u32[]{:S(2)}) %copy-start.9) | copy-done | bytes 65560
  36.2 0.8 %copy-done.10 = f32[4,32,128]{2,1,0:T(8,128)S(1)} copy-done((f32[4,32,128]{2,1,0:T(8,128)S(1)}, f32[4,32,128]{2,1,0:T(8,128)}, u32[]{:S(2)}) %copy-start.10) | copy-done | bytes 65560
  37.0 3.1 %remap.1 = (f32[4,32,128]{2,1,0:T(8,128)S(1)}, f32[128,128]{1,0:T(8,128)S(1)}, f32[128,128]{1,0:T(8,128)S(1)}, f32[48,128]{1,0:T(8,128)S(1)}) custom-call(f32[32,1,256]{2,1,0:T(1,128)S(1)} %all_to_all.5.table_ref, s32[4,32,128]{2,1,0:T(8,128)S(1)} %copy-done.8, s32[4,32,128]{2,1,0:T(8,128)S(1)} %copy-done.9, f32[4,32,128]{2,1,0:T(8,128)S(1)} %copy-done.10, ...), custom_call_target="tpu_custom_call" | custom-call | tf_op jit(solution)/shard_map/remap/pallas_call | solution.py:386
  40.2 2.7 %collective-permute-start = (f32[128,128]{1,0:T(8,128)S(1)}, f32[128,128]{1,0:T(8,128)S(1)}, u32[]{:S(2)}, u32[]{:S(2)}) collective-permute-start(f32[128,128]{1,0:T(8,128)S(1)} %get-tuple-element.14), channel_id=1, source_target_pairs={{0,32},{32,0},{64,96},{96,64},{128,160},{160,128},{192,224},{224,1... | collective-permute-start | bytes 196616 | tf_op jit(solution)/shard_map/ppermute | solution.py:413
  42.8 2.6 %collective-permute-start.1 = (f32[128,128]{1,0:T(8,128)S(1)}, f32[128,128]{1,0:T(8,128)S(1)}, u32[]{:S(2)}, u32[]{:S(2)}) collective-permute-start(f32[128,128]{1,0:T(8,128)S(1)} %get-tuple-element.15), channel_id=1, source_target_pairs={{32,64},{64,32},{96,128},{128,96},{160,192},{192,160},{224,256},{2... | collective-permute-start | bytes 196616 | tf_op jit(solution)/shard_map/ppermute | solution.py:414
  45.4 0.0 copy-done.1
  45.4 0.0 copy-done.3
  45.5 0.4 columns.1
  45.8 0.5 collective-permute-done.first_ref
  46.3 8.8 %collective-permute-done.1.second_ref = f32[128,128]{1,0:T(8,128)S(1)} collective-permute-done((f32[128,128]{1,0:T(8,128)S(1)}, f32[128,128]{1,0:T(8,128)S(1)}, u32[]{:S(2)}, u32[]{:S(2)}) %collective-permute-start.1) | collective-permute-done | bytes 65568 | tf_op jit(solution)/shard_map/ppermute | solution.py:414
  55.1 0.2 edges.1
  55.3 2.0 %collective-permute-start.2 = (f32[48,128]{1,0:T(8,128)S(1)}, f32[48,128]{1,0:T(8,128)S(1)}, u32[]{:S(2)}, u32[]{:S(2)}) collective-permute-start(f32[48,128]{1,0:T(8,128)S(1)} %get-tuple-element.19), channel_id=1, source_target_pairs={{0,1},{1,0},{2,3},{3,2},{4,5},{5,4},{6,7},{7,6},{8,9},{9,8},{10,11... | collective-permute-start | bytes 73736 | tf_op jit(solution)/shard_map/ppermute | solution.py:445
  57.4 3.2 %collective-permute-start.3 = (f32[48,128]{1,0:T(8,128)S(1)}, f32[48,128]{1,0:T(8,128)S(1)}, u32[]{:S(2)}, u32[]{:S(2)}) collective-permute-start(f32[48,128]{1,0:T(8,128)S(1)} %get-tuple-element.20), channel_id=1, source_target_pairs={{1,2},{2,1},{3,4},{4,3},{5,6},{6,5},{7,8},{8,7},{9,10},{10,9},{11,... | collective-permute-start | bytes 73736 | tf_op jit(solution)/shard_map/ppermute | solution.py:446
  60.5 0.0 collective-permute-done.2.one_ref
  60.5 8.0 %collective-permute-done.3.two_ref = f32[48,128]{1,0:T(8,128)S(1)} collective-permute-done((f32[48,128]{1,0:T(8,128)S(1)}, f32[48,128]{1,0:T(8,128)S(1)}, u32[]{:S(2)}, u32[]{:S(2)}) %collective-permute-start.3) | collective-permute-done | bytes 24608 | tf_op jit(solution)/shard_map/ppermute | solution.py:446
  68.5 4.6 %step.1 = (f32[2,24,32,128]{3,2,1,0:T(8,128)}, f32[32,128]{1,0:T(8,128)}, f32[2,32,128]{2,1,0:T(8,128)}) custom-call(f32[48,128]{1,0:T(8,128)S(1)} %collective-permute-done.2.one_ref, f32[48,128]{1,0:T(8,128)S(1)} %collective-permute-done.3.two_ref, f32[128,128]{1,0:T(8,128)S(1)} %get-tuple-element.21.north_ref, f32[128,128]{1,0:T(8,128)S(1)} %get-tuple-element.22.south_ref, ...), custom_call_target="tpu_custom_call" | custom-call | tf_op jit(solution)/shard_map/step/pallas_call | solution.py:448
  (10 shorter events, 0.0 us)
Async XLA Ops:
  0.6 0.7 copy-start.12
  1.3 0.7 copy-start.13
  2.0 30.2 %copy-start.11 = (s32[32,128]{1,0:T(8,128)S(1)}, s32[32,128]{1,0:T(8,128)}, u32[]{:S(2)}) copy-start(s32[32,128]{1,0:T(8,128)} %count_ref.1) | copy-start | bytes 49156
  2.4 29.8 %copy-start.4 = (f32[2,32,128]{2,1,0:T(8,128)S(1)}, f32[2,32,128]{2,1,0:T(8,128)}, u32[]{:S(2)}) copy-start(f32[2,32,128]{2,1,0:T(8,128)} %transport_ref.5) | copy-start | bytes 98308
  2.4 29.8 %copy-start.5 = (s32[32,128]{1,0:T(8,128)S(1)}, s32[32,128]{1,0:T(8,128)}, u32[]{:S(2)}) copy-start(s32[32,128]{1,0:T(8,128)} %level_ref.7) | copy-start | bytes 49156
  2.4 29.8 %copy-start.6 = (f32[32,128]{1,0:T(8,128)S(1)}, f32[32,128]{1,0:T(8,128)}, u32[]{:S(2)}) copy-start(f32[32,128]{1,0:T(8,128)} %height_ref.5) | copy-start | bytes 49156
  32.2 1.1 %copy-start = (f32[2,24,32,128]{3,2,1,0:T(8,128)S(1)}, f32[2,24,32,128]{3,2,1,0:T(8,128)}, u32[]{:S(2)}) copy-start(f32[2,24,32,128]{3,2,1,0:T(8,128)} %t_ref.3) | copy-start | bytes 2359300
  33.4 1.1 %copy-start.2 = (f32[2,24,32,128]{3,2,1,0:T(8,128)S(1)}, f32[2,24,32,128]{3,2,1,0:T(8,128)}, u32[]{:S(2)}) copy-start(f32[2,24,32,128]{3,2,1,0:T(8,128)} %v_ref.1) | copy-start | bytes 2359300
  34.5 0.8 %copy-start.8 = (s32[4,32,128]{2,1,0:T(8,128)S(1)}, s32[4,32,128]{2,1,0:T(8,128)}, u32[]{:S(2)}) copy-start(s32[4,32,128]{2,1,0:T(8,128)} %owner_ref.1) | copy-start | bytes 196612
  35.3 0.8 %copy-start.9 = (s32[4,32,128]{2,1,0:T(8,128)S(1)}, s32[4,32,128]{2,1,0:T(8,128)}, u32[]{:S(2)}) copy-start(s32[4,32,128]{2,1,0:T(8,128)} %slot_ref.1) | copy-start | bytes 196612
  36.2 0.8 %copy-start.10 = (f32[4,32,128]{2,1,0:T(8,128)S(1)}, f32[4,32,128]{2,1,0:T(8,128)}, u32[]{:S(2)}) copy-start(f32[4,32,128]{2,1,0:T(8,128)} %weight_ref.1) | copy-start | bytes 196612
  37.0 8.4 %copy-start.1 = (f32[2,24,32,128]{3,2,1,0:T(8,128)S(1)}, f32[2,24,32,128]{3,2,1,0:T(8,128)}, u32[]{:S(2)}) copy-start(f32[2,24,32,128]{3,2,1,0:T(8,128)} %t_ref.3) | copy-start | bytes 2359300
  37.0 8.4 %copy-start.3 = (f32[2,24,32,128]{3,2,1,0:T(8,128)S(1)}, f32[2,24,32,128]{3,2,1,0:T(8,128)}, u32[]{:S(2)}) copy-start(f32[2,24,32,128]{3,2,1,0:T(8,128)} %v_ref.1) | copy-start | bytes 2359300
  37.0 8.4 %copy-start.7 = (f32[32,128]{1,0:T(8,128)S(1)}, f32[32,128]{1,0:T(8,128)}, u32[]{:S(2)}) copy-start(f32[32,128]{1,0:T(8,128)} %diff_ref.3) | copy-start | bytes 49156
  40.2 6.2 %collective-permute-start = (f32[128,128]{1,0:T(8,128)S(1)}, f32[128,128]{1,0:T(8,128)S(1)}, u32[]{:S(2)}, u32[]{:S(2)}) collective-permute-start(f32[128,128]{1,0:T(8,128)S(1)} %get-tuple-element.14), channel_id=1, source_target_pairs={{0,32},{32,0},{64,96},{96,64},{128,160},{160,128},{192,224},{224,1... | collective-permute-start | bytes 196616 | tf_op jit(solution)/shard_map/ppermute | solution.py:413
  42.8 12.3 %collective-permute-start.1 = (f32[128,128]{1,0:T(8,128)S(1)}, f32[128,128]{1,0:T(8,128)S(1)}, u32[]{:S(2)}, u32[]{:S(2)}) collective-permute-start(f32[128,128]{1,0:T(8,128)S(1)} %get-tuple-element.15), channel_id=1, source_target_pairs={{32,64},{64,32},{96,128},{128,96},{160,192},{192,160},{224,256},{2... | collective-permute-start | bytes 196616 | tf_op jit(solution)/shard_map/ppermute | solution.py:414
  55.3 5.2 %collective-permute-start.2 = (f32[48,128]{1,0:T(8,128)S(1)}, f32[48,128]{1,0:T(8,128)S(1)}, u32[]{:S(2)}, u32[]{:S(2)}) collective-permute-start(f32[48,128]{1,0:T(8,128)S(1)} %get-tuple-element.19), channel_id=1, source_target_pairs={{0,1},{1,0},{2,3},{3,2},{4,5},{5,4},{6,7},{7,6},{8,9},{9,8},{10,11... | collective-permute-start | bytes 73736 | tf_op jit(solution)/shard_map/ppermute | solution.py:445
  57.4 11.2 %collective-permute-start.3 = (f32[48,128]{1,0:T(8,128)S(1)}, f32[48,128]{1,0:T(8,128)S(1)}, u32[]{:S(2)}, u32[]{:S(2)}) collective-permute-start(f32[48,128]{1,0:T(8,128)S(1)} %get-tuple-element.20), channel_id=1, source_target_pairs={{1,2},{2,1},{3,4},{4,3},{5,6},{6,5},{7,8},{8,7},{9,10},{10,9},{11,... | collective-permute-start | bytes 73736 | tf_op jit(solution)/shard_map/ppermute | solution.py:446

commit v2 on v1

v2 whole, which is shorter than its diff:
```python
import jax
import jax.numpy as jnp
from jax import lax
from jax.experimental import pallas as pl
from jax.experimental.pallas import tpu as pltpu
from jax.sharding import PartitionSpec as P

SUBSTEPS = 6
HALO = 8
FIELDS = 7
HEIGHT, EAST, NORTH, LEVELS, FRESH, WIND_E, WIND_N = range(FIELDS)
ROW_RIM = FIELDS * HALO
ROW_T = ROW_RIM + HALO
OWNER, SLOT, USED = 32, 64, 96

adv_rate = 0.1
heat_gain = 0.5
salt_gain = 0.5
wave_div = 0.5
wave_grad = 0.8
fresh_gain = 0.2
wind_gain = 0.2

F32 = jnp.float32


def lanes(shape):
    return lax.broadcasted_iota(jnp.int32, shape, len(shape) - 1)


def rows_of(shape):
    return lax.broadcasted_iota(jnp.int32, shape, len(shape) - 2)


def turn(x, by, axis):
    size = x.shape[axis]
    by = by % size
    return x if by == 0 else pltpu.roll(x, by, axis)


def is_even(axis):
    return lax.rem(lax.axis_index(axis), 2) == 0


def is_top():
    return lax.axis_index("lat") == lax.axis_size("lat") - 1


def pick_kernel(atm_hbm, rows_hbm, out_ref, atm_ref, rows_ref, sems):
    copies = [
        pltpu.make_async_copy(atm_hbm, atm_ref, sems.at[0]),
        pltpu.make_async_copy(rows_hbm, rows_ref, sems.at[1]),
    ]
    for copy in copies:
        copy.start()
    for copy in copies:
        copy.wait()
    rows = rows_ref[0, 0]
    both = jnp.concatenate([rows, rows], axis=1)
    lane = both & 127
    part = both >> 7
    low = lanes(both.shape) < 64
    values = []
    for f in range(4):
        acc = None
        for k in range(atm_ref.shape[2] // 128):
            row = jnp.broadcast_to(atm_ref[0, f : f + 1, k * 128 : (k + 1) * 128], both.shape)
            value = jnp.take_along_axis(row, lane, axis=1)
            acc = value if k == 0 else jnp.where(part == k, value, acc)
        values.append(acc)
    out_ref[:, 0, 0:128] = jnp.where(low, values[0], values[1])
    out_ref[:, 0, 128:256] = jnp.where(low, values[2], values[3])
    for f in range(1, 4):
        at = 128 + f * 128
        out_ref[:, 0, at : at + 128] = jnp.where(low, turn(values[f], -1, 0), turn(values[f], 1, 0))


def edge_kernel(
    picked_ref, t_ref, v_ref, level_ref, diff_ref, height_ref, transport_ref, owner_ref, slot_ref,
    weight_ref, count_ref, one_ref, two_ref, t_0_ref, rows_ref, inv_ref, pick_row_ref, pick_lane_ref, used_ref,
):
    depth = t_ref.shape[1]
    shape = t_ref.shape[2:]
    rows, cols = shape
    lane = lanes(shape)
    level = level_ref[...]
    half = lax.axis_size("lon") // 2
    count = count_ref[...]
    for k in range(owner_ref.shape[0]):
        owner = owner_ref[k]
        high = owner >= half
        pick_row_ref[k] = jnp.where(high, owner - half, owner)
        pick_lane_ref[k] = jnp.where(high, slot_ref[k] + 64, slot_ref[k])
        used_ref[k] = jnp.where(count > k, weight_ref[k], 0.0)
    fields = [height_ref[...], transport_ref[0], transport_ref[1], level.astype(F32)]
    fields += [owner_ref[k].astype(F32) for k in range(4)]
    fields += [slot_ref[k].astype(F32) for k in range(4)]
    fields += [used_ref[k] for k in range(4)]
    west = jnp.zeros(shape, F32)
    east = jnp.zeros(shape, F32)
    for g, field in enumerate(fields):
        here = (lane >= g * HALO) & (lane < (g + 1) * HALO)
        west = jnp.where(here, turn(field, g * HALO, 1), west)
        east = jnp.where(here, turn(field, (g + 1) * HALO, 1), east)
    west_t = jnp.zeros(shape, F32)
    east_t = jnp.zeros(shape, F32)
    for c in range(2):
        for l in range(depth):
            f = c * depth + l
            moved = turn(t_ref[c, l], f + 1, 1)
            west_t = jnp.where(lane == f + 1, moved, west_t)
            east_t = jnp.where(lane == f, moved, east_t)
    for l in range(depth):
        at = 2 * depth + l
        east_t = jnp.where(lane == at, turn(v_ref[0, l], at + 1, 1), east_t)
    even = is_even("lon")
    one_ref[:rows] = jnp.where(even, east, west)
    two_ref[:rows] = jnp.where(even, west, east)
    one_ref[rows:] = jnp.where(even, east_t, west_t)
    two_ref[rows:] = jnp.where(even, west_t, east_t)
    t_0_ref[...] = turn(west_t, -1, 1)
    for c in range(2):
        for l in range(depth):
            at = c * depth + l
            rows_ref[0, at : at + 1] = t_ref[c, l, rows - 1 : rows]
            rows_ref[1, at : at + 1] = t_ref[c, l, 0:1]
    for l in range(depth):
        at = 2 * depth + l
        rows_ref[0, at : at + 1] = v_ref[1, l, rows - 1 : rows]
    rows_ref[1, 2 * depth :] = jnp.zeros((depth, cols), F32)
    diff = diff_ref[...]
    above = jnp.zeros(shape, F32)
    inv = None
    for l in range(depth):
        below = jnp.where(level > l + 1, diff, 0.0) if l < depth - 1 else jnp.zeros(shape, F32)
        pivot = 1.0 + above + below
        if l > 0:
            pivot = pivot - above * above * inv
        inv = 1.0 / pivot
        inv_ref[l] = inv
        above = below


def remap_kernel(
    table_ref, one_ref, two_ref, pick_row_ref, pick_lane_ref, used_ref, rows_ref, level_ref, height_ref,
    transport_ref, flux_ref, rim_ref, first_ref, second_ref, tab, side, pack,
):
    n_lon = table_ref.shape[0]
    half = n_lon // 2
    rows, cols = height_ref.shape
    low = lanes((half, 128)) < 64
    for pair in range(2):
        part = table_ref[:, 0, pair * 128 : (pair + 1) * 128]
        lo, hi = part[:half], part[half:]
        tab[2 * pair] = jnp.where(low, lo, turn(hi, 64, 1))
        tab[2 * pair + 1] = jnp.where(low, turn(lo, 64, 1), hi)
    total = [jnp.zeros((rows, cols), F32) for _ in range(4)]
    for k in range(used_ref.shape[0]):
        lane = pick_lane_ref[k]
        row = pick_row_ref[k]
        acc = [None] * 4
        for r in range(half):
            here = row == r
            for f in range(4):
                source = jnp.broadcast_to(tab[f, r : r + 1, :], lane.shape)
                value = jnp.take_along_axis(source, lane, axis=1)
                acc[f] = value if r == 0 else jnp.where(here, value, acc[f])
        used = used_ref[k]
        total = [t + a * used for t, a in zip(total, acc)]
    for f in range(4):
        flux_ref[f] = total[f]

    even = is_even("lon")
    one, two = one_ref[:rows], two_ref[:rows]
    east = jnp.where(even, one, two)
    west = jnp.where(even, two, one)
    lane = lanes(east.shape)
    from_east = lane < 64
    valid = (lane >= 32) & (lane < 96)
    owner = jnp.where(valid, jnp.where(from_east, east, turn(west, 32, 1)), 0.0).astype(jnp.int32)
    slot = jnp.where(valid, jnp.where(from_east, turn(east, -32, 1), west), 0.0).astype(jnp.int32)
    used = jnp.where(valid, jnp.where(from_east, turn(east, -64, 1), turn(west, -32, 1)), 0.0)
    slot = jnp.where(from_east, slot, slot + 64)
    for f in range(3):
        side[f] = table_ref[:, 0, 256 + f * 128 : 384 + f * 128]
    acc = [None] * 3
    for r in range(n_lon):
        here = owner == r
        for f in range(3):
            source = jnp.broadcast_to(side[f, r : r + 1, :], slot.shape)
            value = jnp.take_along_axis(source, slot, axis=1)
            acc[f] = value if r == 0 else jnp.where(here, value, acc[f])
    rim = []
    inner, outer = lane < HALO, lane >= cols - HALO
    for g in range(4):
        rim.append((turn(east, -g * HALO, 1), turn(west, cols - (g + 1) * HALO, 1)))
    for f in range(3):
        v = acc[f] * used
        v = v + turn(v, -16, 1)
        v = v + turn(v, -8, 1)
        rim.append((turn(v, -32, 1), turn(v, 56, 1)))
    rim = [jnp.where(inner, e, jnp.where(outer, w, 0.0)) for e, w in rim]
    for i in range(FIELDS):
        rim_ref[i] = rim[i]

    level_f = level_ref[...].astype(F32)
    own = (
        height_ref[...], transport_ref[0], transport_ref[1], level_f, total[1], total[2], total[3],
    )
    lane = lanes((HALO, cols))
    for s, at in ((0, rows - HALO), (1, 0)):
        cut = slice(at, at + HALO)
        rims = jnp.zeros((HALO, cols), F32)
        for i in range(FIELDS):
            pack[s, i * HALO : (i + 1) * HALO] = own[i][cut]
            start = 2 * HALO * i
            here = (lane >= start) & (lane < start + 2 * HALO)
            rims = jnp.where(here, turn(rim[i][cut], start + HALO, 1), rims)
        pack[s, ROW_RIM:ROW_T] = rims
        pack[s, ROW_T:] = rows_ref[s]
    even = is_even("lat")
    north_going, south_going = pack[0], pack[1]
    first_ref[...] = jnp.where(even, north_going, south_going)
    second_ref[...] = jnp.where(even, south_going, north_going)


def step_kernel(
    one_ref, two_ref, first_ref, second_ref, height_ref, transport_ref, level_ref, flux_ref, rim_ref,
    t_0_ref, rows_ref, inv_ref, diff_ref, t_ref, v_ref,
    t_out, height_out, transport_out, north_ref, south_flux,
):
    top = is_top()
    level = level_ref[...]
    level_f = level.astype(F32)
    rows, cols = level.shape
    depth = t_ref.shape[1]
    even = is_even("lat")
    a, b = first_ref[...], second_ref[...]
    south = jnp.where(even, b, a)
    north = jnp.where(even, a, b)
    mirrored = jnp.take_along_axis(north, 127 - lanes(north.shape), axis=1)
    north = jnp.where(top, mirrored, north)
    north_ref[...] = north
    even = is_even("lon")
    one, two = one_ref[rows:], two_ref[rows:]
    t_e = jnp.where(even, one, two)
    t_w = jnp.where(even, two, one)
    own = (
        height_ref[...], transport_ref[0], transport_ref[1], level_f,
        flux_ref[1], flux_ref[2], flux_ref[3],
    )
    ext = []
    lane = lanes((HALO, cols))
    side = (lane < HALO) | (lane >= cols - HALO)
    for i in range(FIELDS):
        at = slice(i * HALO, (i + 1) * HALO)
        whole = jnp.concatenate([south[at], own[i], north[at]], axis=0)
        start = jnp.where(top, cols - 2 * HALO * (FIELDS - i) - HALO, cols - 2 * HALO * i - HALO)
        north_rim = jnp.where(side, pltpu.roll(north[ROW_RIM:ROW_T], start, 1), 0.0)
        south_rim = jnp.where(side, turn(south[ROW_RIM:ROW_T], -(2 * HALO * i + HALO), 1), 0.0)
        rim = jnp.concatenate([south_rim, rim_ref[i], north_rim], axis=0)
        ext.append(jnp.concatenate([whole, rim], axis=1))


    def coefficients(f):
        wet = (f[LEVELS] > 0.0).astype(F32)
        return (
            wet,
            wave_grad * (f[LEVELS] / depth),
            fresh_gain * f[FRESH] * wet,
            wind_gain * f[WIND_E] * wet,
            wind_gain * f[WIND_N] * wet,
        )

    mine = [x for x in ext]
    fold = [x[HALO + rows :] for x in ext]
    wet, grad, fresh, wind_e, wind_n = coefficients(mine)
    p_wet, p_grad, p_fresh, p_wind_e, p_wind_n = coefficients(fold)
    h, e, n = mine[HEIGHT], mine[EAST], mine[NORTH]
    p_h, p_e, p_n = fold[HEIGHT], fold[EAST], fold[NORTH]
    row = rows_of(h.shape)
    last = HALO + rows - 1
    across = (row == last) & top
    p_last = rows_of(p_h.shape) == HALO - 1
    for _ in range(SUBSTEPS):
        h = (h - wave_div * ((e - turn(e, 1, 1)) + (n - turn(n, 1, 0)))) * wet + fresh
        p_h = (p_h - wave_div * ((p_e - turn(p_e, -1, 1)) + (p_n - turn(p_n, 1, 0)))) * p_wet + p_fresh
        h_n = jnp.where(across, jnp.broadcast_to(p_h[HALO - 1 :], h.shape), turn(h, -1, 0))
        p_h_n = jnp.where(p_last, jnp.broadcast_to(h[last : last + 1], p_h.shape), turn(p_h, -1, 0))
        e = (e - grad * (turn(h, -1, 1) - h)) * wet + wind_e
        n = (n - grad * (h_n - h)) * wet + wind_n
        p_e = (p_e - p_grad * (turn(p_h, 1, 1) - p_h)) * p_wet + p_wind_e
        p_n = (p_n - p_grad * (p_h_n - p_h)) * p_wet + p_wind_n
    inside = slice(HALO, HALO + rows)
    height_out[...] = h[inside, :cols]
    transport_out[0] = e[inside, :cols]
    transport_out[1] = n[inside, :cols]

    ext_level = ext[LEVELS]
    level_e = turn(ext_level, -1, 1)[inside, :cols]
    level_w = turn(ext_level, 1, 1)[inside, :cols]
    first = LEVELS * HALO
    level_n_row = jnp.where(top, north[first + HALO - 1 : first + HALO], north[first : first + 1])
    level_s_row = south[first + HALO - 1 : first + HALO]
    shape = (rows, cols)
    lane = lanes(shape)
    row = rows_of(shape)
    level_n = jnp.where(row == rows - 1, jnp.broadcast_to(level_n_row, shape), turn(level_f, -1, 0))
    face_e = jnp.minimum(level_f, level_e)
    face_n = jnp.minimum(level_f, level_n)
    face_s = jnp.minimum(level_f[0:1], level_s_row)
    t_0 = t_0_ref[...]
    u_w = jnp.where(lane < depth, turn(t_w, -2 * depth, 1), turn(t_w, -depth, 1))
    layer = jnp.where(lane < depth, lane, lane - depth).astype(F32)
    face_w = jnp.broadcast_to(jnp.minimum(level_f, level_w)[:, 0:1], shape)
    west_flux = jnp.where(layer < face_w, u_w * ((t_w + t_0) * 0.5), 0.0)
    for c in range(2):
        planes = slice(ROW_T + c * depth, ROW_T + (c + 1) * depth)
        flux = south[ROW_T + 2 * depth : ROW_T + 3 * depth] * (
            (south[planes] + rows_ref[1, c * depth : (c + 1) * depth]) * 0.5
        )
        deep = rows_of(flux.shape).astype(F32) < face_s
        south_flux[c * depth : (c + 1) * depth] = jnp.where(deep, flux, 0.0)

    diff = diff_ref[...]
    wet_0 = (level > 0).astype(F32)
    source = (heat_gain * flux_ref[0] * wet_0, -salt_gain * flux_ref[1] * wet_0)
    right = [None, None]
    for l in range(depth):
        mask_e = face_e > l
        mask_n = face_n > l
        u_l, v_l = v_ref[0, l], v_ref[1, l]
        above = jnp.where(level > l, diff, 0.0)
        inv = inv_ref[l]
        for c in range(2):
            f = c * depth + l
            t = t_ref[c, l]
            east = jnp.where(lane == cols - 1, turn(t_e, cols - 2 - f, 1), turn(t, -1, 1))
            flux_e = jnp.where(mask_e, u_l * ((t + east) * 0.5), 0.0)
            flux_w = jnp.where(lane == 0, turn(west_flux, -f, 1), turn(flux_e, 1, 1))
            north_row = jnp.broadcast_to(north_ref[ROW_T + f : ROW_T + f + 1], shape)
            up = jnp.where(row == rows - 1, north_row, turn(t, -1, 0))
            flux_n = jnp.where(mask_n, v_l * ((t + up) * 0.5), 0.0)
            south_row = jnp.broadcast_to(south_flux[f : f + 1], shape)
            flux_s = jnp.where(row == 0, south_row, turn(flux_n, 1, 0))
            forced = t - adv_rate * ((flux_e - flux_w) + (flux_n - flux_s))
            if l == 0:
                forced = forced + source[c]
                right[c] = forced * inv
            else:
                right[c] = (forced + above * right[c]) * inv
            t_out[c, l] = right[c]
    for l in range(depth - 2, -1, -1):
        below = jnp.where(level > l + 1, diff, 0.0) * inv_ref[l]
        for c in range(2):
            right[c] = t_out[c, l] + below * right[c]
            t_out[c, l] = right[c]


def vmem(count):
    return [pl.BlockSpec(memory_space=pltpu.VMEM)] * count


def params():
    return pltpu.CompilerParams(vmem_limit_bytes=24 * 1024 * 1024)


def shape_of(*shape):
    return jax.ShapeDtypeStruct(shape, F32)


def lat_pairs(n_lat, n_lon):
    def at(i, j):
        return i * n_lon + j

    first, second = [], []
    for j in range(n_lon):
        for i in range(0, n_lat, 2):
            first += [(at(i, j), at(i + 1, j)), (at(i + 1, j), at(i, j))]
        for i in range(1, n_lat - 1, 2):
            second += [(at(i, j), at(i + 1, j)), (at(i + 1, j), at(i, j))]
        second.append((at(n_lat - 1, j), at(n_lat - 1, n_lon - 1 - j)))
    return first, second


def lon_pairs(n_lon):
    first, second = [], []
    for j in range(0, n_lon, 2):
        first += [(j, j + 1), (j + 1, j)]
        k, m = j + 1, (j + 2) % n_lon
        second += [(k, m), (m, k)]
    return first, second


def per_device(
    tracers,
    velocity,
    diffusivity,
    ocean_levels,
    surface_height,
    transport,
    atm_flux,
    send_rows,
    src_owner,
    src_slot,
    xgrid_weights,
    xgrid_count,
):
    n_lat, n_lon = lax.axis_size("lat"), lax.axis_size("lon")
    depth, rows, cols = tracers.shape[1:]
    slots = send_rows.shape[3]
    picked = pl.pallas_call(
        pick_kernel,
        out_shape=shape_of(n_lon, 1, 10 * slots),
        in_specs=[pl.BlockSpec(memory_space=pl.ANY)] * 2,
        out_specs=vmem(1)[0],
        scratch_shapes=[
            pltpu.VMEM(atm_flux.shape, F32),
            pltpu.VMEM(send_rows.shape, jnp.int32),
            pltpu.SemaphoreType.DMA((2,)),
        ],
        compiler_params=params(),
        name="pick",
    )(atm_flux, send_rows)
    table = lax.all_to_all(picked, "lon", split_axis=0, concat_axis=0, tiled=True)

    block = (rows, cols)
    lat_rows = ROW_T + 3 * depth
    one, two, t_0, edge_rows, inv, pick_row, pick_lane, used = pl.pallas_call(
        edge_kernel,
        out_shape=(
            shape_of(2 * rows, cols),
            shape_of(2 * rows, cols),
            shape_of(*block),
            shape_of(2, 3 * depth, cols),
            shape_of(depth, *block),
            jax.ShapeDtypeStruct((4, *block), jnp.int32),
            jax.ShapeDtypeStruct((4, *block), jnp.int32),
            shape_of(4, *block),
        ),
        in_specs=[pl.BlockSpec(memory_space=pl.ANY)] + vmem(10),
        out_specs=vmem(8),
        compiler_params=params(),
        cost_estimate=pl.CostEstimate(flops=2000000, bytes_accessed=2000000, transcendentals=0),
        name="edges",
    )(
        picked, tracers, velocity, ocean_levels, diffusivity, surface_height, transport, src_owner, src_slot,
        xgrid_weights, xgrid_count,
    )
    pairs = lon_pairs(n_lon)
    two = lax.ppermute(two, "lon", pairs[1])
    one = lax.ppermute(one, "lon", pairs[0])

    flux, rim, first, second = pl.pallas_call(
        remap_kernel,
        out_shape=(
            shape_of(4, *block),
            shape_of(FIELDS, *block),
            shape_of(lat_rows, cols),
            shape_of(lat_rows, cols),
        ),
        in_specs=vmem(10),
        out_specs=vmem(4),
        scratch_shapes=[
            pltpu.VMEM((4, n_lon // 2, 128), F32),
            pltpu.VMEM((3, n_lon, 128), F32),
            pltpu.VMEM((2, lat_rows, cols), F32),
        ],
        compiler_params=params(),
        name="remap",
    )(
        table, one, two, pick_row, pick_lane, used, edge_rows, ocean_levels, surface_height, transport,
    )
    pairs = lat_pairs(n_lat, n_lon)
    second = lax.ppermute(second, ("lat", "lon"), pairs[1])
    first = lax.ppermute(first, ("lat", "lon"), pairs[0])

    return pl.pallas_call(
        step_kernel,
        out_shape=(shape_of(2, depth, rows, cols), shape_of(rows, cols), shape_of(2, rows, cols)),
        in_specs=vmem(15),
        out_specs=tuple(vmem(3)),
        scratch_shapes=[pltpu.VMEM((lat_rows, cols), F32), pltpu.VMEM((2 * depth, cols), F32)],
        compiler_params=params(),
        name="step",
    )(
        one, two, first, second, surface_height, transport, ocean_levels, flux, rim,
        t_0, edge_rows, inv, diffusivity, tracers, velocity,
    )


def solution(mesh):
    return jax.shard_map(
        per_device,
        mesh=mesh,
        in_specs=(
            P(None, None, "lat", "lon"),
            P(None, None, "lat", "lon"),
            P("lat", "lon"),
            P("lat", "lon"),
            P("lat", "lon"),
            P(None, "lat", "lon"),
            P("lat", None, "lon"),
            P("lat", "lon", None, None),
            P(None, "lat", "lon"),
            P(None, "lat", "lon"),
            P(None, "lat", "lon"),
            P("lat", "lon"),
        ),
        out_specs=(P(None, None, "lat", "lon"), P("lat", "lon"), P(None, "lat", "lon")),
        check_vma=False,
    )
```

time: 73.7 us -> 60 us (0.81)
  blocking collectives: 29.8 us -> 0 us
  starting transfers between devices: 10.4 us -> 39.1 us
  waiting for transfers between devices: 17.3 us -> 4.05 us
  Pallas kernels: 8.65 us -> 10.6 us
  local copies, waits for them, and re-layouts: 6.22 us -> 4.56 us
    all_to_all x1 -> x0, blocking collectives: 29.8 us -> none  [per_device(): lax.all_to_all(picked, 'lon', split_axis=0, concat_axis=0, tiled=True)]
    all_to_all x0 -> x1, starting transfers between devices: none -> 15.4 us  [per_device(): lax.all_to_all(picked, 'lon', split_axis=0, concat_axis=0, tiled=True)]
    ppermute x1, starting transfers between devices: 2.59 us -> 9.27 us  [per_device(): second = lax.ppermute(second, ('lat', 'lon'), pairs[1])]
    ppermute x1, starting transfers between devices: 3.16 us -> 9.64 us  [per_device(): two = lax.ppermute(two, 'lon', pairs[1])]
    ppermute x1, waiting for transfers between devices: 8.79 us -> 2.36 us  [per_device(): second = lax.ppermute(second, ('lat', 'lon'), pairs[1])]
    ppermute x1, waiting for transfers between devices: 7.99 us -> 1.69 us  [per_device(): two = lax.ppermute(two, 'lon', pairs[1])]
    pallas_call x4 -> x3, Pallas kernels: 4.02 us -> 6 us  [the longest x1 4.47 us: per_device(): pl.pallas_call(remap_kernel, out_shape=(shape_of(4, *block), shape_of(FIE...]
    unnamed x28, local copies, waits for them, and re-layouts: 6.22 us -> 4.56 us
  transfers between devices with their start and end apart: 4 -> 5, of which waited for: 3 -> 2; matrix products, arithmetic and copies ran while one was open for 0% -> 0% of each run, Pallas kernels for 1% -> 1%
where the time goes in v2:
time: 60 us; the launch traced here: 59.2 us
  starting transfers between devices  39.1 us (65%)
  Pallas kernels  10.6 us (18%)
  local copies, waits for them, and re-layouts  4.56 us (8%)
  waiting for transfers between devices  4.05 us (7%)
  between operations  0.83 us (1%)
    all_to_all x1, starting transfers between devices, per_device(): lax.all_to_all(picked, 'lon', split_axis=0, concat_axis=0, tiled=True)  15.4 us
    ppermute x1, starting transfers between devices, per_device(): two = lax.ppermute(two, 'lon', pairs[1])  9.64 us
    ppermute x1, starting transfers between devices, per_device(): second = lax.ppermute(second, ('lat', 'lon'), pairs[1])  9.27 us
    pallas_call x1, Pallas kernels, per_device(): pl.pallas_call(step_kernel, out_shape=(shape_of(2, depth, rows, cols), sh...  4.62 us
    unnamed x28, local copies, waits for them, and re-layouts  4.56 us
    pallas_call x1, Pallas kernels, per_device(): pl.pallas_call(remap_kernel, out_shape=(shape_of(4, *block), shape_of(FIE...  4.47 us
    ppermute x1, starting transfers between devices, per_device(): first = lax.ppermute(first, ('lat', 'lon'), pairs[0])  2.65 us
    ppermute x1, waiting for transfers between devices, per_device(): second = lax.ppermute(second, ('lat', 'lon'), pairs[1])  2.36 us
  transfers between devices with their start and end apart: 5, of which 2 were waited for; matrix products, arithmetic and copies ran while one was open for 0% of the time, Pallas kernels for 1%

profile of v2, /device:TPU:120, one launch (start us, length us, event | category | flops | bytes accessed | tf_op | source)
XLA Modules:
  0.0 59.2 jit_solution(16788433532219965477)
XLA Ops:
  0.6 0.0 copy-start.12
  0.6 0.7 %copy-done.12 = s32[1,1,32,64]{3,2,1,0:T(8,128)S(1)} copy-done((s32[1,1,32,64]{3,2,1,0:T(8,128)S(1)}, s32[1,1,32,64]{3,2,1,0:T(8,128)}, u32[]{:S(2)}) %copy-start.12) | copy-done | bytes 8216
  1.4 0.7 %copy-done.13 = f32[1,4,512]{2,1,0:T(4,128)S(1)} copy-done((f32[1,4,512]{2,1,0:T(4,128)S(1)}, f32[1,4,512]{2,1,0:T(4,128)}, u32[]{:S(2)}) %copy-start.13) | copy-done | bytes 8216
  2.0 1.0 %pick.1.picked_ref = f32[32,1,640]{2,1,0:T(1,128)} custom-call(f32[1,4,512]{2,1,0:T(4,128)S(1)} %copy-done.13, s32[1,1,32,64]{3,2,1,0:T(8,128)S(1)} %copy-done.12), custom_call_target="tpu_custom_call" | custom-call | tf_op jit(solution)/shard_map/pick/pallas_call | solution.py:412
  3.1 0.0 copy-start.4
  3.1 0.0 copy-start.5
  3.1 0.0 copy-start.6
  3.1 0.0 copy-start.7
  3.1 0.0 copy-start.8
  3.1 0.0 copy-start.11
  3.1 15.4 %all-to-all-start = ((f32[32,1,640]{2,1,0:T(1,128)}), f32[32,1,640]{2,1,0:T(1,128)S(1)}, u32[]{:S(2)}, u32[]{:S(2)}) async-start(f32[32,1,640]{2,1,0:T(1,128)} %pick.1.picked_ref), calls=%async_computation | async-start | bytes 163840 | tf_op jit(solution)/shard_map/all_to_all | solution.py:425
  18.5 0.0 copy-done.9
  18.5 0.0 copy-done.4
  18.5 0.0 copy-done.5
  18.6 0.0 copy-done.6
  18.6 0.0 copy-start
  18.6 1.1 %copy-done = f32[2,24,32,128]{3,2,1,0:T(8,128)S(1)} copy-done((f32[2,24,32,128]{3,2,1,0:T(8,128)S(1)}, f32[2,24,32,128]{3,2,1,0:T(8,128)}, u32[]{:S(2)}) %copy-start) | copy-done | bytes 786456
  19.7 1.1 %copy-done.2 = f32[2,24,32,128]{3,2,1,0:T(8,128)S(1)} copy-done((f32[2,24,32,128]{3,2,1,0:T(8,128)S(1)}, f32[2,24,32,128]{3,2,1,0:T(8,128)}, u32[]{:S(2)}) %copy-start.2) | copy-done | bytes 786456
  20.9 0.8 %copy-done.10 = f32[4,32,128]{2,1,0:T(8,128)S(1)} copy-done((f32[4,32,128]{2,1,0:T(8,128)S(1)}, f32[4,32,128]{2,1,0:T(8,128)}, u32[]{:S(2)}) %copy-start.10) | copy-done | bytes 65560
  21.7 0.5 edges.1
  22.2 2.2 %collective-permute-start = (f32[64,128]{1,0:T(8,128)S(1)}, f32[64,128]{1,0:T(8,128)S(1)}, u32[]{:S(2)}, u32[]{:S(2)}) collective-permute-start(f32[64,128]{1,0:T(8,128)S(1)} %get-tuple-element.15), channel_id=1, source_target_pairs={{0,1},{1,0},{2,3},{3,2},{4,5},{5,4},{6,7},{7,6},{8,9},{9,8},{10,11... | collective-permute-start | bytes 98312 | tf_op jit(solution)/shard_map/ppermute | solution.py:452
  24.4 9.6 %collective-permute-start.1 = (f32[64,128]{1,0:T(8,128)S(1)}, f32[64,128]{1,0:T(8,128)S(1)}, u32[]{:S(2)}, u32[]{:S(2)}) collective-permute-start(f32[64,128]{1,0:T(8,128)S(1)} %get-tuple-element.16), channel_id=1, source_target_pairs={{1,2},{2,1},{3,4},{4,3},{5,6},{6,5},{7,8},{8,7},{9,10},{10,9},{11,... | collective-permute-start | bytes 98312 | tf_op jit(solution)/shard_map/ppermute | solution.py:451
  34.1 0.0 collective-permute-done.one_ref
  34.1 1.7 %collective-permute-done.1.two_ref = f32[64,128]{1,0:T(8,128)S(1)} collective-permute-done((f32[64,128]{1,0:T(8,128)S(1)}, f32[64,128]{1,0:T(8,128)S(1)}, u32[]{:S(2)}, u32[]{:S(2)}) %collective-permute-start.1) | collective-permute-done | bytes 32800 | tf_op jit(solution)/shard_map/ppermute | solution.py:451
  35.8 0.0 all-to-all-done.table_ref
  35.8 4.5 %remap.1 = (f32[4,32,128]{2,1,0:T(8,128)S(1)}, f32[7,32,128]{2,1,0:T(8,128)S(1)}, f32[136,128]{1,0:T(8,128)S(1)}, f32[136,128]{1,0:T(8,128)S(1)}) custom-call(f32[32,1,640]{2,1,0:T(1,128)S(1)} %all-to-all-done.table_ref, f32[64,128]{1,0:T(8,128)S(1)} %collective-permute-done.one_ref, f32[64,128]{1,0:T(8,128)S(1)} %collective-permute-done.1.two_ref, ...), custom_call_target="tpu_custom_call" | custom-call | tf_op jit(solution)/shard_map/remap/pallas_call | solution.py:454
  40.3 2.7 %collective-permute-start.2 = (f32[136,128]{1,0:T(8,128)S(1)}, f32[136,128]{1,0:T(8,128)S(1)}, u32[]{:S(2)}, u32[]{:S(2)}) collective-permute-start(f32[136,128]{1,0:T(8,128)S(1)} %get-tuple-element.21), channel_id=1, source_target_pairs={{0,32},{32,0},{64,96},{96,64},{128,160},{160,128},{192,224},{224,1... | collective-permute-start | bytes 208904 | tf_op jit(solution)/shard_map/ppermute | solution.py:476
  42.9 9.3 %collective-permute-start.3 = (f32[136,128]{1,0:T(8,128)S(1)}, f32[136,128]{1,0:T(8,128)S(1)}, u32[]{:S(2)}, u32[]{:S(2)}) collective-permute-start(f32[136,128]{1,0:T(8,128)S(1)} %get-tuple-element.22), channel_id=1, source_target_pairs={{32,64},{64,32},{96,128},{128,96},{160,192},{192,160},{224,256},{2... | collective-permute-start | bytes 208904 | tf_op jit(solution)/shard_map/ppermute | solution.py:475
  52.2 0.0 collective-permute-done.2.first_ref
  52.2 2.4 %collective-permute-done.3.second_ref = f32[136,128]{1,0:T(8,128)S(1)} collective-permute-done((f32[136,128]{1,0:T(8,128)S(1)}, f32[136,128]{1,0:T(8,128)S(1)}, u32[]{:S(2)}, u32[]{:S(2)}) %collective-permute-start.3) | collective-permute-done | bytes 69664 | tf_op jit(solution)/shard_map/ppermute | solution.py:475
  54.6 0.0 copy-done.1
  54.6 4.6 %step.1 = (f32[2,24,32,128]{3,2,1,0:T(8,128)}, f32[32,128]{1,0:T(8,128)}, f32[2,32,128]{2,1,0:T(8,128)}) custom-call(f32[64,128]{1,0:T(8,128)S(1)} %collective-permute-done.one_ref, f32[64,128]{1,0:T(8,128)S(1)} %collective-permute-done.1.two_ref, f32[136,128]{1,0:T(8,128)S(1)} %collective-permute-done.2.first_ref, ...), custom_call_target="tpu_custom_call" | custom-call | tf_op jit(solution)/shard_map/step/pallas_call | solution.py:478
  (10 shorter events, 0.0 us)
Async XLA Ops:
  0.6 0.7 %copy-start.12 = (s32[1,1,32,64]{3,2,1,0:T(8,128)S(1)}, s32[1,1,32,64]{3,2,1,0:T(8,128)}, u32[]{:S(2)}) copy-start(s32[1,1,32,64]{3,2,1,0:T(8,128)} %rows_hbm.1) | copy-start | bytes 24580
  1.3 0.7 %copy-start.13 = (f32[1,4,512]{2,1,0:T(4,128)S(1)}, f32[1,4,512]{2,1,0:T(4,128)}, u32[]{:S(2)}) copy-start(f32[1,4,512]{2,1,0:T(4,128)} %atm_hbm.1) | copy-start | bytes 24580
  2.0 16.5 %copy-start.9 = (s32[4,32,128]{2,1,0:T(8,128)S(1)}, s32[4,32,128]{2,1,0:T(8,128)}, u32[]{:S(2)}) copy-start(s32[4,32,128]{2,1,0:T(8,128)} %slot_ref.1) | copy-start | bytes 196612
  3.1 15.5 %copy-start.4 = (f32[2,32,128]{2,1,0:T(8,128)S(1)}, f32[2,32,128]{2,1,0:T(8,128)}, u32[]{:S(2)}) copy-start(f32[2,32,128]{2,1,0:T(8,128)} %transport_ref.5) | copy-start | bytes 98308
  3.1 15.5 %copy-start.5 = (s32[32,128]{1,0:T(8,128)S(1)}, s32[32,128]{1,0:T(8,128)}, u32[]{:S(2)}) copy-start(s32[32,128]{1,0:T(8,128)} %level_ref.5) | copy-start | bytes 49156
  3.1 15.5 %copy-start.6 = (f32[32,128]{1,0:T(8,128)S(1)}, f32[32,128]{1,0:T(8,128)}, u32[]{:S(2)}) copy-start(f32[32,128]{1,0:T(8,128)} %height_ref.5) | copy-start | bytes 49156
  3.1 15.5 %copy-start.7 = (f32[32,128]{1,0:T(8,128)S(1)}, f32[32,128]{1,0:T(8,128)}, u32[]{:S(2)}) copy-start(f32[32,128]{1,0:T(8,128)} %diff_ref.3) | copy-start | bytes 49156
  3.1 15.5 %copy-start.8 = (s32[4,32,128]{2,1,0:T(8,128)S(1)}, s32[4,32,128]{2,1,0:T(8,128)}, u32[]{:S(2)}) copy-start(s32[4,32,128]{2,1,0:T(8,128)} %owner_ref.1) | copy-start | bytes 196612
  3.1 15.5 %copy-start.11 = (s32[32,128]{1,0:T(8,128)S(1)}, s32[32,128]{1,0:T(8,128)}, u32[]{:S(2)}) copy-start(s32[32,128]{1,0:T(8,128)} %count_ref.1) | copy-start | bytes 49156
  3.1 32.7 %all-to-all-start = ((f32[32,1,640]{2,1,0:T(1,128)}), f32[32,1,640]{2,1,0:T(1,128)S(1)}, u32[]{:S(2)}, u32[]{:S(2)}) async-start(f32[32,1,640]{2,1,0:T(1,128)} %pick.1.picked_ref), calls=%async_computation | async-start | bytes 163840 | tf_op jit(solution)/shard_map/all_to_all | solution.py:425
  18.6 1.1 %copy-start = (f32[2,24,32,128]{3,2,1,0:T(8,128)S(1)}, f32[2,24,32,128]{3,2,1,0:T(8,128)}, u32[]{:S(2)}) copy-start(f32[2,24,32,128]{3,2,1,0:T(8,128)} %t_ref.3) | copy-start | bytes 2359300
  19.7 1.1 %copy-start.2 = (f32[2,24,32,128]{3,2,1,0:T(8,128)S(1)}, f32[2,24,32,128]{3,2,1,0:T(8,128)}, u32[]{:S(2)}) copy-start(f32[2,24,32,128]{3,2,1,0:T(8,128)} %v_ref.3) | copy-start | bytes 2359300
  20.9 0.8 %copy-start.10 = (f32[4,32,128]{2,1,0:T(8,128)S(1)}, f32[4,32,128]{2,1,0:T(8,128)}, u32[]{:S(2)}) copy-start(f32[4,32,128]{2,1,0:T(8,128)} %weight_ref.1) | copy-start | bytes 196612
  21.7 32.9 %copy-start.1 = (f32[2,24,32,128]{3,2,1,0:T(8,128)S(1)}, f32[2,24,32,128]{3,2,1,0:T(8,128)}, u32[]{:S(2)}) copy-start(f32[2,24,32,128]{3,2,1,0:T(8,128)} %t_ref.3) | copy-start | bytes 2359300
  21.7 32.9 %copy-start.3 = (f32[2,24,32,128]{3,2,1,0:T(8,128)S(1)}, f32[2,24,32,128]{3,2,1,0:T(8,128)}, u32[]{:S(2)}) copy-start(f32[2,24,32,128]{3,2,1,0:T(8,128)} %v_ref.3) | copy-start | bytes 2359300
  22.2 11.8 %collective-permute-start = (f32[64,128]{1,0:T(8,128)S(1)}, f32[64,128]{1,0:T(8,128)S(1)}, u32[]{:S(2)}, u32[]{:S(2)}) collective-permute-start(f32[64,128]{1,0:T(8,128)S(1)} %get-tuple-element.15), channel_id=1, source_target_pairs={{0,1},{1,0},{2,3},{3,2},{4,5},{5,4},{6,7},{7,6},{8,9},{9,8},{10,11... | collective-permute-start | bytes 98312 | tf_op jit(solution)/shard_map/ppermute | solution.py:452
  24.4 11.3 %collective-permute-start.1 = (f32[64,128]{1,0:T(8,128)S(1)}, f32[64,128]{1,0:T(8,128)S(1)}, u32[]{:S(2)}, u32[]{:S(2)}) collective-permute-start(f32[64,128]{1,0:T(8,128)S(1)} %get-tuple-element.16), channel_id=1, source_target_pairs={{1,2},{2,1},{3,4},{4,3},{5,6},{6,5},{7,8},{8,7},{9,10},{10,9},{11,... | collective-permute-start | bytes 98312 | tf_op jit(solution)/shard_map/ppermute | solution.py:451
  40.3 11.9 %collective-permute-start.2 = (f32[136,128]{1,0:T(8,128)S(1)}, f32[136,128]{1,0:T(8,128)S(1)}, u32[]{:S(2)}, u32[]{:S(2)}) collective-permute-start(f32[136,128]{1,0:T(8,128)S(1)} %get-tuple-element.21), channel_id=1, source_target_pairs={{0,32},{32,0},{64,96},{96,64},{128,160},{160,128},{192,224},{224,1... | collective-permute-start | bytes 208904 | tf_op jit(solution)/shard_map/ppermute | solution.py:476
  42.9 11.6 %collective-permute-start.3 = (f32[136,128]{1,0:T(8,128)S(1)}, f32[136,128]{1,0:T(8,128)S(1)}, u32[]{:S(2)}, u32[]{:S(2)}) collective-permute-start(f32[136,128]{1,0:T(8,128)S(1)} %get-tuple-element.22), channel_id=1, source_target_pairs={{32,64},{64,32},{96,128},{128,96},{160,192},{192,160},{224,256},{2... | collective-permute-start | bytes 208904 | tf_op jit(solution)/shard_map/ppermute | solution.py:475

commit v3 on v2

v3 whole, which is shorter than its diff:
```python
import jax
import jax.numpy as jnp
from jax import lax
from jax.experimental import pallas as pl
from jax.experimental.pallas import tpu as pltpu
from jax.sharding import PartitionSpec as P

SUBSTEPS = 6
HALO = 8
FIELDS = 7
HEIGHT, EAST, NORTH, LEVELS, FRESH, WIND_E, WIND_N = range(FIELDS)
ROW_RIM = FIELDS * HALO
ROW_T = ROW_RIM + HALO
LISTS = 256
OWNER, SLOT, USED = 32, 64, 96

adv_rate = 0.1
heat_gain = 0.5
salt_gain = 0.5
wave_div = 0.5
wave_grad = 0.8
fresh_gain = 0.2
wind_gain = 0.2

F32 = jnp.float32


def lanes(shape):
    return lax.broadcasted_iota(jnp.int32, shape, len(shape) - 1)


def rows_of(shape):
    return lax.broadcasted_iota(jnp.int32, shape, len(shape) - 2)


def turn(x, by, axis):
    size = x.shape[axis]
    by = by % size
    return x if by == 0 else pltpu.roll(x, by, axis)


def is_even(axis):
    return lax.rem(lax.axis_index(axis), 2) == 0


def is_top():
    return lax.axis_index("lat") == lax.axis_size("lat") - 1


def pick_kernel(atm_hbm, rows_hbm, out_ref, atm_ref, rows_ref, sems):
    copies = [
        pltpu.make_async_copy(atm_hbm, atm_ref, sems.at[0]),
        pltpu.make_async_copy(rows_hbm, rows_ref, sems.at[1]),
    ]
    for copy in copies:
        copy.start()
    for copy in copies:
        copy.wait()
    rows = rows_ref[0, 0]
    both = jnp.concatenate([rows, rows], axis=1)
    lane = both & 127
    part = both >> 7
    low = lanes(both.shape) < 64
    values = []
    for f in range(4):
        acc = None
        for k in range(atm_ref.shape[2] // 128):
            row = jnp.broadcast_to(atm_ref[0, f : f + 1, k * 128 : (k + 1) * 128], both.shape)
            value = jnp.take_along_axis(row, lane, axis=1)
            acc = value if k == 0 else jnp.where(part == k, value, acc)
        values.append(acc)
    out_ref[:, 0, 0:128] = jnp.where(low, values[0], values[1])
    out_ref[:, 0, 128:256] = jnp.where(low, values[2], values[3])
    for f in range(1, 4):
        at = 128 + f * 128
        out_ref[:, 0, at : at + 128] = jnp.where(low, turn(values[f], -1, 0), turn(values[f], 1, 0))


def edge_kernel(
    picked_ref, t_hbm, v_hbm, level_ref, height_ref, transport_ref, owner_ref, slot_ref, weight_ref, count_ref,
    two_ref, one_ref, t_0_ref, rows_ref, pick_row_ref, pick_lane_ref, used_ref, t_ref, v_ref, sems,
):
    copies = [
        pltpu.make_async_copy(t_hbm.at[0], t_ref.at[0], sems.at[0]),
        pltpu.make_async_copy(v_hbm.at[0], v_ref.at[0], sems.at[1]),
        pltpu.make_async_copy(t_hbm.at[1], t_ref.at[1], sems.at[2]),
        pltpu.make_async_copy(v_hbm.at[1], v_ref.at[1], sems.at[3]),
    ]
    for copy in copies:
        copy.start()
    depth = t_ref.shape[1]
    shape = t_ref.shape[2:]
    rows, cols = shape
    lane = lanes(shape)
    level = level_ref[...]
    half = lax.axis_size("lon") // 2
    count = count_ref[...]
    for k in range(owner_ref.shape[0]):
        owner = owner_ref[k]
        high = owner >= half
        pick_row_ref[k] = jnp.where(high, owner - half, owner)
        pick_lane_ref[k] = jnp.where(high, slot_ref[k] + 64, slot_ref[k])
        used_ref[k] = jnp.where(count > k, weight_ref[k], 0.0)
    fields = [height_ref[...], transport_ref[0], transport_ref[1], level.astype(F32)]
    fields += [owner_ref[k].astype(F32) for k in range(4)]
    fields += [slot_ref[k].astype(F32) for k in range(4)]
    fields += [used_ref[k] for k in range(4)]
    west = jnp.zeros(shape, F32)
    east = jnp.zeros(shape, F32)
    for g, field in enumerate(fields):
        here = (lane >= g * HALO) & (lane < (g + 1) * HALO)
        west = jnp.where(here, turn(field, g * HALO, 1), west)
        east = jnp.where(here, turn(field, (g + 1) * HALO, 1), east)
    west_t = jnp.zeros(shape, F32)
    east_t = jnp.zeros(shape, F32)
    for c in range(2):
        copies[2 * c].wait()
        for l in range(depth):
            f = c * depth + l
            moved = turn(t_ref[c, l], f + 1, 1)
            west_t = jnp.where(lane == f + 1, moved, west_t)
            east_t = jnp.where(lane == f, moved, east_t)
    copies[1].wait()
    for l in range(depth):
        at = 2 * depth + l
        east_t = jnp.where(lane == at, turn(v_ref[0, l], at + 1, 1), east_t)
    even = is_even("lon")
    one_ref[:rows] = jnp.where(even, east, west)
    two_ref[:rows] = jnp.where(even, west, east)
    one_ref[rows:] = jnp.where(even, east_t, west_t)
    two_ref[rows:] = jnp.where(even, west_t, east_t)
    t_0_ref[...] = turn(west_t, -1, 1)
    for c in range(2):
        for l in range(depth):
            at = c * depth + l
            rows_ref[0, at : at + 1] = t_ref[c, l, rows - 1 : rows]
            rows_ref[1, at : at + 1] = t_ref[c, l, 0:1]
    copies[3].wait()
    for l in range(depth):
        at = 2 * depth + l
        rows_ref[0, at : at + 1] = v_ref[1, l, rows - 1 : rows]
    rows_ref[1, 2 * depth :] = jnp.zeros((depth, cols), F32)

def own_lookup(tab, row_ref, lane_ref, used_ref, cut, fields):
    total = {f: None for f in fields}
    for k in range(used_ref.shape[0]):
        lane = lane_ref[k, cut]
        row = row_ref[k, cut]
        acc = {}
        for r in range(tab.shape[1]):
            here = row == r
            for f in fields:
                source = jnp.broadcast_to(tab[f, r : r + 1, :], lane.shape)
                value = jnp.take_along_axis(source, lane, axis=1)
                acc[f] = value if r == 0 else jnp.where(here, value, acc[f])
        used = used_ref[k, cut]
        for f in fields:
            total[f] = acc[f] * used if k == 0 else total[f] + acc[f] * used
    return total


def rim_of(east, west, by_east, by_west):
    lane = lanes(east.shape)
    outer = jnp.where(lane >= 128 - HALO, turn(west, by_west, 1), 0.0)
    return jnp.where(lane < HALO, turn(east, by_east, 1), outer)


def from_lon(one_ref, two_ref, cut):
    even = is_even("lon")
    one, two = one_ref[cut], two_ref[cut]
    return jnp.where(even, one, two), jnp.where(even, two, one)


def state_rims(east, west):
    return [rim_of(east, west, -g * HALO, 128 - (g + 1) * HALO) for g in range(4)]


def side_lookup(side, east, west):
    lane = lanes(east.shape)
    from_east = lane < 64
    valid = (lane >= 32) & (lane < 96)
    owner = jnp.where(valid, jnp.where(from_east, east, turn(west, 32, 1)), 0.0).astype(jnp.int32)
    slot = jnp.where(valid, jnp.where(from_east, turn(east, -32, 1), west), 0.0).astype(jnp.int32)
    used = jnp.where(valid, jnp.where(from_east, turn(east, -64, 1), turn(west, -32, 1)), 0.0)
    slot = jnp.where(from_east, slot, slot + 64)
    acc = [None] * 3
    for r in range(side.shape[1]):
        here = owner == r
        for f in range(3):
            source = jnp.broadcast_to(side[f, r : r + 1, :], slot.shape)
            value = jnp.take_along_axis(source, slot, axis=1)
            acc[f] = value if r == 0 else jnp.where(here, value, acc[f])
    rims = []
    for f in range(3):
        v = acc[f] * used
        v = v + turn(v, -16, 1)
        v = v + turn(v, -8, 1)
        rims.append(rim_of(v, v, -32, 56))
    return rims


def rim_lookup_kernel(
    table_ref, two_ref, one_ref, pick_row_ref, pick_lane_ref, used_ref, rows_ref, level_ref, height_ref,
    transport_ref, after_ref, second_ref, first_ref, flux_ref, rim_ref, tab, side, pack,
):
    n_lon = table_ref.shape[0]
    half = n_lon // 2
    rows, cols = height_ref.shape
    low = lanes((half, 128)) < 64
    for pair in range(2):
        part = table_ref[:, 0, pair * 128 : (pair + 1) * 128]
        lo, hi = part[:half], part[half:]
        tab[2 * pair] = jnp.where(low, lo, turn(hi, 64, 1))
        tab[2 * pair + 1] = jnp.where(low, turn(lo, 64, 1), hi)
    for f in range(3):
        side[f] = table_ref[:, 0, LISTS + f * 128 : LISTS + (f + 1) * 128]
    lane = lanes((HALO, cols))
    for s, at in ((0, rows - HALO), (1, 0)):
        cut = slice(at, at + HALO)
        found = own_lookup(tab, pick_row_ref, pick_lane_ref, used_ref, cut, (1, 2, 3))
        east, west = from_lon(one_ref, two_ref, cut)
        rims = side_lookup(side, east, west)
        for f in range(3):
            flux_ref[s, f] = found[f + 1]
            rim_ref[s, f] = rims[f]
        rims = state_rims(east, west) + rims
        own = [
            height_ref[cut], transport_ref[0, cut], transport_ref[1, cut], level_ref[cut].astype(F32),
            found[1], found[2], found[3],
        ]
        packed = jnp.zeros((HALO, cols), F32)
        for i in range(FIELDS):
            pack[s, i * HALO : (i + 1) * HALO] = own[i]
            start = 2 * HALO * i
            here = (lane >= start) & (lane < start + 2 * HALO)
            packed = jnp.where(here, turn(rims[i], start + HALO, 1), packed)
        pack[s, ROW_RIM:ROW_T] = packed
        pack[s, ROW_T:] = rows_ref[s]
    even = is_even("lat")
    north_going, south_going = pack[0], pack[1]
    second_ref[...] = jnp.where(even, south_going, north_going)
    first_ref[...] = jnp.where(even, north_going, south_going)


def lookup_kernel(
    edge_flux_ref, edge_rim_ref, tab, side, two_ref, one_ref, pick_row_ref, pick_lane_ref, used_ref,
    flux_ref, rim_ref,
):
    rows = used_ref.shape[1]
    for at in range(0, rows, HALO):
        cut = slice(at, at + HALO)
        inner = 0 < at < rows - HALO
        found = own_lookup(tab, pick_row_ref, pick_lane_ref, used_ref, cut, (0, 1, 2, 3) if inner else (0,))
        s = 1 if at == 0 else 0
        flux_ref[0, cut] = found[0]
        for f in range(1, 4):
            flux_ref[f, cut] = found[f] if inner else edge_flux_ref[s, f - 1]
        east, west = from_lon(one_ref, two_ref, cut)
        rims = state_rims(east, west)
        if inner:
            rims += side_lookup(side, east, west)
        else:
            rims += [edge_rim_ref[s, f] for f in range(3)]
        for i in range(FIELDS):
            rim_ref[i, cut] = rims[i]


def tracer_kernel(
    two_ref, one_ref, t_0_ref, level_ref, diff_ref, t_ref, v_ref, x_ref, unit_ref, inv_rows_ref, gain_ref,
):
    depth, rows, cols = t_ref.shape[1:]
    shape = (rows, cols)
    east, west = from_lon(one_ref, two_ref, slice(0, rows))
    t_e, t_w = from_lon(one_ref, two_ref, slice(rows, 2 * rows))
    level = level_ref[...]
    level_f = level.astype(F32)
    lane = lanes(shape)
    row = rows_of(shape)
    first = LEVELS * HALO
    last = cols - 1
    level_e = jnp.where(lane == last, turn(east, last - first, 1), turn(level_f, -1, 1))
    level_n = turn(level_f, -1, 0)
    face_e = jnp.minimum(level_f, level_e)
    face_n = jnp.where(row == rows - 1, 0.0, jnp.minimum(level_f, level_n))
    t_0 = t_0_ref[...]
    u_w = jnp.where(lane < depth, turn(t_w, -2 * depth, 1), turn(t_w, -depth, 1))
    layer = jnp.where(lane < depth, lane, lane - depth).astype(F32)
    level_w = west[:, first + HALO - 1 : first + HALO]
    face_w = jnp.broadcast_to(jnp.minimum(level_f[:, 0:1], level_w), shape)
    west_flux = jnp.where(layer < face_w, u_w * ((t_w + t_0) * 0.5), 0.0)
    diff = diff_ref[...]
    above = jnp.zeros(shape, F32)
    inv = None
    right = [None, None, None]
    for l in range(depth):
        below = jnp.where(level > l + 1, diff, 0.0) if l < depth - 1 else jnp.zeros(shape, F32)
        pivot = 1.0 + above + below
        if l > 0:
            pivot = pivot - above * above * inv
        inv = 1.0 / pivot
        inv_rows_ref[0, l : l + 1] = inv[rows - 1 : rows]
        inv_rows_ref[1, l : l + 1] = inv[0:1]
        gain_ref[l] = below * inv
        mask_e = face_e > l
        mask_n = face_n > l
        u_l, v_l = v_ref[0, l] * 0.5, v_ref[1, l] * 0.5
        for c in range(2):
            f = c * depth + l
            t = t_ref[c, l]
            t_east = jnp.where(lane == last, turn(t_e, last - 1 - f, 1), turn(t, -1, 1))
            flux_e = jnp.where(mask_e, u_l * (t + t_east), 0.0)
            flux_w = jnp.where(lane == 0, turn(west_flux, -f, 1), turn(flux_e, 1, 1))
            flux_n = jnp.where(mask_n, v_l * (t + turn(t, -1, 0)), 0.0)
            flux_s = turn(flux_n, 1, 0)
            forced = t - adv_rate * ((flux_e - flux_w) + (flux_n - flux_s))
            right[c] = forced * inv if l == 0 else (forced + above * right[c]) * inv
            x_ref[c, l] = right[c]
        right[2] = inv if l == 0 else above * right[2] * inv
        unit_ref[l] = right[2]
        above = below
    for l in range(depth - 2, -1, -1):
        gain = gain_ref[l]
        for c in range(2):
            right[c] = x_ref[c, l] + gain * right[c]
            x_ref[c, l] = right[c]
        right[2] = unit_ref[l] + gain * right[2]
        unit_ref[l] = right[2]


def step_kernel(
    second_ref, first_ref, height_ref, transport_ref, level_ref, diff_ref, flux_ref, rim_ref, rows_ref, inv_rows_ref,
    x_ref, unit_ref, t_out, height_out, transport_out, north_ref, shift, fixed, sems,
):
    top = is_top()
    level = level_ref[...]
    level_f = level.astype(F32)
    rows, cols = level.shape
    depth = x_ref.shape[1]
    even = is_even("lat")
    a, b = first_ref[...], second_ref[...]
    south = jnp.where(even, b, a)
    north = jnp.where(even, a, b)
    mirrored = jnp.take_along_axis(north, 127 - lanes(north.shape), axis=1)
    north = jnp.where(top, mirrored, north)
    north_ref[...] = north

    first = LEVELS * HALO
    level_n = jnp.where(top, north[first + HALO - 1 : first + HALO], north[first : first + 1])
    level_s = south[first + HALO - 1 : first + HALO]
    sides = ((north, level_n, rows - 1, -adv_rate), (south, level_s, 0, adv_rate))
    chains = []
    for s, (message, level_out, at, gain) in enumerate(sides):
        level_in = level_f[at : at + 1]
        face = jnp.minimum(level_in, level_out)
        speed = rows_ref[0, 2 * depth :] if s == 0 else message[ROW_T + 2 * depth :]
        for c in range(2):
            planes = slice(c * depth, (c + 1) * depth)
            outside = message[ROW_T + c * depth : ROW_T + (c + 1) * depth]
            flux = speed * ((outside + rows_ref[s, planes]) * 0.5)
            deep = rows_of(flux.shape).astype(F32) < face
            shift[s, planes] = jnp.where(deep, gain * flux, 0.0)
            chains.append((s, c, level_in, diff_ref[at : at + 1]))
    right = [None] * 4
    for l in range(depth):
        for i, (s, c, level_in, diff_in) in enumerate(chains):
            at = c * depth + l
            inv = inv_rows_ref[s, l : l + 1]
            value = shift[s, at : at + 1]
            if l > 0:
                value = value + jnp.where(level_in > l, diff_in, 0.0) * right[i]
            right[i] = value * inv
            shift[s, at : at + 1] = right[i]
    for l in range(depth - 2, -1, -1):
        for i, (s, c, level_in, diff_in) in enumerate(chains):
            at = c * depth + l
            inv = inv_rows_ref[s, l : l + 1]
            below = jnp.where(level_in > l + 1, diff_in, 0.0) * inv
            right[i] = shift[s, at : at + 1] + below * right[i]
            shift[s, at : at + 1] = right[i]
    wet_0 = (level > 0).astype(F32)
    source = (heat_gain * flux_ref[0] * wet_0, -salt_gain * flux_ref[1] * wet_0)
    row = rows_of((HALO, cols))
    lo, hi = slice(0, HALO), slice(rows - HALO, rows)
    mid = slice(HALO, rows - HALO)
    copies = []
    for c in range(2):
        for l in range(depth):
            at = c * depth + l
            x = x_ref[c, l] + unit_ref[l] * source[c]
            add_s = jnp.broadcast_to(shift[1, at : at + 1], (HALO, cols))
            add_n = jnp.broadcast_to(shift[0, at : at + 1], (HALO, cols))
            fixed[c, l, lo] = x[lo] + jnp.where(row == 0, add_s, 0.0)
            fixed[c, l, mid] = x[mid]
            fixed[c, l, hi] = x[hi] + jnp.where(row == HALO - 1, add_n, 0.0)
        copies.append(pltpu.make_async_copy(fixed.at[c], t_out.at[c], sems.at[c]))
        copies[c].start()

    own = (
        height_ref[...], transport_ref[0], transport_ref[1], level_f,
        flux_ref[1], flux_ref[2], flux_ref[3],
    )
    ext = []
    lane = lanes((HALO, cols))
    side = (lane < HALO) | (lane >= cols - HALO)
    for i in range(FIELDS):
        at = slice(i * HALO, (i + 1) * HALO)
        whole = jnp.concatenate([south[at], own[i], north[at]], axis=0)
        start = jnp.where(top, cols - 2 * HALO * (FIELDS - i) - HALO, cols - 2 * HALO * i - HALO)
        north_rim = jnp.where(side, pltpu.roll(north[ROW_RIM:ROW_T], start, 1), 0.0)
        south_rim = jnp.where(side, turn(south[ROW_RIM:ROW_T], -(2 * HALO * i + HALO), 1), 0.0)
        rim = jnp.concatenate([south_rim, rim_ref[i], north_rim], axis=0)
        ext.append(jnp.concatenate([whole, rim], axis=1))


    def coefficients(f):
        wet = (f[LEVELS] > 0.0).astype(F32)
        return (
            wet,
            wave_grad * (f[LEVELS] / depth),
            fresh_gain * f[FRESH] * wet,
            wind_gain * f[WIND_E] * wet,
            wind_gain * f[WIND_N] * wet,
        )

    mine = [x for x in ext]
    fold = [x[HALO + rows :] for x in ext]
    wet, grad, fresh, wind_e, wind_n = coefficients(mine)
    p_wet, p_grad, p_fresh, p_wind_e, p_wind_n = coefficients(fold)
    h, e, n = mine[HEIGHT], mine[EAST], mine[NORTH]
    p_h, p_e, p_n = fold[HEIGHT], fold[EAST], fold[NORTH]
    row = rows_of(h.shape)
    last = HALO + rows - 1
    across = (row == last) & top
    p_last = rows_of(p_h.shape) == HALO - 1
    for _ in range(SUBSTEPS):
        h = (h - wave_div * ((e - turn(e, 1, 1)) + (n - turn(n, 1, 0)))) * wet + fresh
        p_h = (p_h - wave_div * ((p_e - turn(p_e, -1, 1)) + (p_n - turn(p_n, 1, 0)))) * p_wet + p_fresh
        h_n = jnp.where(across, jnp.broadcast_to(p_h[HALO - 1 :], h.shape), turn(h, -1, 0))
        p_h_n = jnp.where(p_last, jnp.broadcast_to(h[last : last + 1], p_h.shape), turn(p_h, -1, 0))
        e = (e - grad * (turn(h, -1, 1) - h)) * wet + wind_e
        n = (n - grad * (h_n - h)) * wet + wind_n
        p_e = (p_e - p_grad * (turn(p_h, 1, 1) - p_h)) * p_wet + p_wind_e
        p_n = (p_n - p_grad * (p_h_n - p_h)) * p_wet + p_wind_n
    inside = slice(HALO, HALO + rows)
    height_out[...] = h[inside, :cols]
    transport_out[0] = e[inside, :cols]
    transport_out[1] = n[inside, :cols]

    for copy in copies:
        copy.wait()


def vmem(count):
    return [pl.BlockSpec(memory_space=pltpu.VMEM)] * count


def params(mib=24):
    return pltpu.CompilerParams(vmem_limit_bytes=mib * 1024 * 1024)


def work(mb):
    return pl.CostEstimate(flops=mb * 1000000, bytes_accessed=mb * 1000000, transcendentals=0)


def in_hbm(x):
    return pltpu.with_memory_space_constraint(x, pltpu.HBM)


def shape_of(*shape):
    return jax.ShapeDtypeStruct(shape, F32)


def lat_pairs(n_lat, n_lon):
    def at(i, j):
        return i * n_lon + j

    first, second = [], []
    for j in range(n_lon):
        for i in range(0, n_lat, 2):
            first += [(at(i, j), at(i + 1, j)), (at(i + 1, j), at(i, j))]
        for i in range(1, n_lat - 1, 2):
            second += [(at(i, j), at(i + 1, j)), (at(i + 1, j), at(i, j))]
        second.append((at(n_lat - 1, j), at(n_lat - 1, n_lon - 1 - j)))
    return first, second


def lon_pairs(n_lon):
    first, second = [], []
    for j in range(0, n_lon, 2):
        first += [(j, j + 1), (j + 1, j)]
        k, m = j + 1, (j + 2) % n_lon
        second += [(k, m), (m, k)]
    return first, second


def per_device(
    tracers,
    velocity,
    diffusivity,
    ocean_levels,
    surface_height,
    transport,
    atm_flux,
    send_rows,
    src_owner,
    src_slot,
    xgrid_weights,
    xgrid_count,
):
    n_lat, n_lon = lax.axis_size("lat"), lax.axis_size("lon")
    depth, rows, cols = tracers.shape[1:]
    slots = send_rows.shape[3]
    picked = pl.pallas_call(
        pick_kernel,
        out_shape=shape_of(n_lon, 1, 10 * slots),
        in_specs=[pl.BlockSpec(memory_space=pltpu.HBM)] * 2,
        out_specs=vmem(1)[0],
        scratch_shapes=[
            pltpu.VMEM(atm_flux.shape, F32),
            pltpu.VMEM(send_rows.shape, jnp.int32),
            pltpu.SemaphoreType.DMA((2,)),
        ],
        compiler_params=params(24),
        cost_estimate=work(40),
        name="pick",
    )(in_hbm(atm_flux), in_hbm(send_rows))
    table = lax.all_to_all(picked, "lon", split_axis=0, concat_axis=0, tiled=True)

    block = (rows, cols)
    lat_rows = ROW_T + 3 * depth
    two, one, t_0, edge_rows, pick_row, pick_lane, used, tracers, velocity = pl.pallas_call(
        edge_kernel,
        out_shape=(
            shape_of(2 * rows, cols),
            shape_of(2 * rows, cols),
            shape_of(*block),
            shape_of(2, 3 * depth, cols),
            jax.ShapeDtypeStruct((4, *block), jnp.int32),
            jax.ShapeDtypeStruct((4, *block), jnp.int32),
            shape_of(4, *block),
            shape_of(2, depth, *block),
            shape_of(2, depth, *block),
        ),
        in_specs=[pl.BlockSpec(memory_space=pl.ANY)] + [pl.BlockSpec(memory_space=pltpu.HBM)] * 2 + vmem(7),
        out_specs=vmem(9),
        scratch_shapes=[pltpu.SemaphoreType.DMA((4,))],
        compiler_params=params(),
        cost_estimate=work(2),
        name="edges",
    )(
        picked, in_hbm(tracers), in_hbm(velocity), ocean_levels, surface_height, transport, src_owner, src_slot,
        xgrid_weights, xgrid_count,
    )
    pairs = lon_pairs(n_lon)
    two = lax.ppermute(two, "lon", pairs[1])
    one = lax.ppermute(one, "lon", pairs[0])

    solved, unit, inv_rows = pl.pallas_call(
        tracer_kernel,
        out_shape=(shape_of(2, depth, *block), shape_of(depth, *block), shape_of(2, depth, cols)),
        in_specs=vmem(7),
        out_specs=vmem(3),
        scratch_shapes=[pltpu.VMEM((depth, *block), F32)],
        compiler_params=params(),
        cost_estimate=work(8),
        name="tracers",
    )(two, one, t_0, ocean_levels, diffusivity, tracers, velocity)

    second, first, edge_flux, edge_rim, tab, side = pl.pallas_call(
        rim_lookup_kernel,
        out_shape=(
            shape_of(lat_rows, cols),
            shape_of(lat_rows, cols),
            shape_of(2, 3, HALO, cols),
            shape_of(2, 3, HALO, cols),
            shape_of(4, n_lon // 2, 128),
            shape_of(3, n_lon, 128),
        ),
        in_specs=vmem(10) + [pl.BlockSpec(memory_space=pl.ANY)],
        out_specs=vmem(6),
        scratch_shapes=[pltpu.VMEM((2, lat_rows, cols), F32)],
        compiler_params=params(),
        cost_estimate=work(8),
        name="rim_lookup",
    )(
        table, two, one, pick_row, pick_lane, used, edge_rows, ocean_levels, surface_height, transport,
        inv_rows,
    )
    pairs = lat_pairs(n_lat, n_lon)
    second = lax.ppermute(second, ("lat", "lon"), pairs[1])
    first = lax.ppermute(first, ("lat", "lon"), pairs[0])

    flux, rim = pl.pallas_call(
        lookup_kernel,
        out_shape=(shape_of(4, *block), shape_of(FIELDS, *block)),
        in_specs=vmem(9),
        out_specs=vmem(2),
        compiler_params=params(),
        cost_estimate=work(8),
        name="lookup",
    )(edge_flux, edge_rim, tab, side, two, one, pick_row, pick_lane, used)

    return pl.pallas_call(
        step_kernel,
        out_shape=(shape_of(2, depth, rows, cols), shape_of(rows, cols), shape_of(2, rows, cols)),
        in_specs=vmem(12),
        out_specs=(pl.BlockSpec(memory_space=pl.ANY), *vmem(2)),
        scratch_shapes=[
            pltpu.VMEM((lat_rows, cols), F32),
            pltpu.VMEM((2, 2 * depth, cols), F32),
            pltpu.VMEM((2, depth, rows, cols), F32),
            pltpu.SemaphoreType.DMA((2,)),
        ],
        compiler_params=params(),
        name="step",
    )(
        second, first, surface_height, transport, ocean_levels, diffusivity, flux, rim, edge_rows, inv_rows,
        solved, unit,
    )


def solution(mesh):
    return jax.shard_map(
        per_device,
        mesh=mesh,
        in_specs=(
            P(None, None, "lat", "lon"),
            P(None, None, "lat", "lon"),
            P("lat", "lon"),
            P("lat", "lon"),
            P("lat", "lon"),
            P(None, "lat", "lon"),
            P("lat", None, "lon"),
            P("lat", "lon", None, None),
            P(None, "lat", "lon"),
            P(None, "lat", "lon"),
            P(None, "lat", "lon"),
            P("lat", "lon"),
        ),
        out_specs=(P(None, None, "lat", "lon"), P("lat", "lon"), P(None, "lat", "lon")),
        check_vma=False,
    )
```

time: 60 us -> 54.8 us (0.913)
  local copies, waits for them, and re-layouts: 4.56 us -> 0.05 us
  Pallas kernels: 10.6 us -> 13.1 us
  starting transfers between devices: 39.1 us -> 37.1 us
  waiting for transfers between devices: 4.05 us -> 3.28 us
    unnamed x28 -> x16, local copies, waits for them, and re-layouts: 4.56 us -> 0.05 us
    pallas_call x1 -> x3, Pallas kernels: 4.47 us -> 7.23 us  [the longest x1 3.31 us: per_device(): pl.pallas_call(tracer_kernel, out_shape=(shape_of(2, depth, *block), shap...]
    ppermute x1, waiting for transfers between devices: 2.36 us -> 0.01 us  [per_device(): second = lax.ppermute(second, ('lat', 'lon'), pairs[1])]
    pallas_call x1, Pallas kernels: 4.62 us -> 2.45 us  [per_device(): pl.pallas_call(step_kernel, out_shape=(shape_of(2, depth, rows, cols), sh...]
    ppermute x1, waiting for transfers between devices: 0.01 us -> 2.11 us  [per_device(): first = lax.ppermute(first, ('lat', 'lon'), pairs[0])]
    ppermute x1, waiting for transfers between devices: 1.69 us -> 0.01 us  [per_device(): two = lax.ppermute(two, 'lon', pairs[1])]
    pallas_call x1, Pallas kernels: 0.53 us -> 1.69 us  [per_device(): pl.pallas_call(edge_kernel, out_shape=(shape_of(2 * rows, cols), shape_of...]
    ppermute x1, waiting for transfers between devices: 0.01 us -> 1.16 us  [per_device(): one = lax.ppermute(one, 'lon', pairs[0])]
  transfers between devices with their start and end apart: 5 -> 5, of which waited for: 2 -> 2; matrix products, arithmetic and copies ran while one was open for 0% -> 0% of each run, Pallas kernels for 1% -> 13%
where the time goes in v3:
time: 54.8 us; the launch traced here: 54.5 us
  starting transfers between devices  37.1 us (68%)
  Pallas kernels  13.1 us (24%)
  waiting for transfers between devices  3.28 us (6%)
  between operations  0.85 us (2%)
    all_to_all x1, starting transfers between devices, per_device(): lax.all_to_all(picked, 'lon', split_axis=0, concat_axis=0, tiled=True)  15.4 us
    ppermute x1, starting transfers between devices, per_device(): two = lax.ppermute(two, 'lon', pairs[1])  9.55 us
    ppermute x1, starting transfers between devices, per_device(): second = lax.ppermute(second, ('lat', 'lon'), pairs[1])  8.36 us
    pallas_call x1, Pallas kernels, per_device(): pl.pallas_call(tracer_kernel, out_shape=(shape_of(2, depth, *block), shap...  3.31 us
    pallas_call x1, Pallas kernels, per_device(): pl.pallas_call(step_kernel, out_shape=(shape_of(2, depth, rows, cols), sh...  2.45 us
    pallas_call x1, Pallas kernels, per_device(): pl.pallas_call(lookup_kernel, out_shape=(shape_of(4, *block), shape_of(FI...  2.15 us
    ppermute x1, waiting for transfers between devices, per_device(): first = lax.ppermute(first, ('lat', 'lon'), pairs[0])  2.11 us
    ppermute x1, starting transfers between devices, per_device(): one = lax.ppermute(one, 'lon', pairs[0])  1.92 us
  transfers between devices with their start and end apart: 5, of which 2 were waited for; matrix products, arithmetic and copies ran while one was open for 0% of the time, Pallas kernels for 13%

profile of v3, /device:TPU:120, one launch (start us, length us, event | category | flops | bytes accessed | tf_op | source)
XLA Modules:
  0.0 54.5 jit_solution(12976308287414972195)
XLA Ops:
  0.6 0.0 copy-start.5
  0.6 0.0 copy-start.6
  0.7 1.8 %pick.1.picked_ref = f32[32,1,640]{2,1,0:T(1,128)} custom-call(f32[1,4,512]{2,1,0:T(4,128)} %atm_hbm.1, s32[1,1,32,64]{3,2,1,0:T(8,128)} %rows_hbm.1), custom_call_target="tpu_custom_call" | custom-call | flops 40000000 | bytes 40000000 | tf_op jit(solution)/shard_map/pick/pallas_call | solution.py:513
  2.4 0.0 copy-start
  2.4 0.0 copy-start.1
  2.4 0.0 copy-start.2
  2.5 0.0 copy-start.4
  2.5 0.0 copy-start.7
  2.5 15.4 %all-to-all-start = ((f32[32,1,640]{2,1,0:T(1,128)}), f32[32,1,640]{2,1,0:T(1,128)S(1)}, u32[]{:S(2)}, u32[]{:S(2)}) async-start(f32[32,1,640]{2,1,0:T(1,128)} %pick.1.picked_ref), calls=%async_computation | async-start | bytes 163840 | tf_op jit(solution)/shard_map/all_to_all | solution.py:527
  17.9 0.0 copy-done.5
  17.9 0.0 copy-done.6
  17.9 0.0 copy-done
  17.9 0.0 copy-done.1
  17.9 0.0 copy-done.2
  17.9 0.0 copy-done.4
  17.9 0.0 copy-done.7
  17.9 0.0 copy-start.3
  18.0 1.7 %edges.1 = (f32[64,128]{1,0:T(8,128)S(1)}, f32[64,128]{1,0:T(8,128)S(1)}, f32[32,128]{1,0:T(8,128)S(1)}, f32[2,72,128]{2,1,0:T(8,128)S(1)}, s32[4,32,128]{2,1,0:...) custom-call(f32[32,1,640]{2,1,0:T(1,128)} %pick.1.picked_ref, ...), custom_call_target="tpu_custom_call" | custom-call | flops 2000000 | bytes 2000000 | tf_op jit(solution)/shard_map/edges/pallas_call | solution.py:531
  19.7 9.6 %collective-permute-start = (f32[64,128]{1,0:T(8,128)S(1)}, f32[64,128]{1,0:T(8,128)S(1)}, u32[]{:S(2)}, u32[]{:S(2)}) collective-permute-start(f32[64,128]{1,0:T(8,128)S(1)} %get-tuple-element.23), channel_id=1, source_target_pairs={{1,2},{2,1},{3,4},{4,3},{5,6},{6,5},{7,8},{8,7},{9,10},{10,9},{11,... | collective-permute-start | bytes 98312 | tf_op jit(solution)/shard_map/ppermute | solution.py:555
  29.2 1.9 %collective-permute-start.1 = (f32[64,128]{1,0:T(8,128)S(1)}, f32[64,128]{1,0:T(8,128)S(1)}, u32[]{:S(2)}, u32[]{:S(2)}) collective-permute-start(f32[64,128]{1,0:T(8,128)S(1)} %get-tuple-element.24), channel_id=1, source_target_pairs={{0,1},{1,0},{2,3},{3,2},{4,5},{5,4},{6,7},{7,6},{8,9},{9,8},{10,11... | collective-permute-start | bytes 98312 | tf_op jit(solution)/shard_map/ppermute | solution.py:556
  31.1 0.0 collective-permute-done.two_ref
  31.2 1.2 %collective-permute-done.1.one_ref = f32[64,128]{1,0:T(8,128)S(1)} collective-permute-done((f32[64,128]{1,0:T(8,128)S(1)}, f32[64,128]{1,0:T(8,128)S(1)}, u32[]{:S(2)}, u32[]{:S(2)}) %collective-permute-start.1) | collective-permute-done | bytes 32800 | tf_op jit(solution)/shard_map/ppermute | solution.py:556
  32.3 0.0 copy-done.3
  32.3 3.3 %tracers.1 = (f32[2,24,32,128]{3,2,1,0:T(8,128)S(1)}, f32[24,32,128]{2,1,0:T(8,128)S(1)}, f32[2,24,128]{2,1,0:T(8,128)S(1)}) custom-call(f32[64,128]{1,0:T(8,128)S(1)} %collective-permute-done.two_ref, f32[64,128]{1,0:T(8,128)S(1)} %collective-permute-done.1.one_ref, f32[32,128]{1,0:T(8,128)S(1)} %get-tuple-element.29.t_0_ref, s32[32,128]{1,0:T(8,128)S(1)} %copy-done.1, ...), custom_call_target="tpu_custom_call" | custom-call | flops 8000000 | bytes 8000000 | tf_op jit(solution)/shard_map/tracers/pallas_call | solution.py:558
  35.6 0.0 all-to-all-done.table_ref
  35.6 1.8 %rim_lookup.1 = (f32[136,128]{1,0:T(8,128)S(1)}, f32[136,128]{1,0:T(8,128)S(1)}, f32[2,3,8,128]{3,2,1,0:T(8,128)S(1)}, f32[2,3,8,128]{3,2,1,0:T(8,128)S(1)}, f32...) custom-call(f32[32,1,640]{2,1,0:T(1,128)S(1)} %all-to-all-done.table_ref, f32[64,128]{1,0:T(8,128)S(1)} %collective-permute-done.two_ref, ...), custom_call_target="tpu_custom_call" | custom-call | flops 8000000 | bytes 8000000 | tf_op jit(solution)/shard_map/rim_lookup/pallas_call | solution.py:569
  37.4 8.4 %collective-permute-start.2 = (f32[136,128]{1,0:T(8,128)S(1)}, f32[136,128]{1,0:T(8,128)S(1)}, u32[]{:S(2)}, u32[]{:S(2)}) collective-permute-start(f32[136,128]{1,0:T(8,128)S(1)} %get-tuple-element.33), channel_id=1, source_target_pairs={{32,64},{64,32},{96,128},{128,96},{160,192},{192,160},{224,256},{2... | collective-permute-start | bytes 208904 | tf_op jit(solution)/shard_map/ppermute | solution.py:590
  45.8 1.9 %collective-permute-start.3 = (f32[136,128]{1,0:T(8,128)S(1)}, f32[136,128]{1,0:T(8,128)S(1)}, u32[]{:S(2)}, u32[]{:S(2)}) collective-permute-start(f32[136,128]{1,0:T(8,128)S(1)} %get-tuple-element.34), channel_id=1, source_target_pairs={{0,32},{32,0},{64,96},{96,64},{128,160},{160,128},{192,224},{224,1... | collective-permute-start | bytes 208904 | tf_op jit(solution)/shard_map/ppermute | solution.py:591
  47.7 2.1 %lookup.1 = (f32[4,32,128]{2,1,0:T(8,128)S(1)}, f32[7,32,128]{2,1,0:T(8,128)S(1)}) custom-call(f32[2,3,8,128]{3,2,1,0:T(8,128)S(1)} %get-tuple-element.35.edge_flux_ref, f32[2,3,8,128]{3,2,1,0:T(8,128)S(1)} %get-tuple-element.36.edge_rim_ref, f32[4,16,128]{2,1,0:T(8,128)S(1)} %get-tuple-element.37.tab, f32[3,32,128]{2,1,0:T(8,128)S(1)} %get-tuple-element.38.side, ...), custom_call_target="tpu_custom_call" | custom-call | flops 8000000 | bytes 8000000 | tf_op jit(solution)/shard_map/lookup/pallas_call | solution.py:593
  49.9 0.0 collective-permute-done.2.second_ref
  49.9 2.1 %collective-permute-done.3.first_ref = f32[136,128]{1,0:T(8,128)S(1)} collective-permute-done((f32[136,128]{1,0:T(8,128)S(1)}, f32[136,128]{1,0:T(8,128)S(1)}, u32[]{:S(2)}, u32[]{:S(2)}) %collective-permute-start.3) | collective-permute-done | bytes 69664 | tf_op jit(solution)/shard_map/ppermute | solution.py:591
  52.0 2.5 %step.1 = (f32[2,24,32,128]{3,2,1,0:T(8,128)}, f32[32,128]{1,0:T(8,128)}, f32[2,32,128]{2,1,0:T(8,128)}) custom-call(f32[136,128]{1,0:T(8,128)S(1)} %collective-permute-done.2.second_ref, f32[136,128]{1,0:T(8,128)S(1)} %collective-permute-done.3.first_ref, f32[32,128]{1,0:T(8,128)S(1)} %copy-done.2, f32[2,32,128]{2,1,0:T(8,128)S(1)} %copy-done, ...), custom_call_target="tpu_custom_call" | custom-call | tf_op jit(solution)/shard_map/step/pallas_call | solution.py:603
Async XLA Ops:
  0.6 17.2 %copy-start.5 = (s32[4,32,128]{2,1,0:T(8,128)S(1)}, s32[4,32,128]{2,1,0:T(8,128)}, u32[]{:S(2)}) copy-start(s32[4,32,128]{2,1,0:T(8,128)} %slot_ref.1) | copy-start | bytes 196612
  0.6 17.2 %copy-start.6 = (f32[4,32,128]{2,1,0:T(8,128)S(1)}, f32[4,32,128]{2,1,0:T(8,128)}, u32[]{:S(2)}) copy-start(f32[4,32,128]{2,1,0:T(8,128)} %weight_ref.1) | copy-start | bytes 196612
  2.4 15.5 %copy-start = (f32[2,32,128]{2,1,0:T(8,128)S(1)}, f32[2,32,128]{2,1,0:T(8,128)}, u32[]{:S(2)}) copy-start(f32[2,32,128]{2,1,0:T(8,128)} %transport_ref.5) | copy-start | bytes 98308
  2.4 15.5 %copy-start.1 = (s32[32,128]{1,0:T(8,128)S(1)}, s32[32,128]{1,0:T(8,128)}, u32[]{:S(2)}) copy-start(s32[32,128]{1,0:T(8,128)} %level_ref.7) | copy-start | bytes 49156
  2.4 15.5 %copy-start.2 = (f32[32,128]{1,0:T(8,128)S(1)}, f32[32,128]{1,0:T(8,128)}, u32[]{:S(2)}) copy-start(f32[32,128]{1,0:T(8,128)} %height_ref.5) | copy-start | bytes 49156
  2.5 15.5 %copy-start.4 = (s32[4,32,128]{2,1,0:T(8,128)S(1)}, s32[4,32,128]{2,1,0:T(8,128)}, u32[]{:S(2)}) copy-start(s32[4,32,128]{2,1,0:T(8,128)} %owner_ref.1) | copy-start | bytes 196612
  2.5 15.5 %copy-start.7 = (s32[32,128]{1,0:T(8,128)S(1)}, s32[32,128]{1,0:T(8,128)}, u32[]{:S(2)}) copy-start(s32[32,128]{1,0:T(8,128)} %count_ref.1) | copy-start | bytes 49156
  2.5 33.2 %all-to-all-start = ((f32[32,1,640]{2,1,0:T(1,128)}), f32[32,1,640]{2,1,0:T(1,128)S(1)}, u32[]{:S(2)}, u32[]{:S(2)}) async-start(f32[32,1,640]{2,1,0:T(1,128)} %pick.1.picked_ref), calls=%async_computation | async-start | bytes 163840 | tf_op jit(solution)/shard_map/all_to_all | solution.py:527
  17.9 14.4 %copy-start.3 = (f32[32,128]{1,0:T(8,128)S(1)}, f32[32,128]{1,0:T(8,128)}, u32[]{:S(2)}) copy-start(f32[32,128]{1,0:T(8,128)} %diff_ref.3) | copy-start | bytes 49156
  19.7 11.5 %collective-permute-start = (f32[64,128]{1,0:T(8,128)S(1)}, f32[64,128]{1,0:T(8,128)S(1)}, u32[]{:S(2)}, u32[]{:S(2)}) collective-permute-start(f32[64,128]{1,0:T(8,128)S(1)} %get-tuple-element.23), channel_id=1, source_target_pairs={{1,2},{2,1},{3,4},{4,3},{5,6},{6,5},{7,8},{8,7},{9,10},{10,9},{11,... | collective-permute-start | bytes 98312 | tf_op jit(solution)/shard_map/ppermute | solution.py:555
  29.2 3.1 %collective-permute-start.1 = (f32[64,128]{1,0:T(8,128)S(1)}, f32[64,128]{1,0:T(8,128)S(1)}, u32[]{:S(2)}, u32[]{:S(2)}) collective-permute-start(f32[64,128]{1,0:T(8,128)S(1)} %get-tuple-element.24), channel_id=1, source_target_pairs={{0,1},{1,0},{2,3},{3,2},{4,5},{5,4},{6,7},{7,6},{8,9},{9,8},{10,11... | collective-permute-start | bytes 98312 | tf_op jit(solution)/shard_map/ppermute | solution.py:556
  37.4 12.5 %collective-permute-start.2 = (f32[136,128]{1,0:T(8,128)S(1)}, f32[136,128]{1,0:T(8,128)S(1)}, u32[]{:S(2)}, u32[]{:S(2)}) collective-permute-start(f32[136,128]{1,0:T(8,128)S(1)} %get-tuple-element.33), channel_id=1, source_target_pairs={{32,64},{64,32},{96,128},{128,96},{160,192},{192,160},{224,256},{2... | collective-permute-start | bytes 208904 | tf_op jit(solution)/shard_map/ppermute | solution.py:590
  45.8 6.2 %collective-permute-start.3 = (f32[136,128]{1,0:T(8,128)S(1)}, f32[136,128]{1,0:T(8,128)S(1)}, u32[]{:S(2)}, u32[]{:S(2)}) collective-permute-start(f32[136,128]{1,0:T(8,128)S(1)} %get-tuple-element.34), channel_id=1, source_target_pairs={{0,32},{32,0},{64,96},{96,64},{128,160},{160,128},{192,224},{224,1... | collective-permute-start | bytes 208904 | tf_op jit(solution)/shard_map/ppermute | solution.py:591

commit v4 on v3

--- a/solution.py
+++ b/solution.py
@@ -175,14 +175,20 @@
     return [rim_of(east, west, -g * HALO, 128 - (g + 1) * HALO) for g in range(4)]
 
 
-def side_lookup(side, east, west):
+def side_lookup(side, sides):
+    (east, west), (east_2, west_2) = sides
     lane = lanes(east.shape)
-    from_east = lane < 64
-    valid = (lane >= 32) & (lane < 96)
-    owner = jnp.where(valid, jnp.where(from_east, east, turn(west, 32, 1)), 0.0).astype(jnp.int32)
-    slot = jnp.where(valid, jnp.where(from_east, turn(east, -32, 1), west), 0.0).astype(jnp.int32)
-    used = jnp.where(valid, jnp.where(from_east, turn(east, -64, 1), turn(west, -32, 1)), 0.0)
-    slot = jnp.where(from_east, slot, slot + 64)
+    quarter = lane >> 5
+
+    def gathered(by):
+        parts = (turn(west_2, -32 - by, 1), turn(east, -by, 1), turn(west, 32 - by, 1), turn(east_2, 64 - by, 1))
+        low = jnp.where(quarter == 0, parts[0], parts[1])
+        return jnp.where(quarter < 2, low, jnp.where(quarter == 2, parts[2], parts[3]))
+
+    owner = gathered(0).astype(jnp.int32)
+    slot = gathered(32).astype(jnp.int32)
+    used = gathered(64)
+    slot = jnp.where((quarter & 1) == 0, slot + 64, slot)
     acc = [None] * 3
     for r in range(side.shape[1]):
         here = owner == r
@@ -190,12 +196,13 @@
             source = jnp.broadcast_to(side[f, r : r + 1, :], slot.shape)
             value = jnp.take_along_axis(source, slot, axis=1)
             acc[f] = value if r == 0 else jnp.where(here, value, acc[f])
-    rims = []
+    rims = ([], [])
     for f in range(3):
         v = acc[f] * used
         v = v + turn(v, -16, 1)
         v = v + turn(v, -8, 1)
-        rims.append(rim_of(v, v, -32, 56))
+        rims[0].append(rim_of(v, v, -32, 56))
+        rims[1].append(rim_of(v, v, -96, 120))
     return rims
 
 
@@ -215,15 +222,15 @@
     for f in range(3):
         side[f] = table_ref[:, 0, LISTS + f * 128 : LISTS + (f + 1) * 128]
     lane = lanes((HALO, cols))
-    for s, at in ((0, rows - HALO), (1, 0)):
-        cut = slice(at, at + HALO)
+    cuts = (slice(rows - HALO, rows), slice(0, HALO))
+    sides = [from_lon(one_ref, two_ref, cut) for cut in cuts]
+    side_rims = side_lookup(side, sides)
+    for s, cut in enumerate(cuts):
         found = own_lookup(tab, pick_row_ref, pick_lane_ref, used_ref, cut, (1, 2, 3))
-        east, west = from_lon(one_ref, two_ref, cut)
-        rims = side_lookup(side, east, west)
         for f in range(3):
             flux_ref[s, f] = found[f + 1]
-            rim_ref[s, f] = rims[f]
-        rims = state_rims(east, west) + rims
+            rim_ref[s, f] = side_rims[s][f]
+        rims = state_rims(*sides[s]) + side_rims[s]
         own = [
             height_ref[cut], transport_ref[0, cut], transport_ref[1, cut], level_ref[cut].astype(F32),
             found[1], found[2], found[3],
@@ -247,26 +254,34 @@
     flux_ref, rim_ref,
 ):
     rows = used_ref.shape[1]
-    for at in range(0, rows, HALO):
-        cut = slice(at, at + HALO)
-        inner = 0 < at < rows - HALO
-        found = own_lookup(tab, pick_row_ref, pick_lane_ref, used_ref, cut, (0, 1, 2, 3) if inner else (0,))
-        s = 1 if at == 0 else 0
-        flux_ref[0, cut] = found[0]
-        for f in range(1, 4):
-            flux_ref[f, cut] = found[f] if inner else edge_flux_ref[s, f - 1]
-        east, west = from_lon(one_ref, two_ref, cut)
-        rims = state_rims(east, west)
-        if inner:
-            rims += side_lookup(side, east, west)
-        else:
-            rims += [edge_rim_ref[s, f] for f in range(3)]
-        for i in range(FIELDS):
-            rim_ref[i, cut] = rims[i]
+    cuts = [slice(at, at + HALO) for at in range(0, rows, HALO)]
+    sides = [from_lon(one_ref, two_ref, cut) for cut in cuts]
+    for at in range(1, len(cuts) - 1, 2):
+        side_rims = side_lookup(side, sides[at : at + 2])
+        for i in range(2):
+            cut = cuts[at + i]
+            found = own_lookup(tab, pick_row_ref, pick_lane_ref, used_ref, cut, (0, 1, 2, 3))
+            for f in range(4):
+                flux_ref[f, cut] = found[f]
+            for g, rim in enumerate(state_rims(*sides[at + i]) + side_rims[i]):
+                rim_ref[g, cut] = rim
+    for s, at in ((0, len(cuts) - 1), (1, 0)):
+        cut = cuts[at]
+        flux_ref[0, cut] = own_lookup(tab, pick_row_ref, pick_lane_ref, used_ref, cut, (0,))[0]
+        for f in range(3):
+            flux_ref[f + 1, cut] = edge_flux_ref[s, f]
+        for g, rim in enumerate(state_rims(*sides[at]) + [edge_rim_ref[s, f] for f in range(3)]):
+            rim_ref[g, cut] = rim
+
+
+def split(x):
+    hi = x.astype(jnp.bfloat16)
+    return hi, (x - hi.astype(F32)).astype(jnp.bfloat16)
 
 
 def tracer_kernel(
     two_ref, one_ref, t_0_ref, level_ref, diff_ref, t_ref, v_ref, x_ref, unit_ref, inv_rows_ref, gain_ref,
+    parts, rims, net_x,
 ):
     depth, rows, cols = t_ref.shape[1:]
     shape = (rows, cols)
@@ -287,7 +302,30 @@
     layer = jnp.where(lane < depth, lane, lane - depth).astype(F32)
     level_w = west[:, first + HALO - 1 : first + HALO]
     face_w = jnp.broadcast_to(jnp.minimum(level_f[:, 0:1], level_w), shape)
-    west_flux = jnp.where(layer < face_w, u_w * ((t_w + t_0) * 0.5), 0.0)
+    west_flux = jnp.where((layer < face_w) & (lane < 2 * depth), u_w * ((t_w + t_0) * 0.5), 0.0)
+    both = []
+    for x in (turn(t_e, -1, 1), west_flux):
+        hi, lo = split(x)
+        both.append(jnp.where(lane < 64, hi.astype(F32), turn(lo.astype(F32), 64, 1)))
+    plane = lane & 63
+    for f in range(2 * depth):
+        at = slice(f * rows, (f + 1) * rows)
+        here = plane == f
+        parts[at, 0:128] = jnp.where(here, both[0], 0.0).astype(jnp.bfloat16)
+        parts[at, 128:256] = jnp.where(here, both[1], 0.0).astype(jnp.bfloat16)
+    k = lax.broadcasted_iota(jnp.int32, (2 * cols, cols), 0)
+    into = jnp.where(k < cols, last, 0) == lanes((2 * cols, cols))
+    rims[...] = jnp.dot(parts[...], into.astype(F32).astype(jnp.bfloat16), preferred_element_type=F32)
+    for l in range(depth):
+        mask_e = face_e > l
+        u_l = v_ref[0, l] * 0.5
+        for c in range(2):
+            f = c * depth + l
+            at = slice(f * rows, (f + 1) * rows)
+            t = t_ref[c, l]
+            t_east = jnp.where(lane == last, rims[at], turn(t, -1, 1))
+            flux_e = jnp.where(mask_e, u_l * (t + t_east), 0.0)
+            net_x[at] = flux_e - jnp.where(lane == 0, rims[at], turn(flux_e, 1, 1))
     diff = diff_ref[...]
     above = jnp.zeros(shape, F32)
     inv = None
@@ -301,18 +339,15 @@
         inv_rows_ref[0, l : l + 1] = inv[rows - 1 : rows]
         inv_rows_ref[1, l : l + 1] = inv[0:1]
         gain_ref[l] = below * inv
-        mask_e = face_e > l
         mask_n = face_n > l
-        u_l, v_l = v_ref[0, l] * 0.5, v_ref[1, l] * 0.5
+        v_l = v_ref[1, l] * 0.5
         for c in range(2):
             f = c * depth + l
+            at = slice(f * rows, (f + 1) * rows)
             t = t_ref[c, l]
-            t_east = jnp.where(lane == last, turn(t_e, last - 1 - f, 1), turn(t, -1, 1))
-            flux_e = jnp.where(mask_e, u_l * (t + t_east), 0.0)
-            flux_w = jnp.where(lane == 0, turn(west_flux, -f, 1), turn(flux_e, 1, 1))
             flux_n = jnp.where(mask_n, v_l * (t + turn(t, -1, 0)), 0.0)
             flux_s = turn(flux_n, 1, 0)
-            forced = t - adv_rate * ((flux_e - flux_w) + (flux_n - flux_s))
+            forced = t - adv_rate * (net_x[at] + (flux_n - flux_s))
             right[c] = forced * inv if l == 0 else (forced + above * right[c]) * inv
             x_ref[c, l] = right[c]
         right[2] = inv if l == 0 else above * right[2] * inv
@@ -329,13 +364,27 @@
 
 def step_kernel(
     second_ref, first_ref, height_ref, transport_ref, level_ref, diff_ref, flux_ref, rim_ref, rows_ref, inv_rows_ref,
-    x_ref, unit_ref, t_out, height_out, transport_out, north_ref, shift, fixed, sems,
+    x_ref, unit_ref, t_out, height_out, transport_out, north_ref, shift, fixed, result, sems,
 ):
     top = is_top()
     level = level_ref[...]
     level_f = level.astype(F32)
     rows, cols = level.shape
     depth = x_ref.shape[1]
+    wet_0 = (level > 0).astype(F32)
+    source = (heat_gain * flux_ref[0] * wet_0, -salt_gain * flux_ref[1] * wet_0)
+    lo, hi = slice(0, HALO), slice(rows - HALO, rows)
+    mid = slice(HALO, rows - HALO)
+    copies = []
+
+    def send(value, out):
+        copies.append(pltpu.make_async_copy(value, out, sems.at[len(copies)]))
+        copies[-1].start()
+
+    for c in range(2):
+        for l in range(depth):
+            fixed[c, l, mid] = x_ref[c, l, mid] + unit_ref[l, mid] * source[c][mid]
+        send(fixed.at[c, :, mid], t_out.at[c, :, mid])
     even = is_even("lat")
     a, b = first_ref[...], second_ref[...]
     south = jnp.where(even, b, a)
@@ -377,23 +426,15 @@
             below = jnp.where(level_in > l + 1, diff_in, 0.0) * inv
             right[i] = shift[s, at : at + 1] + below * right[i]
             shift[s, at : at + 1] = right[i]
-    wet_0 = (level > 0).astype(F32)
-    source = (heat_gain * flux_ref[0] * wet_0, -salt_gain * flux_ref[1] * wet_0)
     row = rows_of((HALO, cols))
-    lo, hi = slice(0, HALO), slice(rows - HALO, rows)
-    mid = slice(HALO, rows - HALO)
-    copies = []
-    for c in range(2):
-        for l in range(depth):
-            at = c * depth + l
-            x = x_ref[c, l] + unit_ref[l] * source[c]
-            add_s = jnp.broadcast_to(shift[1, at : at + 1], (HALO, cols))
-            add_n = jnp.broadcast_to(shift[0, at : at + 1], (HALO, cols))
-            fixed[c, l, lo] = x[lo] + jnp.where(row == 0, add_s, 0.0)
-            fixed[c, l, mid] = x[mid]
-            fixed[c, l, hi] = x[hi] + jnp.where(row == HALO - 1, add_n, 0.0)
-        copies.append(pltpu.make_async_copy(fixed.at[c], t_out.at[c], sems.at[c]))
-        copies[c].start()
+    for s, cut, at_row in ((0, hi, HALO - 1), (1, lo, 0)):
+        for c in range(2):
+            for l in range(depth):
+                at = c * depth + l
+                add = jnp.broadcast_to(shift[s, at : at + 1], (HALO, cols))
+                x = x_ref[c, l, cut] + unit_ref[l, cut] * source[c][cut]
+                fixed[c, l, cut] = x + jnp.where(row == at_row, add, 0.0)
+        send(fixed.at[:, :, cut], t_out.at[:, :, cut])
 
     own = (
         height_ref[...], transport_ref[0], transport_ref[1], level_f,
@@ -442,9 +483,11 @@
         p_e = (p_e - p_grad * (turn(p_h, 1, 1) - p_h)) * p_wet + p_wind_e
         p_n = (p_n - p_grad * (p_h_n - p_h)) * p_wet + p_wind_n
     inside = slice(HALO, HALO + rows)
-    height_out[...] = h[inside, :cols]
-    transport_out[0] = e[inside, :cols]
-    transport_out[1] = n[inside, :cols]
+    result[0] = h[inside, :cols]
+    result[1] = e[inside, :cols]
+    result[2] = n[inside, :cols]
+    send(result.at[0], height_out)
+    send(result.at[1:3], transport_out)
 
     for copy in copies:
         copy.wait()
@@ -560,7 +603,12 @@
         out_shape=(shape_of(2, depth, *block), shape_of(depth, *block), shape_of(2, depth, cols)),
         in_specs=vmem(7),
         out_specs=vmem(3),
-        scratch_shapes=[pltpu.VMEM((depth, *block), F32)],
+        scratch_shapes=[
+            pltpu.VMEM((depth, *block), F32),
+            pltpu.VMEM((2 * depth * rows, 2 * cols), jnp.bfloat16),
+            pltpu.VMEM((2 * depth * rows, cols), F32),
+            pltpu.VMEM((2 * depth * rows, cols), F32),
+        ],
         compiler_params=params(),
         cost_estimate=work(8),
         name="tracers",
@@ -604,12 +652,13 @@
         step_kernel,
         out_shape=(shape_of(2, depth, rows, cols), shape_of(rows, cols), shape_of(2, rows, cols)),
         in_specs=vmem(12),
-        out_specs=(pl.BlockSpec(memory_space=pl.ANY), *vmem(2)),
+        out_specs=(pl.BlockSpec(memory_space=pl.ANY),) * 3,
         scratch_shapes=[
             pltpu.VMEM((lat_rows, cols), F32),
             pltpu.VMEM((2, 2 * depth, cols), F32),
             pltpu.VMEM((2, depth, rows, cols), F32),
-            pltpu.SemaphoreType.DMA((2,)),
+            pltpu.VMEM((3, rows, cols), F32),
+            pltpu.SemaphoreType.DMA((6,)),
         ],
         compiler_params=params(),
         name="step",

time: 54.8 us -> 51.3 us (0.936)
  Pallas kernels: 13.1 us -> 8.51 us
  waiting for transfers between devices: 3.28 us -> 4.37 us
    pallas_call x1, Pallas kernels: 3.31 us -> 1.32 us  [per_device(): pl.pallas_call(tracer_kernel, out_shape=(shape_of(2, depth, *block), shap...]
    pallas_call x1, Pallas kernels: 2.15 us -> 1.06 us  [per_device(): pl.pallas_call(lookup_kernel, out_shape=(shape_of(4, *block), shape_of(FI...]
    pallas_call x1, Pallas kernels: 1.78 us -> 0.86 us  [per_device(): pl.pallas_call(rim_lookup_kernel, out_shape=(shape_of(lat_rows, cols), sh...]
    ppermute x1, waiting for transfers between devices: 0.01 us -> 0.68 us  [per_device(): second = lax.ppermute(second, ('lat', 'lon'), pairs[1])]
    pallas_call x1, Pallas kernels: 2.45 us -> 1.81 us  [per_device(): pl.pallas_call(step_kernel, out_shape=(shape_of(2, depth, rows, cols), sh...]
  transfers between devices with their start and end apart: 5 -> 5, of which waited for: 2 -> 3; matrix products, arithmetic and copies ran while one was open for 0% -> 0% of each run, Pallas kernels for 13% -> 8%
where the time goes in v4:
time: 51.3 us; the launch traced here: 50.9 us
  starting transfers between devices  37.1 us (72%)
  Pallas kernels  8.51 us (17%)
  waiting for transfers between devices  4.37 us (9%)
  between operations  0.84 us (2%)
    all_to_all x1, starting transfers between devices, per_device(): lax.all_to_all(picked, 'lon', split_axis=0, concat_axis=0, tiled=True)  15.4 us
    ppermute x1, starting transfers between devices, per_device(): two = lax.ppermute(two, 'lon', pairs[1])  9.55 us
    ppermute x1, starting transfers between devices, per_device(): second = lax.ppermute(second, ('lat', 'lon'), pairs[1])  8.37 us
    ppermute x1, waiting for transfers between devices, per_device(): first = lax.ppermute(first, ('lat', 'lon'), pairs[0])  2.53 us
    ppermute x1, starting transfers between devices, per_device(): one = lax.ppermute(one, 'lon', pairs[0])  1.92 us
    ppermute x1, starting transfers between devices, per_device(): first = lax.ppermute(first, ('lat', 'lon'), pairs[0])  1.92 us
    pallas_call x1, Pallas kernels, per_device(): pl.pallas_call(step_kernel, out_shape=(shape_of(2, depth, rows, cols), sh...  1.81 us
    pallas_call x1, Pallas kernels, per_device(): pl.pallas_call(pick_kernel, out_shape=shape_of(n_lon, 1, 10 * slots), in_...  1.75 us
  transfers between devices with their start and end apart: 5, of which 3 were waited for; matrix products, arithmetic and copies ran while one was open for 0% of the time, Pallas kernels for 8%

profile of v4, /device:TPU:120, one launch (start us, length us, event | category | flops | bytes accessed | tf_op | source)
XLA Modules:
  0.0 50.9 jit_solution(6228641066038480818)
XLA Ops:
  0.6 0.0 copy-start.5
  0.6 0.0 copy-start.6
  0.7 1.8 %pick.1.picked_ref = f32[32,1,640]{2,1,0:T(1,128)} custom-call(f32[1,4,512]{2,1,0:T(4,128)} %atm_hbm.1, s32[1,1,32,64]{3,2,1,0:T(8,128)} %rows_hbm.1), custom_call_target="tpu_custom_call" | custom-call | flops 40000000 | bytes 40000000 | tf_op jit(solution)/shard_map/pick/pallas_call | solution.py:556
  2.4 0.0 copy-start
  2.4 0.0 copy-start.1
  2.4 0.0 copy-start.2
  2.5 0.0 copy-start.4
  2.5 0.0 copy-start.7
  2.5 15.4 %all-to-all-start = ((f32[32,1,640]{2,1,0:T(1,128)}), f32[32,1,640]{2,1,0:T(1,128)S(1)}, u32[]{:S(2)}, u32[]{:S(2)}) async-start(f32[32,1,640]{2,1,0:T(1,128)} %pick.1.picked_ref), calls=%async_computation | async-start | bytes 163840 | tf_op jit(solution)/shard_map/all_to_all | solution.py:570
  17.9 0.0 copy-done.5
  17.9 0.0 copy-done.6
  17.9 0.0 copy-done
  17.9 0.0 copy-done.1
  17.9 0.0 copy-done.2
  17.9 0.0 copy-done.4
  17.9 0.0 copy-done.7
  17.9 0.0 copy-start.3
  18.0 1.7 %edges.1 = (f32[64,128]{1,0:T(8,128)S(1)}, f32[64,128]{1,0:T(8,128)S(1)}, f32[32,128]{1,0:T(8,128)S(1)}, f32[2,72,128]{2,1,0:T(8,128)S(1)}, s32[4,32,128]{2,1,0:...) custom-call(f32[32,1,640]{2,1,0:T(1,128)} %pick.1.picked_ref, ...), custom_call_target="tpu_custom_call" | custom-call | flops 2000000 | bytes 2000000 | tf_op jit(solution)/shard_map/edges/pallas_call | solution.py:574
  19.7 9.6 %collective-permute-start = (f32[64,128]{1,0:T(8,128)S(1)}, f32[64,128]{1,0:T(8,128)S(1)}, u32[]{:S(2)}, u32[]{:S(2)}) collective-permute-start(f32[64,128]{1,0:T(8,128)S(1)} %get-tuple-element.23), channel_id=1, source_target_pairs={{1,2},{2,1},{3,4},{4,3},{5,6},{6,5},{7,8},{8,7},{9,10},{10,9},{11,... | collective-permute-start | bytes 98312 | tf_op jit(solution)/shard_map/ppermute | solution.py:598
  29.2 1.9 %collective-permute-start.1 = (f32[64,128]{1,0:T(8,128)S(1)}, f32[64,128]{1,0:T(8,128)S(1)}, u32[]{:S(2)}, u32[]{:S(2)}) collective-permute-start(f32[64,128]{1,0:T(8,128)S(1)} %get-tuple-element.24), channel_id=1, source_target_pairs={{0,1},{1,0},{2,3},{3,2},{4,5},{5,4},{6,7},{7,6},{8,9},{9,8},{10,11... | collective-permute-start | bytes 98312 | tf_op jit(solution)/shard_map/ppermute | solution.py:599
  31.1 0.0 collective-permute-done.two_ref
  31.2 1.2 %collective-permute-done.1.one_ref = f32[64,128]{1,0:T(8,128)S(1)} collective-permute-done((f32[64,128]{1,0:T(8,128)S(1)}, f32[64,128]{1,0:T(8,128)S(1)}, u32[]{:S(2)}, u32[]{:S(2)}) %collective-permute-start.1) | collective-permute-done | bytes 32800 | tf_op jit(solution)/shard_map/ppermute | solution.py:599
  32.3 0.0 copy-done.3
  32.3 1.3 %tracers.1 = (f32[2,24,32,128]{3,2,1,0:T(8,128)S(1)}, f32[24,32,128]{2,1,0:T(8,128)S(1)}, f32[2,24,128]{2,1,0:T(8,128)S(1)}) custom-call(f32[64,128]{1,0:T(8,128)S(1)} %collective-permute-done.two_ref, f32[64,128]{1,0:T(8,128)S(1)} %collective-permute-done.1.one_ref, f32[32,128]{1,0:T(8,128)S(1)} %get-tuple-element.29.t_0_ref, s32[32,128]{1,0:T(8,128)S(1)} %copy-done.1, ...), custom_call_target="tpu_custom_call" | custom-call | flops 8000000 | bytes 8000000 | tf_op jit(solution)/shard_map/tracers/pallas_call | solution.py:601
  33.6 0.0 all-to-all-done.table_ref
  33.7 0.9 %rim_lookup.1 = (f32[136,128]{1,0:T(8,128)S(1)}, f32[136,128]{1,0:T(8,128)S(1)}, f32[2,3,8,128]{3,2,1,0:T(8,128)S(1)}, f32[2,3,8,128]{3,2,1,0:T(8,128)S(1)}, f32...) custom-call(f32[32,1,640]{2,1,0:T(1,128)S(1)} %all-to-all-done.table_ref, f32[64,128]{1,0:T(8,128)S(1)} %collective-permute-done.two_ref, ...), custom_call_target="tpu_custom_call" | custom-call | flops 8000000 | bytes 8000000 | tf_op jit(solution)/shard_map/rim_lookup/pallas_call | solution.py:617
  34.5 8.4 %collective-permute-start.2 = (f32[136,128]{1,0:T(8,128)S(1)}, f32[136,128]{1,0:T(8,128)S(1)}, u32[]{:S(2)}, u32[]{:S(2)}) collective-permute-start(f32[136,128]{1,0:T(8,128)S(1)} %get-tuple-element.33), channel_id=1, source_target_pairs={{32,64},{64,32},{96,128},{128,96},{160,192},{192,160},{224,256},{2... | collective-permute-start | bytes 208904 | tf_op jit(solution)/shard_map/ppermute | solution.py:638
  42.9 1.9 %collective-permute-start.3 = (f32[136,128]{1,0:T(8,128)S(1)}, f32[136,128]{1,0:T(8,128)S(1)}, u32[]{:S(2)}, u32[]{:S(2)}) collective-permute-start(f32[136,128]{1,0:T(8,128)S(1)} %get-tuple-element.34), channel_id=1, source_target_pairs={{0,32},{32,0},{64,96},{96,64},{128,160},{160,128},{192,224},{224,1... | collective-permute-start | bytes 208904 | tf_op jit(solution)/shard_map/ppermute | solution.py:639
  44.8 1.1 %lookup.1 = (f32[4,32,128]{2,1,0:T(8,128)S(1)}, f32[7,32,128]{2,1,0:T(8,128)S(1)}) custom-call(f32[2,3,8,128]{3,2,1,0:T(8,128)S(1)} %get-tuple-element.35.edge_flux_ref, f32[2,3,8,128]{3,2,1,0:T(8,128)S(1)} %get-tuple-element.36.edge_rim_ref, f32[4,16,128]{2,1,0:T(8,128)S(1)} %get-tuple-element.37.tab, f32[3,32,128]{2,1,0:T(8,128)S(1)} %get-tuple-element.38.side, ...), custom_call_target="tpu_custom_call" | custom-call | flops 8000000 | bytes 8000000 | tf_op jit(solution)/shard_map/lookup/pallas_call | solution.py:641
  45.9 0.7 %collective-permute-done.2.second_ref = f32[136,128]{1,0:T(8,128)S(1)} collective-permute-done((f32[136,128]{1,0:T(8,128)S(1)}, f32[136,128]{1,0:T(8,128)S(1)}, u32[]{:S(2)}, u32[]{:S(2)}) %collective-permute-start.2) | collective-permute-done | bytes 69664 | tf_op jit(solution)/shard_map/ppermute | solution.py:638
  46.6 2.5 %collective-permute-done.3.first_ref = f32[136,128]{1,0:T(8,128)S(1)} collective-permute-done((f32[136,128]{1,0:T(8,128)S(1)}, f32[136,128]{1,0:T(8,128)S(1)}, u32[]{:S(2)}, u32[]{:S(2)}) %collective-permute-start.3) | collective-permute-done | bytes 69664 | tf_op jit(solution)/shard_map/ppermute | solution.py:639
  49.1 1.8 %step.1 = (f32[2,24,32,128]{3,2,1,0:T(8,128)}, f32[32,128]{1,0:T(8,128)}, f32[2,32,128]{2,1,0:T(8,128)}) custom-call(f32[136,128]{1,0:T(8,128)S(1)} %collective-permute-done.2.second_ref, f32[136,128]{1,0:T(8,128)S(1)} %collective-permute-done.3.first_ref, f32[32,128]{1,0:T(8,128)S(1)} %copy-done.2, f32[2,32,128]{2,1,0:T(8,128)S(1)} %copy-done, ...), custom_call_target="tpu_custom_call" | custom-call | tf_op jit(solution)/shard_map/step/pallas_call | solution.py:651
Async XLA Ops:
  0.6 17.2 %copy-start.5 = (s32[4,32,128]{2,1,0:T(8,128)S(1)}, s32[4,32,128]{2,1,0:T(8,128)}, u32[]{:S(2)}) copy-start(s32[4,32,128]{2,1,0:T(8,128)} %slot_ref.1) | copy-start | bytes 196612
  0.6 17.2 %copy-start.6 = (f32[4,32,128]{2,1,0:T(8,128)S(1)}, f32[4,32,128]{2,1,0:T(8,128)}, u32[]{:S(2)}) copy-start(f32[4,32,128]{2,1,0:T(8,128)} %weight_ref.1) | copy-start | bytes 196612
  2.4 15.5 %copy-start = (f32[2,32,128]{2,1,0:T(8,128)S(1)}, f32[2,32,128]{2,1,0:T(8,128)}, u32[]{:S(2)}) copy-start(f32[2,32,128]{2,1,0:T(8,128)} %transport_ref.5) | copy-start | bytes 98308
  2.4 15.5 %copy-start.1 = (s32[32,128]{1,0:T(8,128)S(1)}, s32[32,128]{1,0:T(8,128)}, u32[]{:S(2)}) copy-start(s32[32,128]{1,0:T(8,128)} %level_ref.7) | copy-start | bytes 49156
  2.4 15.5 %copy-start.2 = (f32[32,128]{1,0:T(8,128)S(1)}, f32[32,128]{1,0:T(8,128)}, u32[]{:S(2)}) copy-start(f32[32,128]{1,0:T(8,128)} %height_ref.5) | copy-start | bytes 49156
  2.5 15.5 %copy-start.4 = (s32[4,32,128]{2,1,0:T(8,128)S(1)}, s32[4,32,128]{2,1,0:T(8,128)}, u32[]{:S(2)}) copy-start(s32[4,32,128]{2,1,0:T(8,128)} %owner_ref.1) | copy-start | bytes 196612
  2.5 15.5 %copy-start.7 = (s32[32,128]{1,0:T(8,128)S(1)}, s32[32,128]{1,0:T(8,128)}, u32[]{:S(2)}) copy-start(s32[32,128]{1,0:T(8,128)} %count_ref.1) | copy-start | bytes 49156
  2.5 31.2 %all-to-all-start = ((f32[32,1,640]{2,1,0:T(1,128)}), f32[32,1,640]{2,1,0:T(1,128)S(1)}, u32[]{:S(2)}, u32[]{:S(2)}) async-start(f32[32,1,640]{2,1,0:T(1,128)} %pick.1.picked_ref), calls=%async_computation | async-start | bytes 163840 | tf_op jit(solution)/shard_map/all_to_all | solution.py:570
  17.9 14.4 %copy-start.3 = (f32[32,128]{1,0:T(8,128)S(1)}, f32[32,128]{1,0:T(8,128)}, u32[]{:S(2)}) copy-start(f32[32,128]{1,0:T(8,128)} %diff_ref.3) | copy-start | bytes 49156
  19.7 11.5 %collective-permute-start = (f32[64,128]{1,0:T(8,128)S(1)}, f32[64,128]{1,0:T(8,128)S(1)}, u32[]{:S(2)}, u32[]{:S(2)}) collective-permute-start(f32[64,128]{1,0:T(8,128)S(1)} %get-tuple-element.23), channel_id=1, source_target_pairs={{1,2},{2,1},{3,4},{4,3},{5,6},{6,5},{7,8},{8,7},{9,10},{10,9},{11,... | collective-permute-start | bytes 98312 | tf_op jit(solution)/shard_map/ppermute | solution.py:598
  29.2 3.1 %collective-permute-start.1 = (f32[64,128]{1,0:T(8,128)S(1)}, f32[64,128]{1,0:T(8,128)S(1)}, u32[]{:S(2)}, u32[]{:S(2)}) collective-permute-start(f32[64,128]{1,0:T(8,128)S(1)} %get-tuple-element.24), channel_id=1, source_target_pairs={{0,1},{1,0},{2,3},{3,2},{4,5},{5,4},{6,7},{7,6},{8,9},{9,8},{10,11... | collective-permute-start | bytes 98312 | tf_op jit(solution)/shard_map/ppermute | solution.py:599
  34.5 12.1 %collective-permute-start.2 = (f32[136,128]{1,0:T(8,128)S(1)}, f32[136,128]{1,0:T(8,128)S(1)}, u32[]{:S(2)}, u32[]{:S(2)}) collective-permute-start(f32[136,128]{1,0:T(8,128)S(1)} %get-tuple-element.33), channel_id=1, source_target_pairs={{32,64},{64,32},{96,128},{128,96},{160,192},{192,160},{224,256},{2... | collective-permute-start | bytes 208904 | tf_op jit(solution)/shard_map/ppermute | solution.py:638
  42.9 6.2 %collective-permute-start.3 = (f32[136,128]{1,0:T(8,128)S(1)}, f32[136,128]{1,0:T(8,128)S(1)}, u32[]{:S(2)}, u32[]{:S(2)}) collective-permute-start(f32[136,128]{1,0:T(8,128)S(1)} %get-tuple-element.34), channel_id=1, source_target_pairs={{0,32},{32,0},{64,96},{96,64},{128,160},{160,128},{192,224},{224,1... | collective-permute-start | bytes 208904 | tf_op jit(solution)/shard_map/ppermute | solution.py:639

commit v5 on v4

--- a/solution.py
+++ b/solution.py
@@ -78,19 +78,18 @@
 
 def edge_kernel(
     picked_ref, t_hbm, v_hbm, level_ref, height_ref, transport_ref, owner_ref, slot_ref, weight_ref, count_ref,
-    two_ref, one_ref, t_0_ref, rows_ref, pick_row_ref, pick_lane_ref, used_ref, t_ref, v_ref, sems,
+    two_ref, one_ref, t_0_ref, rows_ref, pick_row_ref, pick_lane_ref, used_ref, t_ref, u_ref, v_rows, sems,
 ):
+    depth, rows, cols = t_ref.shape[1:]
     copies = [
         pltpu.make_async_copy(t_hbm.at[0], t_ref.at[0], sems.at[0]),
-        pltpu.make_async_copy(v_hbm.at[0], v_ref.at[0], sems.at[1]),
+        pltpu.make_async_copy(v_hbm.at[0], u_ref, sems.at[1]),
         pltpu.make_async_copy(t_hbm.at[1], t_ref.at[1], sems.at[2]),
-        pltpu.make_async_copy(v_hbm.at[1], v_ref.at[1], sems.at[3]),
+        pltpu.make_async_copy(v_hbm.at[1, :, rows - HALO : rows], v_rows, sems.at[3]),
     ]
     for copy in copies:
         copy.start()
-    depth = t_ref.shape[1]
-    shape = t_ref.shape[2:]
-    rows, cols = shape
+    shape = (rows, cols)
     lane = lanes(shape)
     level = level_ref[...]
     half = lax.axis_size("lon") // 2
@@ -123,7 +122,7 @@
     copies[1].wait()
     for l in range(depth):
         at = 2 * depth + l
-        east_t = jnp.where(lane == at, turn(v_ref[0, l], at + 1, 1), east_t)
+        east_t = jnp.where(lane == at, turn(u_ref[l], at + 1, 1), east_t)
     even = is_even("lon")
     one_ref[:rows] = jnp.where(even, east, west)
     two_ref[:rows] = jnp.where(even, west, east)
@@ -138,7 +137,7 @@
     copies[3].wait()
     for l in range(depth):
         at = 2 * depth + l
-        rows_ref[0, at : at + 1] = v_ref[1, l, rows - 1 : rows]
+        rows_ref[0, at : at + 1] = v_rows[l, HALO - 1 : HALO]
     rows_ref[1, 2 * depth :] = jnp.zeros((depth, cols), F32)
 
 def own_lookup(tab, row_ref, lane_ref, used_ref, cut, fields):
@@ -208,7 +207,7 @@
 
 def rim_lookup_kernel(
     table_ref, two_ref, one_ref, pick_row_ref, pick_lane_ref, used_ref, rows_ref, level_ref, height_ref,
-    transport_ref, after_ref, second_ref, first_ref, flux_ref, rim_ref, tab, side, pack,
+    transport_ref, first_ref, second_ref, flux_ref, rim_ref, tab, side, pack,
 ):
     n_lon = table_ref.shape[0]
     half = n_lon // 2
@@ -245,8 +244,8 @@
         pack[s, ROW_T:] = rows_ref[s]
     even = is_even("lat")
     north_going, south_going = pack[0], pack[1]
+    first_ref[...] = jnp.where(even, north_going, south_going)
     second_ref[...] = jnp.where(even, south_going, north_going)
-    first_ref[...] = jnp.where(even, north_going, south_going)
 
 
 def lookup_kernel(
@@ -280,10 +279,12 @@
 
 
 def tracer_kernel(
-    two_ref, one_ref, t_0_ref, level_ref, diff_ref, t_ref, v_ref, x_ref, unit_ref, inv_rows_ref, gain_ref,
-    parts, rims, net_x,
+    two_ref, one_ref, t_0_ref, level_ref, diff_ref, t_ref, u_ref, v_hbm, x_ref, unit_ref, inv_rows_ref, gain_ref,
+    parts, rims, net_x, v_ref, sem,
 ):
     depth, rows, cols = t_ref.shape[1:]
+    copy = pltpu.make_async_copy(v_hbm.at[1], v_ref, sem)
+    copy.start()
     shape = (rows, cols)
     east, west = from_lon(one_ref, two_ref, slice(0, rows))
     t_e, t_w = from_lon(one_ref, two_ref, slice(rows, 2 * rows))
@@ -318,7 +319,7 @@
     rims[...] = jnp.dot(parts[...], into.astype(F32).astype(jnp.bfloat16), preferred_element_type=F32)
     for l in range(depth):
         mask_e = face_e > l
-        u_l = v_ref[0, l] * 0.5
+        u_l = u_ref[l] * 0.5
         for c in range(2):
             f = c * depth + l
             at = slice(f * rows, (f + 1) * rows)
@@ -326,6 +327,7 @@
             t_east = jnp.where(lane == last, rims[at], turn(t, -1, 1))
             flux_e = jnp.where(mask_e, u_l * (t + t_east), 0.0)
             net_x[at] = flux_e - jnp.where(lane == 0, rims[at], turn(flux_e, 1, 1))
+    copy.wait()
     diff = diff_ref[...]
     above = jnp.zeros(shape, F32)
     inv = None
@@ -340,7 +342,7 @@
         inv_rows_ref[1, l : l + 1] = inv[0:1]
         gain_ref[l] = below * inv
         mask_n = face_n > l
-        v_l = v_ref[1, l] * 0.5
+        v_l = v_ref[l] * 0.5
         for c in range(2):
             f = c * depth + l
             at = slice(f * rows, (f + 1) * rows)
@@ -363,7 +365,7 @@
 
 
 def step_kernel(
-    second_ref, first_ref, height_ref, transport_ref, level_ref, diff_ref, flux_ref, rim_ref, rows_ref, inv_rows_ref,
+    first_ref, second_ref, height_ref, transport_ref, level_ref, diff_ref, flux_ref, rim_ref, rows_ref, inv_rows_ref,
     x_ref, unit_ref, t_out, height_out, transport_out, north_ref, shift, fixed, result, sems,
 ):
     top = is_top()
@@ -555,7 +557,7 @@
     slots = send_rows.shape[3]
     picked = pl.pallas_call(
         pick_kernel,
-        out_shape=shape_of(n_lon, 1, 10 * slots),
+        out_shape=pltpu.VMEM((n_lon, 1, 10 * slots), F32),
         in_specs=[pl.BlockSpec(memory_space=pltpu.HBM)] * 2,
         out_specs=vmem(1)[0],
         scratch_shapes=[
@@ -571,7 +573,7 @@
 
     block = (rows, cols)
     lat_rows = ROW_T + 3 * depth
-    two, one, t_0, edge_rows, pick_row, pick_lane, used, tracers, velocity = pl.pallas_call(
+    two, one, t_0, edge_rows, pick_row, pick_lane, used, tracers, speed_e = pl.pallas_call(
         edge_kernel,
         out_shape=(
             shape_of(2 * rows, cols),
@@ -582,11 +584,11 @@
             jax.ShapeDtypeStruct((4, *block), jnp.int32),
             shape_of(4, *block),
             shape_of(2, depth, *block),
-            shape_of(2, depth, *block),
+            shape_of(depth, *block),
         ),
         in_specs=[pl.BlockSpec(memory_space=pl.ANY)] + [pl.BlockSpec(memory_space=pltpu.HBM)] * 2 + vmem(7),
         out_specs=vmem(9),
-        scratch_shapes=[pltpu.SemaphoreType.DMA((4,))],
+        scratch_shapes=[pltpu.VMEM((depth, HALO, cols), F32), pltpu.SemaphoreType.DMA((4,))],
         compiler_params=params(),
         cost_estimate=work(2),
         name="edges",
@@ -601,20 +603,22 @@
     solved, unit, inv_rows = pl.pallas_call(
         tracer_kernel,
         out_shape=(shape_of(2, depth, *block), shape_of(depth, *block), shape_of(2, depth, cols)),
-        in_specs=vmem(7),
+        in_specs=vmem(7) + [pl.BlockSpec(memory_space=pltpu.HBM)],
         out_specs=vmem(3),
         scratch_shapes=[
             pltpu.VMEM((depth, *block), F32),
             pltpu.VMEM((2 * depth * rows, 2 * cols), jnp.bfloat16),
             pltpu.VMEM((2 * depth * rows, cols), F32),
             pltpu.VMEM((2 * depth * rows, cols), F32),
+            pltpu.VMEM((depth, *block), F32),
+            pltpu.SemaphoreType.DMA,
         ],
         compiler_params=params(),
         cost_estimate=work(8),
         name="tracers",
-    )(two, one, t_0, ocean_levels, diffusivity, tracers, velocity)
-
-    second, first, edge_flux, edge_rim, tab, side = pl.pallas_call(
+    )(two, one, t_0, ocean_levels, diffusivity, tracers, speed_e, in_hbm(velocity))
+
+    first, second, edge_flux, edge_rim, tab, side = pl.pallas_call(
         rim_lookup_kernel,
         out_shape=(
             shape_of(lat_rows, cols),
@@ -624,7 +628,7 @@
             shape_of(4, n_lon // 2, 128),
             shape_of(3, n_lon, 128),
         ),
-        in_specs=vmem(10) + [pl.BlockSpec(memory_space=pl.ANY)],
+        in_specs=vmem(10),
         out_specs=vmem(6),
         scratch_shapes=[pltpu.VMEM((2, lat_rows, cols), F32)],
         compiler_params=params(),
@@ -632,11 +636,10 @@
         name="rim_lookup",
     )(
         table, two, one, pick_row, pick_lane, used, edge_rows, ocean_levels, surface_height, transport,
-        inv_rows,
     )
     pairs = lat_pairs(n_lat, n_lon)
+    first = lax.ppermute(first, ("lat", "lon"), pairs[0])
     second = lax.ppermute(second, ("lat", "lon"), pairs[1])
-    first = lax.ppermute(first, ("lat", "lon"), pairs[0])
 
     flux, rim = pl.pallas_call(
         lookup_kernel,
@@ -663,7 +666,7 @@
         compiler_params=params(),
         name="step",
     )(
-        second, first, surface_height, transport, ocean_levels, diffusivity, flux, rim, edge_rows, inv_rows,
+        first, second, surface_height, transport, ocean_levels, diffusivity, flux, rim, edge_rows, inv_rows,
         solved, unit,
     )
 

time: 51.3 us -> 51.6 us (level)
    ppermute x1, waiting for transfers between devices: 2.53 us -> 0.01 us  [per_device(): first = lax.ppermute(first, ('lat', 'lon'), pairs[0])]
    ppermute x1, waiting for transfers between devices: 0.68 us -> 2.39 us  [per_device(): second = lax.ppermute(second, ('lat', 'lon'), pairs[1])]
    ppermute x1, starting transfers between devices: 8.37 us -> 7.14 us  [per_device(): second = lax.ppermute(second, ('lat', 'lon'), pairs[1])]
    all_to_all x1, waiting for transfers between devices: 0.01 us -> 0.95 us  [per_device(): lax.all_to_all(picked, 'lon', split_axis=0, concat_axis=0, tiled=True)]
    ppermute x1, starting transfers between devices: 1.92 us -> 2.65 us  [per_device(): first = lax.ppermute(first, ('lat', 'lon'), pairs[0])]
  transfers between devices with their start and end apart: 5 -> 5, of which waited for: 3 -> 3; matrix products, arithmetic and copies ran while one was open for 0% -> 0% of each run, Pallas kernels for 8% -> 9%
where the time goes in v5:
time: 51.6 us; the launch traced here: 50.9 us
  starting transfers between devices  36.7 us (71%)
  Pallas kernels  8.84 us (17%)
  waiting for transfers between devices  4.51 us (9%)
  between operations  0.85 us (2%)
    all_to_all x1, starting transfers between devices, per_device(): lax.all_to_all(picked, 'lon', split_axis=0, concat_axis=0, tiled=True)  15.4 us
    ppermute x1, starting transfers between devices, per_device(): two = lax.ppermute(two, 'lon', pairs[1])  9.55 us
    ppermute x1, starting transfers between devices, per_device(): second = lax.ppermute(second, ('lat', 'lon'), pairs[1])  7.14 us
    ppermute x1, starting transfers between devices, per_device(): first = lax.ppermute(first, ('lat', 'lon'), pairs[0])  2.65 us
    ppermute x1, waiting for transfers between devices, per_device(): second = lax.ppermute(second, ('lat', 'lon'), pairs[1])  2.39 us
    ppermute x1, starting transfers between devices, per_device(): one = lax.ppermute(one, 'lon', pairs[0])  1.92 us
    pallas_call x1, Pallas kernels, per_device(): pl.pallas_call(step_kernel, out_shape=(shape_of(2, depth, rows, cols), sh...  1.82 us
    pallas_call x1, Pallas kernels, per_device(): pl.pallas_call(pick_kernel, out_shape=pltpu.VMEM((n_lon, 1, 10 * slots),...  1.75 us
  transfers between devices with their start and end apart: 5, of which 3 were waited for; matrix products, arithmetic and copies ran while one was open for 0% of the time, Pallas kernels for 9%

profile of v5, /device:TPU:120, one launch (start us, length us, event | category | flops | bytes accessed | tf_op | source)
XLA Modules:
  0.0 50.9 jit_solution(5624822449020029892)
XLA Ops:
  0.6 0.0 copy-start.5
  0.6 0.0 copy-start.6
  0.7 1.8 %pick.1.picked_ref = f32[32,1,640]{2,1,0:T(1,128)} custom-call(f32[1,4,512]{2,1,0:T(4,128)} %atm_hbm.1, s32[1,1,32,64]{3,2,1,0:T(8,128)} %rows_hbm.1), custom_call_target="tpu_custom_call" | custom-call | flops 40000000 | bytes 40000000 | tf_op jit(solution)/shard_map/pick/pallas_call | solution.py:558
  2.4 0.0 copy-start
  2.4 0.0 copy-start.1
  2.4 0.0 copy-start.2
  2.5 0.0 copy-start.4
  2.5 0.0 copy-start.7
  2.5 15.4 %all-to-all-start = ((f32[32,1,640]{2,1,0:T(1,128)}), f32[32,1,640]{2,1,0:T(1,128)S(1)}, u32[]{:S(2)}, u32[]{:S(2)}) async-start(f32[32,1,640]{2,1,0:T(1,128)} %pick.1.picked_ref), calls=%async_computation | async-start | bytes 163840 | tf_op jit(solution)/shard_map/all_to_all | solution.py:572
  17.9 0.0 copy-done.5
  17.9 0.0 copy-done.6
  17.9 0.0 copy-done
  17.9 0.0 copy-done.1
  17.9 0.0 copy-done.2
  17.9 0.0 copy-done.4
  17.9 0.0 copy-done.7
  17.9 1.7 %edges.1 = (f32[64,128]{1,0:T(8,128)S(1)}, f32[64,128]{1,0:T(8,128)S(1)}, f32[32,128]{1,0:T(8,128)S(1)}, f32[2,72,128]{2,1,0:T(8,128)S(1)}, s32[4,32,128]{2,1,0:...) custom-call(f32[32,1,640]{2,1,0:T(1,128)} %pick.1.picked_ref, ...), custom_call_target="tpu_custom_call" | custom-call | flops 2000000 | bytes 2000000 | tf_op jit(solution)/shard_map/edges/pallas_call | solution.py:576
  19.6 9.6 %collective-permute-start = (f32[64,128]{1,0:T(8,128)S(1)}, f32[64,128]{1,0:T(8,128)S(1)}, u32[]{:S(2)}, u32[]{:S(2)}) collective-permute-start(f32[64,128]{1,0:T(8,128)S(1)} %get-tuple-element.23), channel_id=1, source_target_pairs={{1,2},{2,1},{3,4},{4,3},{5,6},{6,5},{7,8},{8,7},{9,10},{10,9},{11,... | collective-permute-start | bytes 98312 | tf_op jit(solution)/shard_map/ppermute | solution.py:600
  29.2 1.9 %collective-permute-start.1 = (f32[64,128]{1,0:T(8,128)S(1)}, f32[64,128]{1,0:T(8,128)S(1)}, u32[]{:S(2)}, u32[]{:S(2)}) collective-permute-start(f32[64,128]{1,0:T(8,128)S(1)} %get-tuple-element.24), channel_id=1, source_target_pairs={{0,1},{1,0},{2,3},{3,2},{4,5},{5,4},{6,7},{7,6},{8,9},{9,8},{10,11... | collective-permute-start | bytes 98312 | tf_op jit(solution)/shard_map/ppermute | solution.py:601
  31.1 0.0 collective-permute-done.two_ref
  31.1 1.2 %collective-permute-done.1.one_ref = f32[64,128]{1,0:T(8,128)S(1)} collective-permute-done((f32[64,128]{1,0:T(8,128)S(1)}, f32[64,128]{1,0:T(8,128)S(1)}, u32[]{:S(2)}, u32[]{:S(2)}) %collective-permute-start.1) | collective-permute-done | bytes 32800 | tf_op jit(solution)/shard_map/ppermute | solution.py:601
  32.3 1.0 %all-to-all-done.table_ref = f32[32,1,640]{2,1,0:T(1,128)S(1)} async-done(((f32[32,1,640]{2,1,0:T(1,128)}), f32[32,1,640]{2,1,0:T(1,128)S(1)}, u32[]{:S(2)}, u32[]{:S(2)}) %all-to-all-start) | async-done | bytes 81952 | tf_op jit(solution)/shard_map/all_to_all | solution.py:572
  33.3 0.0 copy-start.3
  33.3 0.9 %rim_lookup.1 = (f32[136,128]{1,0:T(8,128)S(1)}, f32[136,128]{1,0:T(8,128)S(1)}, f32[2,3,8,128]{3,2,1,0:T(8,128)S(1)}, f32[2,3,8,128]{3,2,1,0:T(8,128)S(1)}, f32...) custom-call(f32[32,1,640]{2,1,0:T(1,128)S(1)} %all-to-all-done.table_ref, f32[64,128]{1,0:T(8,128)S(1)} %collective-permute-done.two_ref, ...), custom_call_target="tpu_custom_call" | custom-call | flops 8000000 | bytes 8000000 | tf_op jit(solution)/shard_map/rim_lookup/pallas_call | solution.py:621
  34.1 2.7 %collective-permute-start.2 = (f32[136,128]{1,0:T(8,128)S(1)}, f32[136,128]{1,0:T(8,128)S(1)}, u32[]{:S(2)}, u32[]{:S(2)}) collective-permute-start(f32[136,128]{1,0:T(8,128)S(1)} %get-tuple-element.29), channel_id=1, source_target_pairs={{0,32},{32,0},{64,96},{96,64},{128,160},{160,128},{192,224},{224,1... | collective-permute-start | bytes 208904 | tf_op jit(solution)/shard_map/ppermute | solution.py:641
  36.8 7.1 %collective-permute-start.3 = (f32[136,128]{1,0:T(8,128)S(1)}, f32[136,128]{1,0:T(8,128)S(1)}, u32[]{:S(2)}, u32[]{:S(2)}) collective-permute-start(f32[136,128]{1,0:T(8,128)S(1)} %get-tuple-element.30), channel_id=1, source_target_pairs={{32,64},{64,32},{96,128},{128,96},{160,192},{192,160},{224,256},{2... | collective-permute-start | bytes 208904 | tf_op jit(solution)/shard_map/ppermute | solution.py:642
  43.9 0.0 copy-done.3
  43.9 1.7 %tracers.1 = (f32[2,24,32,128]{3,2,1,0:T(8,128)S(1)}, f32[24,32,128]{2,1,0:T(8,128)S(1)}, f32[2,24,128]{2,1,0:T(8,128)S(1)}) custom-call(f32[64,128]{1,0:T(8,128)S(1)} %collective-permute-done.two_ref, f32[64,128]{1,0:T(8,128)S(1)} %collective-permute-done.1.one_ref, f32[32,128]{1,0:T(8,128)S(1)} %get-tuple-element.37.t_0_ref, s32[32,128]{1,0:T(8,128)S(1)} %copy-done.1, ...), custom_call_target="tpu_custom_call" | custom-call | flops 8000000 | bytes 8000000 | tf_op jit(solution)/shard_map/tracers/pallas_call | solution.py:603
  45.6 1.1 %lookup.1 = (f32[4,32,128]{2,1,0:T(8,128)S(1)}, f32[7,32,128]{2,1,0:T(8,128)S(1)}) custom-call(f32[2,3,8,128]{3,2,1,0:T(8,128)S(1)} %get-tuple-element.31.edge_flux_ref, f32[2,3,8,128]{3,2,1,0:T(8,128)S(1)} %get-tuple-element.32.edge_rim_ref, f32[4,16,128]{2,1,0:T(8,128)S(1)} %get-tuple-element.33.tab, f32[3,32,128]{2,1,0:T(8,128)S(1)} %get-tuple-element.34.side, ...), custom_call_target="tpu_custom_call" | custom-call | flops 8000000 | bytes 8000000 | tf_op jit(solution)/shard_map/lookup/pallas_call | solution.py:644
  46.7 0.0 collective-permute-done.2.first_ref
  46.7 2.4 %collective-permute-done.3.second_ref = f32[136,128]{1,0:T(8,128)S(1)} collective-permute-done((f32[136,128]{1,0:T(8,128)S(1)}, f32[136,128]{1,0:T(8,128)S(1)}, u32[]{:S(2)}, u32[]{:S(2)}) %collective-permute-start.3) | collective-permute-done | bytes 69664 | tf_op jit(solution)/shard_map/ppermute | solution.py:642
  49.1 1.8 %step.1 = (f32[2,24,32,128]{3,2,1,0:T(8,128)}, f32[32,128]{1,0:T(8,128)}, f32[2,32,128]{2,1,0:T(8,128)}) custom-call(f32[136,128]{1,0:T(8,128)S(1)} %collective-permute-done.2.first_ref, f32[136,128]{1,0:T(8,128)S(1)} %collective-permute-done.3.second_ref, f32[32,128]{1,0:T(8,128)S(1)} %copy-done.2, f32[2,32,128]{2,1,0:T(8,128)S(1)} %copy-done, ...), custom_call_target="tpu_custom_call" | custom-call | tf_op jit(solution)/shard_map/step/pallas_call | solution.py:654
Async XLA Ops:
  0.6 17.2 %copy-start.5 = (s32[4,32,128]{2,1,0:T(8,128)S(1)}, s32[4,32,128]{2,1,0:T(8,128)}, u32[]{:S(2)}) copy-start(s32[4,32,128]{2,1,0:T(8,128)} %slot_ref.1) | copy-start | bytes 196612
  0.6 17.2 %copy-start.6 = (f32[4,32,128]{2,1,0:T(8,128)S(1)}, f32[4,32,128]{2,1,0:T(8,128)}, u32[]{:S(2)}) copy-start(f32[4,32,128]{2,1,0:T(8,128)} %weight_ref.1) | copy-start | bytes 196612
  2.4 15.5 %copy-start = (f32[2,32,128]{2,1,0:T(8,128)S(1)}, f32[2,32,128]{2,1,0:T(8,128)}, u32[]{:S(2)}) copy-start(f32[2,32,128]{2,1,0:T(8,128)} %transport_ref.5) | copy-start | bytes 98308
  2.4 15.5 %copy-start.1 = (s32[32,128]{1,0:T(8,128)S(1)}, s32[32,128]{1,0:T(8,128)}, u32[]{:S(2)}) copy-start(s32[32,128]{1,0:T(8,128)} %level_ref.7) | copy-start | bytes 49156
  2.4 15.5 %copy-start.2 = (f32[32,128]{1,0:T(8,128)S(1)}, f32[32,128]{1,0:T(8,128)}, u32[]{:S(2)}) copy-start(f32[32,128]{1,0:T(8,128)} %height_ref.5) | copy-start | bytes 49156
  2.5 15.5 %copy-start.4 = (s32[4,32,128]{2,1,0:T(8,128)S(1)}, s32[4,32,128]{2,1,0:T(8,128)}, u32[]{:S(2)}) copy-start(s32[4,32,128]{2,1,0:T(8,128)} %owner_ref.1) | copy-start | bytes 196612
  2.5 15.5 %copy-start.7 = (s32[32,128]{1,0:T(8,128)S(1)}, s32[32,128]{1,0:T(8,128)}, u32[]{:S(2)}) copy-start(s32[32,128]{1,0:T(8,128)} %count_ref.1) | copy-start | bytes 49156
  2.5 30.8 %all-to-all-start = ((f32[32,1,640]{2,1,0:T(1,128)}), f32[32,1,640]{2,1,0:T(1,128)S(1)}, u32[]{:S(2)}, u32[]{:S(2)}) async-start(f32[32,1,640]{2,1,0:T(1,128)} %pick.1.picked_ref), calls=%async_computation | async-start | bytes 163840 | tf_op jit(solution)/shard_map/all_to_all | solution.py:572
  19.6 11.5 %collective-permute-start = (f32[64,128]{1,0:T(8,128)S(1)}, f32[64,128]{1,0:T(8,128)S(1)}, u32[]{:S(2)}, u32[]{:S(2)}) collective-permute-start(f32[64,128]{1,0:T(8,128)S(1)} %get-tuple-element.23), channel_id=1, source_target_pairs={{1,2},{2,1},{3,4},{4,3},{5,6},{6,5},{7,8},{8,7},{9,10},{10,9},{11,... | collective-permute-start | bytes 98312 | tf_op jit(solution)/shard_map/ppermute | solution.py:600
  29.2 3.1 %collective-permute-start.1 = (f32[64,128]{1,0:T(8,128)S(1)}, f32[64,128]{1,0:T(8,128)S(1)}, u32[]{:S(2)}, u32[]{:S(2)}) collective-permute-start(f32[64,128]{1,0:T(8,128)S(1)} %get-tuple-element.24), channel_id=1, source_target_pairs={{0,1},{1,0},{2,3},{3,2},{4,5},{5,4},{6,7},{7,6},{8,9},{9,8},{10,11... | collective-permute-start | bytes 98312 | tf_op jit(solution)/shard_map/ppermute | solution.py:601
  33.3 10.7 %copy-start.3 = (f32[32,128]{1,0:T(8,128)S(1)}, f32[32,128]{1,0:T(8,128)}, u32[]{:S(2)}) copy-start(f32[32,128]{1,0:T(8,128)} %diff_ref.3) | copy-start | bytes 49156
  34.1 12.6 %collective-permute-start.2 = (f32[136,128]{1,0:T(8,128)S(1)}, f32[136,128]{1,0:T(8,128)S(1)}, u32[]{:S(2)}, u32[]{:S(2)}) collective-permute-start(f32[136,128]{1,0:T(8,128)S(1)} %get-tuple-element.29), channel_id=1, source_target_pairs={{0,32},{32,0},{64,96},{96,64},{128,160},{160,128},{192,224},{224,1... | collective-permute-start | bytes 208904 | tf_op jit(solution)/shard_map/ppermute | solution.py:641
  36.8 12.3 %collective-permute-start.3 = (f32[136,128]{1,0:T(8,128)S(1)}, f32[136,128]{1,0:T(8,128)S(1)}, u32[]{:S(2)}, u32[]{:S(2)}) collective-permute-start(f32[136,128]{1,0:T(8,128)S(1)} %get-tuple-element.30), channel_id=1, source_target_pairs={{32,64},{64,32},{96,128},{128,96},{160,192},{192,160},{224,256},{2... | collective-permute-start | bytes 208904 | tf_op jit(solution)/shard_map/ppermute | solution.py:642

commit v6 on v5

--- a/solution.py
+++ b/solution.py
@@ -207,7 +207,7 @@
 
 def rim_lookup_kernel(
     table_ref, two_ref, one_ref, pick_row_ref, pick_lane_ref, used_ref, rows_ref, level_ref, height_ref,
-    transport_ref, first_ref, second_ref, flux_ref, rim_ref, tab, side, pack,
+    transport_ref, second_ref, first_ref, flux_ref, rim_ref, tab, side, pack,
 ):
     n_lon = table_ref.shape[0]
     half = n_lon // 2
@@ -244,15 +244,21 @@
         pack[s, ROW_T:] = rows_ref[s]
     even = is_even("lat")
     north_going, south_going = pack[0], pack[1]
+    second_ref[...] = jnp.where(even, south_going, north_going)
     first_ref[...] = jnp.where(even, north_going, south_going)
-    second_ref[...] = jnp.where(even, south_going, north_going)
+
+
+def sources(flux_ref, level_ref, cut):
+    wet = (level_ref[cut] > 0).astype(F32)
+    return heat_gain * flux_ref[0, cut] * wet, -salt_gain * flux_ref[1, cut] * wet
 
 
 def lookup_kernel(
     edge_flux_ref, edge_rim_ref, tab, side, two_ref, one_ref, pick_row_ref, pick_lane_ref, used_ref,
-    flux_ref, rim_ref,
+    level_ref, x_ref, unit_ref, flux_ref, rim_ref, t_out, fixed, sems,
 ):
     rows = used_ref.shape[1]
+    depth = x_ref.shape[1]
     cuts = [slice(at, at + HALO) for at in range(0, rows, HALO)]
     sides = [from_lon(one_ref, two_ref, cut) for cut in cuts]
     for at in range(1, len(cuts) - 1, 2):
@@ -264,6 +270,14 @@
                 flux_ref[f, cut] = found[f]
             for g, rim in enumerate(state_rims(*sides[at + i]) + side_rims[i]):
                 rim_ref[g, cut] = rim
+    mid = slice(HALO, rows - HALO)
+    source = sources(flux_ref, level_ref, mid)
+    copies = []
+    for c in range(2):
+        for l in range(depth):
+            fixed[c, l] = x_ref[c, l, mid] + unit_ref[l, mid] * source[c]
+        copies.append(pltpu.make_async_copy(fixed.at[c], t_out.at[c, :, mid], sems.at[c]))
+        copies[c].start()
     for s, at in ((0, len(cuts) - 1), (1, 0)):
         cut = cuts[at]
         flux_ref[0, cut] = own_lookup(tab, pick_row_ref, pick_lane_ref, used_ref, cut, (0,))[0]
@@ -271,6 +285,8 @@
             flux_ref[f + 1, cut] = edge_flux_ref[s, f]
         for g, rim in enumerate(state_rims(*sides[at]) + [edge_rim_ref[s, f] for f in range(3)]):
             rim_ref[g, cut] = rim
+    for copy in copies:
+        copy.wait()
 
 
 def split(x):
@@ -365,28 +381,21 @@
 
 
 def step_kernel(
-    first_ref, second_ref, height_ref, transport_ref, level_ref, diff_ref, flux_ref, rim_ref, rows_ref, inv_rows_ref,
-    x_ref, unit_ref, t_out, height_out, transport_out, north_ref, shift, fixed, result, sems,
+    second_ref, first_ref, height_ref, transport_ref, level_ref, diff_ref, flux_ref, rim_ref, rows_ref, inv_rows_ref,
+    x_ref, unit_ref, t_middle, t_out, height_out, transport_out, north_ref, shift, fixed, result, sems,
 ):
     top = is_top()
     level = level_ref[...]
     level_f = level.astype(F32)
     rows, cols = level.shape
     depth = x_ref.shape[1]
-    wet_0 = (level > 0).astype(F32)
-    source = (heat_gain * flux_ref[0] * wet_0, -salt_gain * flux_ref[1] * wet_0)
     lo, hi = slice(0, HALO), slice(rows - HALO, rows)
-    mid = slice(HALO, rows - HALO)
     copies = []
 
     def send(value, out):
         copies.append(pltpu.make_async_copy(value, out, sems.at[len(copies)]))
         copies[-1].start()
 
-    for c in range(2):
-        for l in range(depth):
-            fixed[c, l, mid] = x_ref[c, l, mid] + unit_ref[l, mid] * source[c][mid]
-        send(fixed.at[c, :, mid], t_out.at[c, :, mid])
     even = is_even("lat")
     a, b = first_ref[...], second_ref[...]
     south = jnp.where(even, b, a)
@@ -430,13 +439,14 @@
             shift[s, at : at + 1] = right[i]
     row = rows_of((HALO, cols))
     for s, cut, at_row in ((0, hi, HALO - 1), (1, lo, 0)):
+        source = sources(flux_ref, level_ref, cut)
         for c in range(2):
             for l in range(depth):
                 at = c * depth + l
                 add = jnp.broadcast_to(shift[s, at : at + 1], (HALO, cols))
-                x = x_ref[c, l, cut] + unit_ref[l, cut] * source[c][cut]
-                fixed[c, l, cut] = x + jnp.where(row == at_row, add, 0.0)
-        send(fixed.at[:, :, cut], t_out.at[:, :, cut])
+                x = x_ref[c, l, cut] + unit_ref[l, cut] * source[c]
+                fixed[s, c, l] = x + jnp.where(row == at_row, add, 0.0)
+        send(fixed.at[s], t_out.at[:, :, cut])
 
     own = (
         height_ref[...], transport_ref[0], transport_ref[1], level_f,
@@ -618,7 +628,7 @@
         name="tracers",
     )(two, one, t_0, ocean_levels, diffusivity, tracers, speed_e, in_hbm(velocity))
 
-    first, second, edge_flux, edge_rim, tab, side = pl.pallas_call(
+    second, first, edge_flux, edge_rim, tab, side = pl.pallas_call(
         rim_lookup_kernel,
         out_shape=(
             shape_of(lat_rows, cols),
@@ -638,36 +648,40 @@
         table, two, one, pick_row, pick_lane, used, edge_rows, ocean_levels, surface_height, transport,
     )
     pairs = lat_pairs(n_lat, n_lon)
+    second = lax.ppermute(second, ("lat", "lon"), pairs[1])
     first = lax.ppermute(first, ("lat", "lon"), pairs[0])
-    second = lax.ppermute(second, ("lat", "lon"), pairs[1])
-
-    flux, rim = pl.pallas_call(
+
+    flux, rim, t_middle = pl.pallas_call(
         lookup_kernel,
-        out_shape=(shape_of(4, *block), shape_of(FIELDS, *block)),
-        in_specs=vmem(9),
-        out_specs=vmem(2),
+        out_shape=(shape_of(4, *block), shape_of(FIELDS, *block), shape_of(2, depth, *block)),
+        in_specs=vmem(12),
+        out_specs=vmem(2) + [pl.BlockSpec(memory_space=pltpu.HBM)],
+        scratch_shapes=[pltpu.VMEM((2, depth, rows - 2 * HALO, cols), F32), pltpu.SemaphoreType.DMA((2,))],
         compiler_params=params(),
         cost_estimate=work(8),
         name="lookup",
-    )(edge_flux, edge_rim, tab, side, two, one, pick_row, pick_lane, used)
+    )(
+        edge_flux, edge_rim, tab, side, two, one, pick_row, pick_lane, used, ocean_levels, solved, unit,
+    )
 
     return pl.pallas_call(
         step_kernel,
         out_shape=(shape_of(2, depth, rows, cols), shape_of(rows, cols), shape_of(2, rows, cols)),
-        in_specs=vmem(12),
-        out_specs=(pl.BlockSpec(memory_space=pl.ANY),) * 3,
+        in_specs=vmem(12) + [pl.BlockSpec(memory_space=pltpu.HBM)],
+        out_specs=(pl.BlockSpec(memory_space=pltpu.HBM),) * 3,
+        input_output_aliases={12: 0},
         scratch_shapes=[
             pltpu.VMEM((lat_rows, cols), F32),
             pltpu.VMEM((2, 2 * depth, cols), F32),
-            pltpu.VMEM((2, depth, rows, cols), F32),
+            pltpu.VMEM((2, 2, depth, HALO, cols), F32),
             pltpu.VMEM((3, rows, cols), F32),
-            pltpu.SemaphoreType.DMA((6,)),
+            pltpu.SemaphoreType.DMA((4,)),
         ],
         compiler_params=params(),
         name="step",
     )(
-        first, second, surface_height, transport, ocean_levels, diffusivity, flux, rim, edge_rows, inv_rows,
-        solved, unit,
+        second, first, surface_height, transport, ocean_levels, diffusivity, flux, rim, edge_rows, inv_rows,
+        solved, unit, t_middle,
     )
 
 

time: 51.6 us -> 50.3 us (0.975)
  the two profiles are of different devices: /device:TPU:120 before, /device:TPU:112 now
where the time goes in v6:
time: 50.3 us; the launch traced here: 49.9 us
  starting transfers between devices  37.5 us (75%)
  Pallas kernels  9.43 us (19%)
  waiting for transfers between devices  2.12 us (4%)
  between operations  0.85 us (2%)
    all_to_all x1, starting transfers between devices, per_device(): lax.all_to_all(picked, 'lon', split_axis=0, concat_axis=0, tiled=True)  15.4 us
    ppermute x1, starting transfers between devices, per_device(): two = lax.ppermute(two, 'lon', pairs[1])  9.55 us
    ppermute x1, starting transfers between devices, per_device(): first = lax.ppermute(first, ('lat', 'lon'), pairs[0])  8.26 us
    ppermute x1, starting transfers between devices, per_device(): second = lax.ppermute(second, ('lat', 'lon'), pairs[1])  2.36 us
    ppermute x1, starting transfers between devices, per_device(): one = lax.ppermute(one, 'lon', pairs[0])  1.92 us
    pallas_call x1, Pallas kernels, per_device(): pl.pallas_call(step_kernel, out_shape=(shape_of(2, depth, rows, cols), sh...  1.77 us
    pallas_call x1, Pallas kernels, per_device(): pl.pallas_call(pick_kernel, out_shape=pltpu.VMEM((n_lon, 1, 10 * slots),...  1.75 us
    pallas_call x1, Pallas kernels, per_device(): pl.pallas_call(lookup_kernel, out_shape=(shape_of(4, *block), shape_of(FI...  1.69 us
  transfers between devices with their start and end apart: 5, of which 2 were waited for; matrix products, arithmetic and copies ran while one was open for 0% of the time, Pallas kernels for 10%

profile of v6, /device:TPU:112, one launch (start us, length us, event | category | flops | bytes accessed | tf_op | source)
XLA Modules:
  0.0 49.9 jit_solution(4993348146387368879)
XLA Ops:
  0.6 0.0 copy-start.5
  0.6 0.0 copy-start.6
  0.7 1.8 %pick.1.picked_ref = f32[32,1,640]{2,1,0:T(1,128)} custom-call(f32[1,4,512]{2,1,0:T(4,128)} %atm_hbm.1, s32[1,1,32,64]{3,2,1,0:T(8,128)} %rows_hbm.1), custom_call_target="tpu_custom_call" | custom-call | flops 40000000 | bytes 40000000 | tf_op jit(solution)/shard_map/pick/pallas_call | solution.py:568
  2.4 0.0 copy-start
  2.4 0.0 copy-start.1
  2.4 0.0 copy-start.2
  2.5 0.0 copy-start.4
  2.5 0.0 copy-start.7
  2.5 15.4 %all-to-all-start = ((f32[32,1,640]{2,1,0:T(1,128)}), f32[32,1,640]{2,1,0:T(1,128)S(1)}, u32[]{:S(2)}, u32[]{:S(2)}) async-start(f32[32,1,640]{2,1,0:T(1,128)} %pick.1.picked_ref), calls=%async_computation | async-start | bytes 163840 | tf_op jit(solution)/shard_map/all_to_all | solution.py:582
  17.9 0.0 copy-done.5
  17.9 0.0 copy-done.6
  17.9 0.0 copy-done
  17.9 0.0 copy-done.1
  17.9 0.0 copy-done.2
  17.9 0.0 copy-done.4
  17.9 0.0 copy-done.7
  17.9 1.7 %edges.1 = (f32[64,128]{1,0:T(8,128)S(1)}, f32[64,128]{1,0:T(8,128)S(1)}, f32[32,128]{1,0:T(8,128)S(1)}, f32[2,72,128]{2,1,0:T(8,128)S(1)}, s32[4,32,128]{2,1,0:...) custom-call(f32[32,1,640]{2,1,0:T(1,128)} %pick.1.picked_ref, ...), custom_call_target="tpu_custom_call" | custom-call | flops 2000000 | bytes 2000000 | tf_op jit(solution)/shard_map/edges/pallas_call | solution.py:586
  19.6 9.6 %collective-permute-start = (f32[64,128]{1,0:T(8,128)S(1)}, f32[64,128]{1,0:T(8,128)S(1)}, u32[]{:S(2)}, u32[]{:S(2)}) collective-permute-start(f32[64,128]{1,0:T(8,128)S(1)} %get-tuple-element.24), channel_id=1, source_target_pairs={{1,2},{2,1},{3,4},{4,3},{5,6},{6,5},{7,8},{8,7},{9,10},{10,9},{11,... | collective-permute-start | bytes 98312 | tf_op jit(solution)/shard_map/ppermute | solution.py:610
  29.2 1.9 %collective-permute-start.1 = (f32[64,128]{1,0:T(8,128)S(1)}, f32[64,128]{1,0:T(8,128)S(1)}, u32[]{:S(2)}, u32[]{:S(2)}) collective-permute-start(f32[64,128]{1,0:T(8,128)S(1)} %get-tuple-element.25), channel_id=1, source_target_pairs={{0,1},{1,0},{2,3},{3,2},{4,5},{5,4},{6,7},{7,6},{8,9},{9,8},{10,11... | collective-permute-start | bytes 98312 | tf_op jit(solution)/shard_map/ppermute | solution.py:611
  31.1 0.0 collective-permute-done.two_ref
  31.1 1.2 %collective-permute-done.1.one_ref = f32[64,128]{1,0:T(8,128)S(1)} collective-permute-done((f32[64,128]{1,0:T(8,128)S(1)}, f32[64,128]{1,0:T(8,128)S(1)}, u32[]{:S(2)}, u32[]{:S(2)}) %collective-permute-start.1) | collective-permute-done | bytes 32800 | tf_op jit(solution)/shard_map/ppermute | solution.py:611
  32.3 1.0 %all-to-all-done.table_ref = f32[32,1,640]{2,1,0:T(1,128)S(1)} async-done(((f32[32,1,640]{2,1,0:T(1,128)}), f32[32,1,640]{2,1,0:T(1,128)S(1)}, u32[]{:S(2)}, u32[]{:S(2)}) %all-to-all-start) | async-done | bytes 81952 | tf_op jit(solution)/shard_map/all_to_all | solution.py:582
  33.3 0.0 copy-start.3
  33.3 0.9 %rim_lookup.1 = (f32[136,128]{1,0:T(8,128)S(1)}, f32[136,128]{1,0:T(8,128)S(1)}, f32[2,3,8,128]{3,2,1,0:T(8,128)S(1)}, f32[2,3,8,128]{3,2,1,0:T(8,128)S(1)}, f32...) custom-call(f32[32,1,640]{2,1,0:T(1,128)S(1)} %all-to-all-done.table_ref, f32[64,128]{1,0:T(8,128)S(1)} %collective-permute-done.two_ref, ...), custom_call_target="tpu_custom_call" | custom-call | flops 8000000 | bytes 8000000 | tf_op jit(solution)/shard_map/rim_lookup/pallas_call | solution.py:631
  34.1 2.4 %collective-permute-start.2 = (f32[136,128]{1,0:T(8,128)S(1)}, f32[136,128]{1,0:T(8,128)S(1)}, u32[]{:S(2)}, u32[]{:S(2)}) collective-permute-start(f32[136,128]{1,0:T(8,128)S(1)} %get-tuple-element.30), channel_id=1, source_target_pairs={{32,64},{64,32},{96,128},{128,96},{160,192},{192,160},{224,256},{2... | collective-permute-start | bytes 208904 | tf_op jit(solution)/shard_map/ppermute | solution.py:651
  36.5 8.3 %collective-permute-start.3 = (f32[136,128]{1,0:T(8,128)S(1)}, f32[136,128]{1,0:T(8,128)S(1)}, u32[]{:S(2)}, u32[]{:S(2)}) collective-permute-start(f32[136,128]{1,0:T(8,128)S(1)} %get-tuple-element.31), channel_id=1, source_target_pairs={{0,32},{32,0},{64,96},{96,64},{128,160},{160,128},{192,224},{224,1... | collective-permute-start | bytes 208904 | tf_op jit(solution)/shard_map/ppermute | solution.py:652
  44.8 0.0 copy-done.3
  44.8 1.7 %tracers.1 = (f32[2,24,32,128]{3,2,1,0:T(8,128)S(1)}, f32[24,32,128]{2,1,0:T(8,128)S(1)}, f32[2,24,128]{2,1,0:T(8,128)S(1)}) custom-call(f32[64,128]{1,0:T(8,128)S(1)} %collective-permute-done.two_ref, f32[64,128]{1,0:T(8,128)S(1)} %collective-permute-done.1.one_ref, f32[32,128]{1,0:T(8,128)S(1)} %get-tuple-element.36.t_0_ref, s32[32,128]{1,0:T(8,128)S(1)} %copy-done, ...), custom_call_target="tpu_custom_call" | custom-call | flops 8000000 | bytes 8000000 | tf_op jit(solution)/shard_map/tracers/pallas_call | solution.py:613
  46.4 1.7 %lookup.1 = (f32[4,32,128]{2,1,0:T(8,128)S(1)}, f32[7,32,128]{2,1,0:T(8,128)S(1)}, f32[2,24,32,128]{3,2,1,0:T(8,128)}) custom-call(f32[2,3,8,128]{3,2,1,0:T(8,128)S(1)} %get-tuple-element.32.edge_flux_ref, f32[2,3,8,128]{3,2,1,0:T(8,128)S(1)} %get-tuple-element.33.edge_rim_ref, f32[4,16,128]{2,1,0:T(8,128)S(1)} %get-tuple-element.34.tab, ...), custom_call_target="tpu_custom_call" | custom-call | flops 8000000 | bytes 8000000 | tf_op jit(solution)/shard_map/lookup/pallas_call | solution.py:654
  48.1 0.0 collective-permute-done.2.second_ref
  48.1 0.0 collective-permute-done.3.first_ref
  48.2 1.8 %step.1 = (f32[2,24,32,128]{3,2,1,0:T(8,128)}, f32[32,128]{1,0:T(8,128)}, f32[2,32,128]{2,1,0:T(8,128)}) custom-call(f32[136,128]{1,0:T(8,128)S(1)} %collective-permute-done.2.second_ref, f32[136,128]{1,0:T(8,128)S(1)} %collective-permute-done.3.first_ref, f32[32,128]{1,0:T(8,128)S(1)} %copy-done.2, ...), custom_call_target="tpu_custom_call", output_to_operand_aliasing={{0}: (12, {})} | custom-call | tf_op jit(solution)/shard_map/step/pallas_call | solution.py:667
Async XLA Ops:
  0.6 17.2 %copy-start.5 = (s32[4,32,128]{2,1,0:T(8,128)S(1)}, s32[4,32,128]{2,1,0:T(8,128)}, u32[]{:S(2)}) copy-start(s32[4,32,128]{2,1,0:T(8,128)} %slot_ref.1) | copy-start | bytes 196612
  0.6 17.2 %copy-start.6 = (f32[4,32,128]{2,1,0:T(8,128)S(1)}, f32[4,32,128]{2,1,0:T(8,128)}, u32[]{:S(2)}) copy-start(f32[4,32,128]{2,1,0:T(8,128)} %weight_ref.1) | copy-start | bytes 196612
  2.4 15.5 %copy-start = (s32[32,128]{1,0:T(8,128)S(1)}, s32[32,128]{1,0:T(8,128)}, u32[]{:S(2)}) copy-start(s32[32,128]{1,0:T(8,128)} %level_ref.9) | copy-start | bytes 49156
  2.4 15.5 %copy-start.1 = (f32[2,32,128]{2,1,0:T(8,128)S(1)}, f32[2,32,128]{2,1,0:T(8,128)}, u32[]{:S(2)}) copy-start(f32[2,32,128]{2,1,0:T(8,128)} %transport_ref.5) | copy-start | bytes 98308
  2.4 15.5 %copy-start.2 = (f32[32,128]{1,0:T(8,128)S(1)}, f32[32,128]{1,0:T(8,128)}, u32[]{:S(2)}) copy-start(f32[32,128]{1,0:T(8,128)} %height_ref.5) | copy-start | bytes 49156
  2.5 15.5 %copy-start.4 = (s32[4,32,128]{2,1,0:T(8,128)S(1)}, s32[4,32,128]{2,1,0:T(8,128)}, u32[]{:S(2)}) copy-start(s32[4,32,128]{2,1,0:T(8,128)} %owner_ref.1) | copy-start | bytes 196612
  2.5 15.5 %copy-start.7 = (s32[32,128]{1,0:T(8,128)S(1)}, s32[32,128]{1,0:T(8,128)}, u32[]{:S(2)}) copy-start(s32[32,128]{1,0:T(8,128)} %count_ref.1) | copy-start | bytes 49156
  2.5 30.8 %all-to-all-start = ((f32[32,1,640]{2,1,0:T(1,128)}), f32[32,1,640]{2,1,0:T(1,128)S(1)}, u32[]{:S(2)}, u32[]{:S(2)}) async-start(f32[32,1,640]{2,1,0:T(1,128)} %pick.1.picked_ref), calls=%async_computation | async-start | bytes 163840 | tf_op jit(solution)/shard_map/all_to_all | solution.py:582
  19.6 11.5 %collective-permute-start = (f32[64,128]{1,0:T(8,128)S(1)}, f32[64,128]{1,0:T(8,128)S(1)}, u32[]{:S(2)}, u32[]{:S(2)}) collective-permute-start(f32[64,128]{1,0:T(8,128)S(1)} %get-tuple-element.24), channel_id=1, source_target_pairs={{1,2},{2,1},{3,4},{4,3},{5,6},{6,5},{7,8},{8,7},{9,10},{10,9},{11,... | collective-permute-start | bytes 98312 | tf_op jit(solution)/shard_map/ppermute | solution.py:610
  29.2 3.1 %collective-permute-start.1 = (f32[64,128]{1,0:T(8,128)S(1)}, f32[64,128]{1,0:T(8,128)S(1)}, u32[]{:S(2)}, u32[]{:S(2)}) collective-permute-start(f32[64,128]{1,0:T(8,128)S(1)} %get-tuple-element.25), channel_id=1, source_target_pairs={{0,1},{1,0},{2,3},{3,2},{4,5},{5,4},{6,7},{7,6},{8,9},{9,8},{10,11... | collective-permute-start | bytes 98312 | tf_op jit(solution)/shard_map/ppermute | solution.py:611
  33.3 11.5 %copy-start.3 = (f32[32,128]{1,0:T(8,128)S(1)}, f32[32,128]{1,0:T(8,128)}, u32[]{:S(2)}) copy-start(f32[32,128]{1,0:T(8,128)} %diff_ref.3) | copy-start | bytes 49156
  34.1 14.0 %collective-permute-start.2 = (f32[136,128]{1,0:T(8,128)S(1)}, f32[136,128]{1,0:T(8,128)S(1)}, u32[]{:S(2)}, u32[]{:S(2)}) collective-permute-start(f32[136,128]{1,0:T(8,128)S(1)} %get-tuple-element.30), channel_id=1, source_target_pairs={{32,64},{64,32},{96,128},{128,96},{160,192},{192,160},{224,256},{2... | collective-permute-start | bytes 208904 | tf_op jit(solution)/shard_map/ppermute | solution.py:651
  36.5 11.7 %collective-permute-start.3 = (f32[136,128]{1,0:T(8,128)S(1)}, f32[136,128]{1,0:T(8,128)S(1)}, u32[]{:S(2)}, u32[]{:S(2)}) collective-permute-start(f32[136,128]{1,0:T(8,128)S(1)} %get-tuple-element.31), channel_id=1, source_target_pairs={{0,32},{32,0},{64,96},{96,64},{128,160},{160,128},{192,224},{224,1... | collective-permute-start | bytes 208904 | tf_op jit(solution)/shard_map/ppermute | solution.py:652

commit v7 on v5

--- a/solution.py
+++ b/solution.py
@@ -207,7 +207,7 @@
 
 def rim_lookup_kernel(
     table_ref, two_ref, one_ref, pick_row_ref, pick_lane_ref, used_ref, rows_ref, level_ref, height_ref,
-    transport_ref, first_ref, second_ref, flux_ref, rim_ref, tab, side, pack,
+    transport_ref, after_ref, second_ref, first_ref, flux_ref, rim_ref, tab, side, pack,
 ):
     n_lon = table_ref.shape[0]
     half = n_lon // 2
@@ -244,8 +244,8 @@
         pack[s, ROW_T:] = rows_ref[s]
     even = is_even("lat")
     north_going, south_going = pack[0], pack[1]
+    second_ref[...] = jnp.where(even, south_going, north_going)
     first_ref[...] = jnp.where(even, north_going, south_going)
-    second_ref[...] = jnp.where(even, south_going, north_going)
 
 
 def lookup_kernel(
@@ -278,9 +278,9 @@
     return hi, (x - hi.astype(F32)).astype(jnp.bfloat16)
 
 
-def tracer_kernel(
-    two_ref, one_ref, t_0_ref, level_ref, diff_ref, t_ref, u_ref, v_hbm, x_ref, unit_ref, inv_rows_ref, gain_ref,
-    parts, rims, net_x, v_ref, sem,
+def faces_kernel(
+    two_ref, one_ref, t_0_ref, level_ref, diff_ref, t_ref, u_ref, v_hbm,
+    net_x, v_ref, inv_ref, gain_ref, unit_ref, inv_rows_ref, parts, rims, sem,
 ):
     depth, rows, cols = t_ref.shape[1:]
     copy = pltpu.make_async_copy(v_hbm.at[1], v_ref, sem)
@@ -291,13 +291,10 @@
     level = level_ref[...]
     level_f = level.astype(F32)
     lane = lanes(shape)
-    row = rows_of(shape)
     first = LEVELS * HALO
     last = cols - 1
     level_e = jnp.where(lane == last, turn(east, last - first, 1), turn(level_f, -1, 1))
-    level_n = turn(level_f, -1, 0)
     face_e = jnp.minimum(level_f, level_e)
-    face_n = jnp.where(row == rows - 1, 0.0, jnp.minimum(level_f, level_n))
     t_0 = t_0_ref[...]
     u_w = jnp.where(lane < depth, turn(t_w, -2 * depth, 1), turn(t_w, -depth, 1))
     layer = jnp.where(lane < depth, lane, lane - depth).astype(F32)
@@ -327,45 +324,58 @@
             t_east = jnp.where(lane == last, rims[at], turn(t, -1, 1))
             flux_e = jnp.where(mask_e, u_l * (t + t_east), 0.0)
             net_x[at] = flux_e - jnp.where(lane == 0, rims[at], turn(flux_e, 1, 1))
-    copy.wait()
     diff = diff_ref[...]
     above = jnp.zeros(shape, F32)
-    inv = None
-    right = [None, None, None]
+    inv = unit = None
     for l in range(depth):
         below = jnp.where(level > l + 1, diff, 0.0) if l < depth - 1 else jnp.zeros(shape, F32)
         pivot = 1.0 + above + below
         if l > 0:
             pivot = pivot - above * above * inv
         inv = 1.0 / pivot
+        inv_ref[l] = inv
         inv_rows_ref[0, l : l + 1] = inv[rows - 1 : rows]
         inv_rows_ref[1, l : l + 1] = inv[0:1]
         gain_ref[l] = below * inv
+        unit = inv if l == 0 else above * unit * inv
+        unit_ref[l] = unit
+        above = below
+    for l in range(depth - 2, -1, -1):
+        unit = unit_ref[l] + gain_ref[l] * unit
+        unit_ref[l] = unit
+    copy.wait()
+
+
+def solve_kernel(net_x, level_ref, diff_ref, t_ref, v_ref, inv_ref, gain_ref, x_ref):
+    depth, rows, cols = t_ref.shape[1:]
+    shape = (rows, cols)
+    level = level_ref[...]
+    level_f = level.astype(F32)
+    face_n = jnp.where(rows_of(shape) == rows - 1, 0.0, jnp.minimum(level_f, turn(level_f, -1, 0)))
+    diff = diff_ref[...]
+    right = [None, None]
+    for l in range(depth):
+        above = jnp.where(level > l, diff, 0.0)
+        inv = inv_ref[l]
         mask_n = face_n > l
         v_l = v_ref[l] * 0.5
         for c in range(2):
             f = c * depth + l
-            at = slice(f * rows, (f + 1) * rows)
             t = t_ref[c, l]
             flux_n = jnp.where(mask_n, v_l * (t + turn(t, -1, 0)), 0.0)
             flux_s = turn(flux_n, 1, 0)
-            forced = t - adv_rate * (net_x[at] + (flux_n - flux_s))
+            forced = t - adv_rate * (net_x[f * rows : (f + 1) * rows] + (flux_n - flux_s))
             right[c] = forced * inv if l == 0 else (forced + above * right[c]) * inv
             x_ref[c, l] = right[c]
-        right[2] = inv if l == 0 else above * right[2] * inv
-        unit_ref[l] = right[2]
-        above = below
     for l in range(depth - 2, -1, -1):
         gain = gain_ref[l]
         for c in range(2):
             right[c] = x_ref[c, l] + gain * right[c]
             x_ref[c, l] = right[c]
-        right[2] = unit_ref[l] + gain * right[2]
-        unit_ref[l] = right[2]
 
 
 def step_kernel(
-    first_ref, second_ref, height_ref, transport_ref, level_ref, diff_ref, flux_ref, rim_ref, rows_ref, inv_rows_ref,
+    second_ref, first_ref, height_ref, transport_ref, level_ref, diff_ref, flux_ref, rim_ref, rows_ref, inv_rows_ref,
     x_ref, unit_ref, t_out, height_out, transport_out, north_ref, shift, fixed, result, sems,
 ):
     top = is_top()
@@ -600,25 +610,29 @@
     two = lax.ppermute(two, "lon", pairs[1])
     one = lax.ppermute(one, "lon", pairs[0])
 
-    solved, unit, inv_rows = pl.pallas_call(
-        tracer_kernel,
-        out_shape=(shape_of(2, depth, *block), shape_of(depth, *block), shape_of(2, depth, cols)),
+    net_x, speed_n, inv, gain, unit, inv_rows = pl.pallas_call(
+        faces_kernel,
+        out_shape=(
+            shape_of(2 * depth * rows, cols),
+            shape_of(depth, *block),
+            shape_of(depth, *block),
+            shape_of(depth, *block),
+            shape_of(depth, *block),
+            shape_of(2, depth, cols),
+        ),
         in_specs=vmem(7) + [pl.BlockSpec(memory_space=pltpu.HBM)],
-        out_specs=vmem(3),
+        out_specs=vmem(6),
         scratch_shapes=[
-            pltpu.VMEM((depth, *block), F32),
             pltpu.VMEM((2 * depth * rows, 2 * cols), jnp.bfloat16),
             pltpu.VMEM((2 * depth * rows, cols), F32),
-            pltpu.VMEM((2 * depth * rows, cols), F32),
-            pltpu.VMEM((depth, *block), F32),
             pltpu.SemaphoreType.DMA,
         ],
         compiler_params=params(),
-        cost_estimate=work(8),
-        name="tracers",
+        cost_estimate=work(4),
+        name="faces",
     )(two, one, t_0, ocean_levels, diffusivity, tracers, speed_e, in_hbm(velocity))
 
-    first, second, edge_flux, edge_rim, tab, side = pl.pallas_call(
+    second, first, edge_flux, edge_rim, tab, side = pl.pallas_call(
         rim_lookup_kernel,
         out_shape=(
             shape_of(lat_rows, cols),
@@ -628,7 +642,7 @@
             shape_of(4, n_lon // 2, 128),
             shape_of(3, n_lon, 128),
         ),
-        in_specs=vmem(10),
+        in_specs=vmem(10) + [pl.BlockSpec(memory_space=pl.ANY)],
         out_specs=vmem(6),
         scratch_shapes=[pltpu.VMEM((2, lat_rows, cols), F32)],
         compiler_params=params(),
@@ -636,10 +650,21 @@
         name="rim_lookup",
     )(
         table, two, one, pick_row, pick_lane, used, edge_rows, ocean_levels, surface_height, transport,
+        inv_rows,
     )
     pairs = lat_pairs(n_lat, n_lon)
+    second = lax.ppermute(second, ("lat", "lon"), pairs[1])
     first = lax.ppermute(first, ("lat", "lon"), pairs[0])
-    second = lax.ppermute(second, ("lat", "lon"), pairs[1])
+
+    solved = pl.pallas_call(
+        solve_kernel,
+        out_shape=shape_of(2, depth, *block),
+        in_specs=vmem(7),
+        out_specs=vmem(1)[0],
+        compiler_params=params(),
+        cost_estimate=work(4),
+        name="solve",
+    )(net_x, ocean_levels, diffusivity, tracers, speed_n, inv, gain)
 
     flux, rim = pl.pallas_call(
         lookup_kernel,
@@ -666,7 +691,7 @@
         compiler_params=params(),
         name="step",
     )(
-        first, second, surface_height, transport, ocean_levels, diffusivity, flux, rim, edge_rows, inv_rows,
+        second, first, surface_height, transport, ocean_levels, diffusivity, flux, rim, edge_rows, inv_rows,
         solved, unit,
     )
 

time: 51.6 us -> 55.1 us (1.068)
  local copies, waits for them, and re-layouts: 0.04 us -> 3.93 us
  waiting for transfers between devices: 4.51 us -> 3.52 us
    unnamed x16 -> x34, local copies, waits for them, and re-layouts: 0.04 us -> 3.93 us
    ppermute x1, waiting for transfers between devices: 2.39 us -> 0.09 us  [per_device(): second = lax.ppermute(second, ('lat', 'lon'), pairs[1])]
    ppermute x1, waiting for transfers between devices: 0.01 us -> 2.27 us  [per_device(): first = lax.ppermute(first, ('lat', 'lon'), pairs[0])]
    ppermute x1, starting transfers between devices: 7.14 us -> 8.19 us  [per_device(): second = lax.ppermute(second, ('lat', 'lon'), pairs[1])]
    all_to_all x1, waiting for transfers between devices: 0.95 us -> 0.01 us  [per_device(): lax.all_to_all(picked, 'lon', split_axis=0, concat_axis=0, tiled=True)]
    ppermute x1, starting transfers between devices: 2.65 us -> 1.92 us  [per_device(): first = lax.ppermute(first, ('lat', 'lon'), pairs[0])]
    pallas_call x1 -> x2, Pallas kernels: 1.65 us -> 2.03 us  [the longest x1 1.56 us: per_device(): pl.pallas_call(faces_kernel, out_shape=(shape_of(2 * depth * rows, cols),...]
where the time goes in v7:
time: 55.1 us; the launch traced here: 54.5 us
  starting transfers between devices  37 us (67%)
  Pallas kernels  9.19 us (17%)
  local copies, waits for them, and re-layouts  3.93 us (7%)
  waiting for transfers between devices  3.52 us (6%)
  between operations  0.89 us (2%)
    all_to_all x1, starting transfers between devices, per_device(): lax.all_to_all(picked, 'lon', split_axis=0, concat_axis=0, tiled=True)  15.4 us
    ppermute x1, starting transfers between devices, per_device(): two = lax.ppermute(two, 'lon', pairs[1])  9.54 us
    ppermute x1, starting transfers between devices, per_device(): second = lax.ppermute(second, ('lat', 'lon'), pairs[1])  8.19 us
    unnamed x34, local copies, waits for them, and re-layouts  3.93 us
    ppermute x1, waiting for transfers between devices, per_device(): first = lax.ppermute(first, ('lat', 'lon'), pairs[0])  2.27 us
    ppermute x1, starting transfers between devices, per_device(): one = lax.ppermute(one, 'lon', pairs[0])  1.92 us
    ppermute x1, starting transfers between devices, per_device(): first = lax.ppermute(first, ('lat', 'lon'), pairs[0])  1.92 us
    pallas_call x1, Pallas kernels, per_device(): pl.pallas_call(step_kernel, out_shape=(shape_of(2, depth, rows, cols), sh...  1.81 us
  transfers between devices with their start and end apart: 5, of which 3 were waited for; matrix products, arithmetic and copies ran while one was open for 0% of the time, Pallas kernels for 9%

profile of v7, /device:TPU:120, one launch (start us, length us, event | category | flops | bytes accessed | tf_op | source)
XLA Modules:
  0.0 54.5 jit_solution(2796687244933292846)
XLA Ops:
  0.6 0.0 copy-start.14
  0.6 0.0 copy-start.15
  0.7 1.8 %pick.1.picked_ref = f32[32,1,640]{2,1,0:T(1,128)} custom-call(f32[1,4,512]{2,1,0:T(4,128)} %atm_hbm.1, s32[1,1,32,64]{3,2,1,0:T(8,128)} %rows_hbm.1), custom_call_target="tpu_custom_call" | custom-call | flops 40000000 | bytes 40000000 | tf_op jit(solution)/shard_map/pick/pallas_call | solution.py:568
  2.4 0.0 copy-start
  2.4 0.0 copy-start.1
  2.4 0.0 copy-start.7
  2.5 0.0 copy-start.13
  2.5 0.0 copy-start.16
  2.5 15.4 %all-to-all-start = ((f32[32,1,640]{2,1,0:T(1,128)}), f32[32,1,640]{2,1,0:T(1,128)S(1)}, u32[]{:S(2)}, u32[]{:S(2)}) async-start(f32[32,1,640]{2,1,0:T(1,128)} %pick.1.picked_ref), calls=%async_computation | async-start | bytes 163840 | tf_op jit(solution)/shard_map/all_to_all | solution.py:582
  17.9 0.0 copy-start.5
  18.0 1.7 %edges.1 = (f32[64,128]{1,0:T(8,128)S(1)}, f32[64,128]{1,0:T(8,128)S(1)}, f32[32,128]{1,0:T(8,128)S(1)}, f32[2,72,128]{2,1,0:T(8,128)S(1)}, s32[4,32,128]{2,1,0:...) custom-call(f32[32,1,640]{2,1,0:T(1,128)} %pick.1.picked_ref, ...), custom_call_target="tpu_custom_call" | custom-call | flops 2000000 | bytes 2000000 | tf_op jit(solution)/shard_map/edges/pallas_call | solution.py:586
  19.7 0.6 %copy-done.2 = f32[4,32,128]{2,1,0:T(8,128)} copy-done((f32[4,32,128]{2,1,0:T(8,128)}, f32[4,32,128]{2,1,0:T(8,128)S(1)}, u32[]{:S(2)}) %copy-start.2) | copy-done | bytes 65560
  20.3 9.5 %collective-permute-start = (f32[64,128]{1,0:T(8,128)S(1)}, f32[64,128]{1,0:T(8,128)S(1)}, u32[]{:S(2)}, u32[]{:S(2)}) collective-permute-start(f32[64,128]{1,0:T(8,128)S(1)} %get-tuple-element.26), channel_id=1, source_target_pairs={{1,2},{2,1},{3,4},{4,3},{5,6},{6,5},{7,8},{8,7},{9,10},{10,9},{11,... | collective-permute-start | bytes 98312 | tf_op jit(solution)/shard_map/ppermute | solution.py:610
  29.8 1.9 %collective-permute-start.1 = (f32[64,128]{1,0:T(8,128)S(1)}, f32[64,128]{1,0:T(8,128)S(1)}, u32[]{:S(2)}, u32[]{:S(2)}) collective-permute-start(f32[64,128]{1,0:T(8,128)S(1)} %get-tuple-element.27), channel_id=1, source_target_pairs={{0,1},{1,0},{2,3},{3,2},{4,5},{5,4},{6,7},{7,6},{8,9},{9,8},{10,11... | collective-permute-start | bytes 98312 | tf_op jit(solution)/shard_map/ppermute | solution.py:611
  31.8 0.0 collective-permute-done.two_ref
  31.8 1.2 %collective-permute-done.1.one_ref = f32[64,128]{1,0:T(8,128)S(1)} collective-permute-done((f32[64,128]{1,0:T(8,128)S(1)}, f32[64,128]{1,0:T(8,128)S(1)}, u32[]{:S(2)}, u32[]{:S(2)}) %collective-permute-start.1) | collective-permute-done | bytes 32800 | tf_op jit(solution)/shard_map/ppermute | solution.py:611
  32.9 1.6 %faces.1 = (f32[1536,128]{1,0:T(8,128)S(1)}, f32[24,32,128]{2,1,0:T(8,128)S(1)}, f32[24,32,128]{2,1,0:T(8,128)S(1)}, f32[24,32,128]{2,1,0:T(8,128)S(1)}, f32[24,...) custom-call(f32[64,128]{1,0:T(8,128)S(1)} %collective-permute-done.two_ref, f32[64,128]{1,0:T(8,128)S(1)} %collective-permute-done.1.one_ref, ...), custom_call_target="tpu_custom_call" | custom-call | flops 4000000 | bytes 4000000 | tf_op jit(solution)/shard_map/faces/pallas_call | solution.py:613
  34.5 0.0 copy-start.10
  34.5 0.6 %copy-done.10 = f32[2,24,128]{2,1,0:T(8,128)} copy-done((f32[2,24,128]{2,1,0:T(8,128)}, f32[2,24,128]{2,1,0:T(8,128)S(1)}, u32[]{:S(2)}) %copy-start.10) | copy-done | bytes 24600
  35.1 0.0 all-to-all-done.table_ref
  35.1 0.8 %copy-done.3 = f32[4,32,128]{2,1,0:T(8,128)S(1)} copy-done((f32[4,32,128]{2,1,0:T(8,128)S(1)}, f32[4,32,128]{2,1,0:T(8,128)}, u32[]{:S(2)}) %copy-start.3) | copy-done | bytes 65560
  36.0 0.7 %copy-done.8 = f32[32,128]{1,0:T(8,128)S(1)} copy-done((f32[32,128]{1,0:T(8,128)S(1)}, f32[32,128]{1,0:T(8,128)}, u32[]{:S(2)}) %copy-start.8) | copy-done | bytes 16408
  36.7 0.7 %copy-done.11 = f32[2,24,128]{2,1,0:T(8,128)S(1)} copy-done((f32[2,24,128]{2,1,0:T(8,128)S(1)}, f32[2,24,128]{2,1,0:T(8,128)}, u32[]{:S(2)}) %copy-start.11) | copy-done | bytes 24600
  37.4 0.9 %rim_lookup.1 = (f32[136,128]{1,0:T(8,128)S(1)}, f32[136,128]{1,0:T(8,128)S(1)}, f32[2,3,8,128]{3,2,1,0:T(8,128)S(1)}, f32[2,3,8,128]{3,2,1,0:T(8,128)S(1)}, f32...) custom-call(f32[32,1,640]{2,1,0:T(1,128)S(1)} %all-to-all-done.table_ref, f32[64,128]{1,0:T(8,128)S(1)} %collective-permute-done.two_ref, ...), custom_call_target="tpu_custom_call" | custom-call | flops 8000000 | bytes 8000000 | tf_op jit(solution)/shard_map/rim_lookup/pallas_call | solution.py:635
  38.3 8.2 %collective-permute-start.2 = (f32[136,128]{1,0:T(8,128)S(1)}, f32[136,128]{1,0:T(8,128)S(1)}, u32[]{:S(2)}, u32[]{:S(2)}) collective-permute-start(f32[136,128]{1,0:T(8,128)S(1)} %get-tuple-element.36), channel_id=1, source_target_pairs={{32,64},{64,32},{96,128},{128,96},{160,192},{192,160},{224,256},{2... | collective-permute-start | bytes 208904 | tf_op jit(solution)/shard_map/ppermute | solution.py:656
  46.5 1.9 %collective-permute-start.3 = (f32[136,128]{1,0:T(8,128)S(1)}, f32[136,128]{1,0:T(8,128)S(1)}, u32[]{:S(2)}, u32[]{:S(2)}) collective-permute-start(f32[136,128]{1,0:T(8,128)S(1)} %get-tuple-element.37), channel_id=1, source_target_pairs={{0,32},{32,0},{64,96},{96,64},{128,160},{160,128},{192,224},{224,1... | collective-permute-start | bytes 208904 | tf_op jit(solution)/shard_map/ppermute | solution.py:657
  48.4 0.5 solve.1.x_ref
  48.9 0.4 copy-done.4
  49.3 1.1 %lookup.1 = (f32[4,32,128]{2,1,0:T(8,128)S(1)}, f32[7,32,128]{2,1,0:T(8,128)S(1)}) custom-call(f32[2,3,8,128]{3,2,1,0:T(8,128)S(1)} %get-tuple-element.38.edge_flux_ref, f32[2,3,8,128]{3,2,1,0:T(8,128)S(1)} %get-tuple-element.39.edge_rim_ref, f32[4,16,128]{2,1,0:T(8,128)S(1)} %get-tuple-element.40.tab, f32[3,32,128]{2,1,0:T(8,128)S(1)} %get-tuple-element.41.side, ...), custom_call_target="tpu_custom_call" | custom-call | flops 8000000 | bytes 8000000 | tf_op jit(solution)/shard_map/lookup/pallas_call | solution.py:669
  50.3 0.1 collective-permute-done.2.second_ref
  50.4 2.3 %collective-permute-done.3.first_ref = f32[136,128]{1,0:T(8,128)S(1)} collective-permute-done((f32[136,128]{1,0:T(8,128)S(1)}, f32[136,128]{1,0:T(8,128)S(1)}, u32[]{:S(2)}, u32[]{:S(2)}) %collective-permute-start.3) | collective-permute-done | bytes 69664 | tf_op jit(solution)/shard_map/ppermute | solution.py:657
  52.7 1.8 %step.1 = (f32[2,24,32,128]{3,2,1,0:T(8,128)}, f32[32,128]{1,0:T(8,128)}, f32[2,32,128]{2,1,0:T(8,128)}) custom-call(f32[136,128]{1,0:T(8,128)S(1)} %collective-permute-done.2.second_ref, f32[136,128]{1,0:T(8,128)S(1)} %collective-permute-done.3.first_ref, f32[32,128]{1,0:T(8,128)S(1)} %copy-done.9, f32[2,32,128]{2,1,0:T(8,128)S(1)} %copy-done.1, ...), custom_call_target="tpu_custom_call" | custom-call | tf_op jit(solution)/shard_map/step/pallas_call | solution.py:679
  (19 shorter events, 0.0 us)
Async XLA Ops:
  0.6 17.2 %copy-start.14 = (s32[4,32,128]{2,1,0:T(8,128)S(1)}, s32[4,32,128]{2,1,0:T(8,128)}, u32[]{:S(2)}) copy-start(s32[4,32,128]{2,1,0:T(8,128)} %slot_ref.1) | copy-start | bytes 196612
  0.6 17.2 %copy-start.15 = (f32[4,32,128]{2,1,0:T(8,128)S(1)}, f32[4,32,128]{2,1,0:T(8,128)}, u32[]{:S(2)}) copy-start(f32[4,32,128]{2,1,0:T(8,128)} %weight_ref.1) | copy-start | bytes 196612
  2.4 15.5 %copy-start = (s32[32,128]{1,0:T(8,128)S(1)}, s32[32,128]{1,0:T(8,128)}, u32[]{:S(2)}) copy-start(s32[32,128]{1,0:T(8,128)} %level_ref.9) | copy-start | bytes 49156
  2.4 15.5 %copy-start.1 = (f32[2,32,128]{2,1,0:T(8,128)S(1)}, f32[2,32,128]{2,1,0:T(8,128)}, u32[]{:S(2)}) copy-start(f32[2,32,128]{2,1,0:T(8,128)} %transport_ref.5) | copy-start | bytes 98308
  2.4 15.5 %copy-start.7 = (f32[32,128]{1,0:T(8,128)S(1)}, f32[32,128]{1,0:T(8,128)}, u32[]{:S(2)}) copy-start(f32[32,128]{1,0:T(8,128)} %height_ref.5) | copy-start | bytes 49156
  2.5 15.5 %copy-start.13 = (s32[4,32,128]{2,1,0:T(8,128)S(1)}, s32[4,32,128]{2,1,0:T(8,128)}, u32[]{:S(2)}) copy-start(s32[4,32,128]{2,1,0:T(8,128)} %owner_ref.1) | copy-start | bytes 196612
  2.5 15.5 %copy-start.16 = (s32[32,128]{1,0:T(8,128)S(1)}, s32[32,128]{1,0:T(8,128)}, u32[]{:S(2)}) copy-start(s32[32,128]{1,0:T(8,128)} %count_ref.1) | copy-start | bytes 49156
  2.5 32.6 %all-to-all-start = ((f32[32,1,640]{2,1,0:T(1,128)}), f32[32,1,640]{2,1,0:T(1,128)S(1)}, u32[]{:S(2)}, u32[]{:S(2)}) async-start(f32[32,1,640]{2,1,0:T(1,128)} %pick.1.picked_ref), calls=%async_computation | async-start | bytes 163840 | tf_op jit(solution)/shard_map/all_to_all | solution.py:582
  17.9 15.0 %copy-start.5 = (f32[32,128]{1,0:T(8,128)S(1)}, f32[32,128]{1,0:T(8,128)}, u32[]{:S(2)}) copy-start(f32[32,128]{1,0:T(8,128)} %diff_ref.5) | copy-start | bytes 49156
  19.7 0.6 %copy-start.2 = (f32[4,32,128]{2,1,0:T(8,128)}, f32[4,32,128]{2,1,0:T(8,128)S(1)}, u32[]{:S(2)}) copy-start(f32[4,32,128]{2,1,0:T(8,128)S(1)} %get-tuple-element.30.used_ref) | copy-start | bytes 196612
  20.3 11.5 %collective-permute-start = (f32[64,128]{1,0:T(8,128)S(1)}, f32[64,128]{1,0:T(8,128)S(1)}, u32[]{:S(2)}, u32[]{:S(2)}) collective-permute-start(f32[64,128]{1,0:T(8,128)S(1)} %get-tuple-element.26), channel_id=1, source_target_pairs={{1,2},{2,1},{3,4},{4,3},{5,6},{6,5},{7,8},{8,7},{9,10},{10,9},{11,... | collective-permute-start | bytes 98312 | tf_op jit(solution)/shard_map/ppermute | solution.py:610
  29.8 3.1 %collective-permute-start.1 = (f32[64,128]{1,0:T(8,128)S(1)}, f32[64,128]{1,0:T(8,128)S(1)}, u32[]{:S(2)}, u32[]{:S(2)}) collective-permute-start(f32[64,128]{1,0:T(8,128)S(1)} %get-tuple-element.27), channel_id=1, source_target_pairs={{0,1},{1,0},{2,3},{3,2},{4,5},{5,4},{6,7},{7,6},{8,9},{9,8},{10,11... | collective-permute-start | bytes 98312 | tf_op jit(solution)/shard_map/ppermute | solution.py:611
  34.5 0.6 %copy-start.10 = (f32[2,24,128]{2,1,0:T(8,128)}, f32[2,24,128]{2,1,0:T(8,128)S(1)}, u32[]{:S(2)}) copy-start(f32[2,24,128]{2,1,0:T(8,128)S(1)} %get-tuple-element.35.after_ref.inv_rows_ref) | copy-start | bytes 73732
  35.1 0.8 %copy-start.3 = (f32[4,32,128]{2,1,0:T(8,128)S(1)}, f32[4,32,128]{2,1,0:T(8,128)}, u32[]{:S(2)}) copy-start(f32[4,32,128]{2,1,0:T(8,128)} %copy-done.2) | copy-start | bytes 196612
  36.0 0.7 %copy-start.8 = (f32[32,128]{1,0:T(8,128)S(1)}, f32[32,128]{1,0:T(8,128)}, u32[]{:S(2)}) copy-start(f32[32,128]{1,0:T(8,128)} %height_ref.5) | copy-start | bytes 49156
  36.7 0.7 %copy-start.11 = (f32[2,24,128]{2,1,0:T(8,128)S(1)}, f32[2,24,128]{2,1,0:T(8,128)}, u32[]{:S(2)}) copy-start(f32[2,24,128]{2,1,0:T(8,128)} %copy-done.10) | copy-start | bytes 73732
  37.4 11.0 %copy-start.6 = (f32[32,128]{1,0:T(8,128)S(1)}, f32[32,128]{1,0:T(8,128)}, u32[]{:S(2)}) copy-start(f32[32,128]{1,0:T(8,128)} %diff_ref.5) | copy-start | bytes 49156
  38.3 12.1 %collective-permute-start.2 = (f32[136,128]{1,0:T(8,128)S(1)}, f32[136,128]{1,0:T(8,128)S(1)}, u32[]{:S(2)}, u32[]{:S(2)}) collective-permute-start(f32[136,128]{1,0:T(8,128)S(1)} %get-tuple-element.36), channel_id=1, source_target_pairs={{32,64},{64,32},{96,128},{128,96},{160,192},{192,160},{224,256},{2... | collective-permute-start | bytes 208904 | tf_op jit(solution)/shard_map/ppermute | solution.py:656
  46.5 6.2 %collective-permute-start.3 = (f32[136,128]{1,0:T(8,128)S(1)}, f32[136,128]{1,0:T(8,128)S(1)}, u32[]{:S(2)}, u32[]{:S(2)}) collective-permute-start(f32[136,128]{1,0:T(8,128)S(1)} %get-tuple-element.37), channel_id=1, source_target_pairs={{0,32},{32,0},{64,96},{96,64},{128,160},{160,128},{192,224},{224,1... | collective-permute-start | bytes 208904 | tf_op jit(solution)/shard_map/ppermute | solution.py:657
  48.4 0.8 %copy-start.4 = (f32[4,32,128]{2,1,0:T(8,128)S(1)}, f32[4,32,128]{2,1,0:T(8,128)}, u32[]{:S(2)}) copy-start(f32[4,32,128]{2,1,0:T(8,128)} %copy-done.2) | copy-start | bytes 196612
  49.3 3.4 %copy-start.9 = (f32[32,128]{1,0:T(8,128)S(1)}, f32[32,128]{1,0:T(8,128)}, u32[]{:S(2)}) copy-start(f32[32,128]{1,0:T(8,128)} %height_ref.5) | copy-start | bytes 49156
  49.3 3.4 %copy-start.12 = (f32[2,24,128]{2,1,0:T(8,128)S(1)}, f32[2,24,128]{2,1,0:T(8,128)}, u32[]{:S(2)}) copy-start(f32[2,24,128]{2,1,0:T(8,128)} %copy-done.10) | copy-start | bytes 73732

commit v8 on v5

--- a/solution.py
+++ b/solution.py
@@ -47,14 +47,18 @@
     return lax.axis_index("lat") == lax.axis_size("lat") - 1
 
 
-def pick_kernel(atm_hbm, rows_hbm, out_ref, atm_ref, rows_ref, sems):
+def pick_kernel(
+    atm_hbm, rows_hbm, t_hbm, v_hbm, out_ref, t_ref, u_ref, atm_ref, rows_ref, sems,
+):
     copies = [
         pltpu.make_async_copy(atm_hbm, atm_ref, sems.at[0]),
         pltpu.make_async_copy(rows_hbm, rows_ref, sems.at[1]),
+        pltpu.make_async_copy(t_hbm, t_ref, sems.at[2]),
+        pltpu.make_async_copy(v_hbm.at[0], u_ref, sems.at[3]),
     ]
     for copy in copies:
         copy.start()
-    for copy in copies:
+    for copy in copies[:2]:
         copy.wait()
     rows = rows_ref[0, 0]
     both = jnp.concatenate([rows, rows], axis=1)
@@ -74,21 +78,17 @@
     for f in range(1, 4):
         at = 128 + f * 128
         out_ref[:, 0, at : at + 128] = jnp.where(low, turn(values[f], -1, 0), turn(values[f], 1, 0))
+    for copy in copies[2:]:
+        copy.wait()
 
 
 def edge_kernel(
-    picked_ref, t_hbm, v_hbm, level_ref, height_ref, transport_ref, owner_ref, slot_ref, weight_ref, count_ref,
-    two_ref, one_ref, t_0_ref, rows_ref, pick_row_ref, pick_lane_ref, used_ref, t_ref, u_ref, v_rows, sems,
+    picked_ref, v_hbm, t_ref, u_ref, level_ref, height_ref, transport_ref, owner_ref, slot_ref, weight_ref, count_ref,
+    two_ref, one_ref, t_0_ref, rows_ref, pick_row_ref, pick_lane_ref, used_ref, v_rows, sem,
 ):
     depth, rows, cols = t_ref.shape[1:]
-    copies = [
-        pltpu.make_async_copy(t_hbm.at[0], t_ref.at[0], sems.at[0]),
-        pltpu.make_async_copy(v_hbm.at[0], u_ref, sems.at[1]),
-        pltpu.make_async_copy(t_hbm.at[1], t_ref.at[1], sems.at[2]),
-        pltpu.make_async_copy(v_hbm.at[1, :, rows - HALO : rows], v_rows, sems.at[3]),
-    ]
-    for copy in copies:
-        copy.start()
+    copy = pltpu.make_async_copy(v_hbm.at[1, :, rows - HALO : rows], v_rows, sem)
+    copy.start()
     shape = (rows, cols)
     lane = lanes(shape)
     level = level_ref[...]
@@ -113,13 +113,11 @@
     west_t = jnp.zeros(shape, F32)
     east_t = jnp.zeros(shape, F32)
     for c in range(2):
-        copies[2 * c].wait()
         for l in range(depth):
             f = c * depth + l
             moved = turn(t_ref[c, l], f + 1, 1)
             west_t = jnp.where(lane == f + 1, moved, west_t)
             east_t = jnp.where(lane == f, moved, east_t)
-    copies[1].wait()
     for l in range(depth):
         at = 2 * depth + l
         east_t = jnp.where(lane == at, turn(u_ref[l], at + 1, 1), east_t)
@@ -134,7 +132,7 @@
             at = c * depth + l
             rows_ref[0, at : at + 1] = t_ref[c, l, rows - 1 : rows]
             rows_ref[1, at : at + 1] = t_ref[c, l, 0:1]
-    copies[3].wait()
+    copy.wait()
     for l in range(depth):
         at = 2 * depth + l
         rows_ref[0, at : at + 1] = v_rows[l, HALO - 1 : HALO]
@@ -207,7 +205,7 @@
 
 def rim_lookup_kernel(
     table_ref, two_ref, one_ref, pick_row_ref, pick_lane_ref, used_ref, rows_ref, level_ref, height_ref,
-    transport_ref, first_ref, second_ref, flux_ref, rim_ref, tab, side, pack,
+    transport_ref, second_ref, first_ref, flux_ref, rim_ref, tab, side, pack,
 ):
     n_lon = table_ref.shape[0]
     half = n_lon // 2
@@ -244,8 +242,8 @@
         pack[s, ROW_T:] = rows_ref[s]
     even = is_even("lat")
     north_going, south_going = pack[0], pack[1]
+    second_ref[...] = jnp.where(even, south_going, north_going)
     first_ref[...] = jnp.where(even, north_going, south_going)
-    second_ref[...] = jnp.where(even, south_going, north_going)
 
 
 def lookup_kernel(
@@ -280,7 +278,7 @@
 
 def tracer_kernel(
     two_ref, one_ref, t_0_ref, level_ref, diff_ref, t_ref, u_ref, v_hbm, x_ref, unit_ref, inv_rows_ref, gain_ref,
-    parts, rims, net_x, v_ref, sem,
+    parts, rims, net_x, v_ref, inv_ref, sem,
 ):
     depth, rows, cols = t_ref.shape[1:]
     copy = pltpu.make_async_copy(v_hbm.at[1], v_ref, sem)
@@ -327,45 +325,49 @@
             t_east = jnp.where(lane == last, rims[at], turn(t, -1, 1))
             flux_e = jnp.where(mask_e, u_l * (t + t_east), 0.0)
             net_x[at] = flux_e - jnp.where(lane == 0, rims[at], turn(flux_e, 1, 1))
-    copy.wait()
     diff = diff_ref[...]
     above = jnp.zeros(shape, F32)
-    inv = None
-    right = [None, None, None]
+    inv = unit = None
     for l in range(depth):
         below = jnp.where(level > l + 1, diff, 0.0) if l < depth - 1 else jnp.zeros(shape, F32)
         pivot = 1.0 + above + below
         if l > 0:
             pivot = pivot - above * above * inv
         inv = 1.0 / pivot
+        inv_ref[l] = inv
         inv_rows_ref[0, l : l + 1] = inv[rows - 1 : rows]
         inv_rows_ref[1, l : l + 1] = inv[0:1]
         gain_ref[l] = below * inv
+        unit = inv if l == 0 else above * unit * inv
+        unit_ref[l] = unit
+        above = below
+    for l in range(depth - 2, -1, -1):
+        unit = unit_ref[l] + gain_ref[l] * unit
+        unit_ref[l] = unit
+    copy.wait()
+    right = [None, None]
+    for l in range(depth):
+        above = jnp.where(level > l, diff, 0.0)
+        inv = inv_ref[l]
         mask_n = face_n > l
         v_l = v_ref[l] * 0.5
         for c in range(2):
             f = c * depth + l
-            at = slice(f * rows, (f + 1) * rows)
             t = t_ref[c, l]
             flux_n = jnp.where(mask_n, v_l * (t + turn(t, -1, 0)), 0.0)
             flux_s = turn(flux_n, 1, 0)
-            forced = t - adv_rate * (net_x[at] + (flux_n - flux_s))
+            forced = t - adv_rate * (net_x[f * rows : (f + 1) * rows] + (flux_n - flux_s))
             right[c] = forced * inv if l == 0 else (forced + above * right[c]) * inv
             x_ref[c, l] = right[c]
-        right[2] = inv if l == 0 else above * right[2] * inv
-        unit_ref[l] = right[2]
-        above = below
     for l in range(depth - 2, -1, -1):
         gain = gain_ref[l]
         for c in range(2):
             right[c] = x_ref[c, l] + gain * right[c]
             x_ref[c, l] = right[c]
-        right[2] = unit_ref[l] + gain * right[2]
-        unit_ref[l] = right[2]
 
 
 def step_kernel(
-    first_ref, second_ref, height_ref, transport_ref, level_ref, diff_ref, flux_ref, rim_ref, rows_ref, inv_rows_ref,
+    second_ref, first_ref, height_ref, transport_ref, level_ref, diff_ref, flux_ref, rim_ref, rows_ref, inv_rows_ref,
     x_ref, unit_ref, t_out, height_out, transport_out, north_ref, shift, fixed, result, sems,
 ):
     top = is_top()
@@ -428,16 +430,6 @@
             below = jnp.where(level_in > l + 1, diff_in, 0.0) * inv
             right[i] = shift[s, at : at + 1] + below * right[i]
             shift[s, at : at + 1] = right[i]
-    row = rows_of((HALO, cols))
-    for s, cut, at_row in ((0, hi, HALO - 1), (1, lo, 0)):
-        for c in range(2):
-            for l in range(depth):
-                at = c * depth + l
-                add = jnp.broadcast_to(shift[s, at : at + 1], (HALO, cols))
-                x = x_ref[c, l, cut] + unit_ref[l, cut] * source[c][cut]
-                fixed[c, l, cut] = x + jnp.where(row == at_row, add, 0.0)
-        send(fixed.at[:, :, cut], t_out.at[:, :, cut])
-
     own = (
         height_ref[...], transport_ref[0], transport_ref[1], level_f,
         flux_ref[1], flux_ref[2], flux_ref[3],
@@ -471,11 +463,21 @@
     p_wet, p_grad, p_fresh, p_wind_e, p_wind_n = coefficients(fold)
     h, e, n = mine[HEIGHT], mine[EAST], mine[NORTH]
     p_h, p_e, p_n = fold[HEIGHT], fold[EAST], fold[NORTH]
-    row = rows_of(h.shape)
+    row_h = rows_of(h.shape)
     last = HALO + rows - 1
-    across = (row == last) & top
+    across = (row_h == last) & top
     p_last = rows_of(p_h.shape) == HALO - 1
-    for _ in range(SUBSTEPS):
+    for step in range(SUBSTEPS):
+        if step == 4:
+            row = rows_of((HALO, cols))
+            for s, cut, at_row in ((0, hi, HALO - 1), (1, lo, 0)):
+                for c in range(2):
+                    for l in range(depth):
+                        at = c * depth + l
+                        add = jnp.broadcast_to(shift[s, at : at + 1], (HALO, cols))
+                        x = x_ref[c, l, cut] + unit_ref[l, cut] * source[c][cut]
+                        fixed[c, l, cut] = x + jnp.where(row == at_row, add, 0.0)
+                send(fixed.at[:, :, cut], t_out.at[:, :, cut])
         h = (h - wave_div * ((e - turn(e, 1, 1)) + (n - turn(n, 1, 0)))) * wet + fresh
         p_h = (p_h - wave_div * ((p_e - turn(p_e, -1, 1)) + (p_n - turn(p_n, 1, 0)))) * p_wet + p_fresh
         h_n = jnp.where(across, jnp.broadcast_to(p_h[HALO - 1 :], h.shape), turn(h, -1, 0))
@@ -555,25 +557,29 @@
     n_lat, n_lon = lax.axis_size("lat"), lax.axis_size("lon")
     depth, rows, cols = tracers.shape[1:]
     slots = send_rows.shape[3]
-    picked = pl.pallas_call(
+    block = (rows, cols)
+    picked, t_near, u_near = pl.pallas_call(
         pick_kernel,
-        out_shape=pltpu.VMEM((n_lon, 1, 10 * slots), F32),
-        in_specs=[pl.BlockSpec(memory_space=pltpu.HBM)] * 2,
-        out_specs=vmem(1)[0],
+        out_shape=(
+            shape_of(n_lon, 1, 10 * slots),
+            shape_of(2, depth, *block),
+            shape_of(depth, *block),
+        ),
+        in_specs=[pl.BlockSpec(memory_space=pltpu.HBM)] * 4,
+        out_specs=vmem(3),
         scratch_shapes=[
             pltpu.VMEM(atm_flux.shape, F32),
             pltpu.VMEM(send_rows.shape, jnp.int32),
-            pltpu.SemaphoreType.DMA((2,)),
+            pltpu.SemaphoreType.DMA((4,)),
         ],
         compiler_params=params(24),
         cost_estimate=work(40),
         name="pick",
-    )(in_hbm(atm_flux), in_hbm(send_rows))
+    )(in_hbm(atm_flux), in_hbm(send_rows), in_hbm(tracers), in_hbm(velocity))
     table = lax.all_to_all(picked, "lon", split_axis=0, concat_axis=0, tiled=True)
 
-    block = (rows, cols)
     lat_rows = ROW_T + 3 * depth
-    two, one, t_0, edge_rows, pick_row, pick_lane, used, tracers, speed_e = pl.pallas_call(
+    two, one, t_0, edge_rows, pick_row, pick_lane, used = pl.pallas_call(
         edge_kernel,
         out_shape=(
             shape_of(2 * rows, cols),
@@ -583,17 +589,15 @@
             jax.ShapeDtypeStruct((4, *block), jnp.int32),
             jax.ShapeDtypeStruct((4, *block), jnp.int32),
             shape_of(4, *block),
-            shape_of(2, depth, *block),
-            shape_of(depth, *block),
         ),
-        in_specs=[pl.BlockSpec(memory_space=pl.ANY)] + [pl.BlockSpec(memory_space=pltpu.HBM)] * 2 + vmem(7),
-        out_specs=vmem(9),
-        scratch_shapes=[pltpu.VMEM((depth, HALO, cols), F32), pltpu.SemaphoreType.DMA((4,))],
+        in_specs=[pl.BlockSpec(memory_space=pl.ANY), pl.BlockSpec(memory_space=pltpu.HBM)] + vmem(9),
+        out_specs=vmem(7),
+        scratch_shapes=[pltpu.VMEM((depth, HALO, cols), F32), pltpu.SemaphoreType.DMA],
         compiler_params=params(),
         cost_estimate=work(2),
         name="edges",
     )(
-        picked, in_hbm(tracers), in_hbm(velocity), ocean_levels, surface_height, transport, src_owner, src_slot,
+        picked, in_hbm(velocity), t_near, u_near, ocean_levels, surface_height, transport, src_owner, src_slot,
         xgrid_weights, xgrid_count,
     )
     pairs = lon_pairs(n_lon)
@@ -611,14 +615,15 @@
             pltpu.VMEM((2 * depth * rows, cols), F32),
             pltpu.VMEM((2 * depth * rows, cols), F32),
             pltpu.VMEM((depth, *block), F32),
+            pltpu.VMEM((depth, *block), F32),
             pltpu.SemaphoreType.DMA,
         ],
         compiler_params=params(),
         cost_estimate=work(8),
         name="tracers",
-    )(two, one, t_0, ocean_levels, diffusivity, tracers, speed_e, in_hbm(velocity))
-
-    first, second, edge_flux, edge_rim, tab, side = pl.pallas_call(
+    )(two, one, t_0, ocean_levels, diffusivity, t_near, u_near, in_hbm(velocity))
+
+    second, first, edge_flux, edge_rim, tab, side = pl.pallas_call(
         rim_lookup_kernel,
         out_shape=(
             shape_of(lat_rows, cols),
@@ -638,8 +643,8 @@
         table, two, one, pick_row, pick_lane, used, edge_rows, ocean_levels, surface_height, transport,
     )
     pairs = lat_pairs(n_lat, n_lon)
+    second = lax.ppermute(second, ("lat", "lon"), pairs[1])
     first = lax.ppermute(first, ("lat", "lon"), pairs[0])
-    second = lax.ppermute(second, ("lat", "lon"), pairs[1])
 
     flux, rim = pl.pallas_call(
         lookup_kernel,
@@ -666,7 +671,7 @@
         compiler_params=params(),
         name="step",
     )(
-        first, second, surface_height, transport, ocean_levels, diffusivity, flux, rim, edge_rows, inv_rows,
+        second, first, surface_height, transport, ocean_levels, diffusivity, flux, rim, edge_rows, inv_rows,
         solved, unit,
     )
 

time: 51.6 us -> 50.3 us (0.975)
  the two profiles are of different devices: /device:TPU:120 before, /device:TPU:64 now
where the time goes in v8:
time: 50.3 us; the launch traced here: 49.9 us
  starting transfers between devices  34.8 us (69%)
  Pallas kernels  9.06 us (18%)
  waiting for transfers between devices  5.13 us (10%)
  between operations  0.85 us (2%)
    all_to_all x1, starting transfers between devices, per_device(): lax.all_to_all(picked, 'lon', split_axis=0, concat_axis=0, tiled=True)  16.3 us
    ppermute x1, starting transfers between devices, per_device(): two = lax.ppermute(two, 'lon', pairs[1])  9.55 us
    ppermute x1, starting transfers between devices, per_device(): second = lax.ppermute(second, ('lat', 'lon'), pairs[1])  5.16 us
    all_to_all x1, waiting for transfers between devices, per_device(): lax.all_to_all(picked, 'lon', split_axis=0, concat_axis=0, tiled=True)  2.77 us
    pallas_call x1, Pallas kernels, per_device(): pl.pallas_call(tracer_kernel, out_shape=(shape_of(2, depth, *block), shap...  1.99 us
    pallas_call x1, Pallas kernels, per_device(): pl.pallas_call(pick_kernel, out_shape=(shape_of(n_lon, 1, 10 * slots), sh...  1.97 us
    ppermute x1, starting transfers between devices, per_device(): first = lax.ppermute(first, ('lat', 'lon'), pairs[0])  1.92 us
    ppermute x1, starting transfers between devices, per_device(): one = lax.ppermute(one, 'lon', pairs[0])  1.92 us
  transfers between devices with their start and end apart: 5, of which 3 were waited for; matrix products, arithmetic and copies ran while one was open for 0% of the time, Pallas kernels for 9%

profile of v8, /device:TPU:64, one launch (start us, length us, event | category | flops | bytes accessed | tf_op | source)
XLA Modules:
  0.0 49.9 jit_solution(9158627345151726452)
XLA Ops:
  0.6 0.0 copy-start.5
  0.6 0.0 copy-start.6
  0.7 2.0 %pick.1 = (f32[32,1,640]{2,1,0:T(1,128)}, f32[2,24,32,128]{3,2,1,0:T(8,128)S(1)}, f32[24,32,128]{2,1,0:T(8,128)S(1)}) custom-call(f32[1,4,512]{2,1,0:T(4,128)} %atm_hbm.1, s32[1,1,32,64]{3,2,1,0:T(8,128)} %rows_hbm.1, f32[2,24,32,128]{3,2,1,0:T(8,128)} %t_hbm.1, f32[2,24,32,128]{3,2,1,0:T(8,128)} %v_hbm.5), custom_call_target="tpu_custom_call" | custom-call | flops 40000000 | bytes 40000000 | tf_op jit(solution)/shard_map/pick/pallas_call | solution.py:561
  2.6 0.0 copy-start
  2.6 0.0 copy-start.1
  2.7 0.0 copy-start.2
  2.7 0.0 copy-start.4
  2.7 0.0 copy-start.7
  2.7 16.3 %all-to-all-start = ((f32[32,1,640]{2,1,0:T(1,128)}), f32[32,1,640]{2,1,0:T(1,128)S(1)}, u32[]{:S(2)}, u32[]{:S(2)}) async-start(f32[32,1,640]{2,1,0:T(1,128)} %get-tuple-element.24.picked_ref), calls=%async_computation | async-start | bytes 163840 | tf_op jit(solution)/shard_map/all_to_all | solution.py:579
  19.0 0.0 copy-done.5
  19.0 0.0 copy-done.6
  19.0 0.0 copy-done
  19.0 0.0 copy-done.1
  19.0 0.0 copy-done.2
  19.0 0.0 copy-done.4
  19.0 0.0 copy-done.7
  19.1 1.4 %edges.1 = (f32[64,128]{1,0:T(8,128)S(1)}, f32[64,128]{1,0:T(8,128)S(1)}, f32[32,128]{1,0:T(8,128)S(1)}, f32[2,72,128]{2,1,0:T(8,128)S(1)}, s32[4,32,128]{2,1,0:...) custom-call(f32[32,1,640]{2,1,0:T(1,128)} %get-tuple-element.24.picked_ref, f32[2,24,32,128]{3,2,1,0:T(8,128)} %v_hbm.5, ...), custom_call_target="tpu_custom_call" | custom-call | flops 2000000 | bytes 2000000 | tf_op jit(solution)/shard_map/edges/pallas_call | solution.py:582
  20.4 9.6 %collective-permute-start = (f32[64,128]{1,0:T(8,128)S(1)}, f32[64,128]{1,0:T(8,128)S(1)}, u32[]{:S(2)}, u32[]{:S(2)}) collective-permute-start(f32[64,128]{1,0:T(8,128)S(1)} %get-tuple-element.27), channel_id=1, source_target_pairs={{1,2},{2,1},{3,4},{4,3},{5,6},{6,5},{7,8},{8,7},{9,10},{10,9},{11,... | collective-permute-start | bytes 98312 | tf_op jit(solution)/shard_map/ppermute | solution.py:604
  30.0 1.9 %collective-permute-start.1 = (f32[64,128]{1,0:T(8,128)S(1)}, f32[64,128]{1,0:T(8,128)S(1)}, u32[]{:S(2)}, u32[]{:S(2)}) collective-permute-start(f32[64,128]{1,0:T(8,128)S(1)} %get-tuple-element.28), channel_id=1, source_target_pairs={{0,1},{1,0},{2,3},{3,2},{4,5},{5,4},{6,7},{7,6},{8,9},{9,8},{10,11... | collective-permute-start | bytes 98312 | tf_op jit(solution)/shard_map/ppermute | solution.py:605
  31.9 0.0 collective-permute-done.two_ref
  31.9 1.2 %collective-permute-done.1.one_ref = f32[64,128]{1,0:T(8,128)S(1)} collective-permute-done((f32[64,128]{1,0:T(8,128)S(1)}, f32[64,128]{1,0:T(8,128)S(1)}, u32[]{:S(2)}, u32[]{:S(2)}) %collective-permute-start.1) | collective-permute-done | bytes 32800 | tf_op jit(solution)/shard_map/ppermute | solution.py:605
  33.1 2.8 %all-to-all-done.table_ref = f32[32,1,640]{2,1,0:T(1,128)S(1)} async-done(((f32[32,1,640]{2,1,0:T(1,128)}), f32[32,1,640]{2,1,0:T(1,128)S(1)}, u32[]{:S(2)}, u32[]{:S(2)}) %all-to-all-start) | async-done | bytes 81952 | tf_op jit(solution)/shard_map/all_to_all | solution.py:579
  35.9 0.0 copy-start.3
  35.9 0.9 %rim_lookup.1 = (f32[136,128]{1,0:T(8,128)S(1)}, f32[136,128]{1,0:T(8,128)S(1)}, f32[2,3,8,128]{3,2,1,0:T(8,128)S(1)}, f32[2,3,8,128]{3,2,1,0:T(8,128)S(1)}, f32...) custom-call(f32[32,1,640]{2,1,0:T(1,128)S(1)} %all-to-all-done.table_ref, f32[64,128]{1,0:T(8,128)S(1)} %collective-permute-done.two_ref, ...), custom_call_target="tpu_custom_call" | custom-call | flops 8000000 | bytes 8000000 | tf_op jit(solution)/shard_map/rim_lookup/pallas_call | solution.py:626
  36.7 5.2 %collective-permute-start.2 = (f32[136,128]{1,0:T(8,128)S(1)}, f32[136,128]{1,0:T(8,128)S(1)}, u32[]{:S(2)}, u32[]{:S(2)}) collective-permute-start(f32[136,128]{1,0:T(8,128)S(1)} %get-tuple-element.33), channel_id=1, source_target_pairs={{32,64},{64,32},{96,128},{128,96},{160,192},{192,160},{224,256},{2... | collective-permute-start | bytes 208904 | tf_op jit(solution)/shard_map/ppermute | solution.py:646
  41.9 1.9 %collective-permute-start.3 = (f32[136,128]{1,0:T(8,128)S(1)}, f32[136,128]{1,0:T(8,128)S(1)}, u32[]{:S(2)}, u32[]{:S(2)}) collective-permute-start(f32[136,128]{1,0:T(8,128)S(1)} %get-tuple-element.34), channel_id=1, source_target_pairs={{0,32},{32,0},{64,96},{96,64},{128,160},{160,128},{192,224},{224,1... | collective-permute-start | bytes 208904 | tf_op jit(solution)/shard_map/ppermute | solution.py:647
  43.8 0.0 copy-done.3
  43.8 2.0 %tracers.1 = (f32[2,24,32,128]{3,2,1,0:T(8,128)S(1)}, f32[24,32,128]{2,1,0:T(8,128)S(1)}, f32[2,24,128]{2,1,0:T(8,128)S(1)}) custom-call(f32[64,128]{1,0:T(8,128)S(1)} %collective-permute-done.two_ref, f32[64,128]{1,0:T(8,128)S(1)} %collective-permute-done.1.one_ref, f32[32,128]{1,0:T(8,128)S(1)} %get-tuple-element.41.t_0_ref, s32[32,128]{1,0:T(8,128)S(1)} %copy-done.1, ...), custom_call_target="tpu_custom_call" | custom-call | flops 8000000 | bytes 8000000 | tf_op jit(solution)/shard_map/tracers/pallas_call | solution.py:607
  45.8 1.1 %lookup.1 = (f32[4,32,128]{2,1,0:T(8,128)S(1)}, f32[7,32,128]{2,1,0:T(8,128)S(1)}) custom-call(f32[2,3,8,128]{3,2,1,0:T(8,128)S(1)} %get-tuple-element.35.edge_flux_ref, f32[2,3,8,128]{3,2,1,0:T(8,128)S(1)} %get-tuple-element.36.edge_rim_ref, f32[4,16,128]{2,1,0:T(8,128)S(1)} %get-tuple-element.37.tab, f32[3,32,128]{2,1,0:T(8,128)S(1)} %get-tuple-element.38.side, ...), custom_call_target="tpu_custom_call" | custom-call | flops 8000000 | bytes 8000000 | tf_op jit(solution)/shard_map/lookup/pallas_call | solution.py:649
  46.9 0.0 collective-permute-done.2.second_ref
  46.9 1.2 %collective-permute-done.3.first_ref = f32[136,128]{1,0:T(8,128)S(1)} collective-permute-done((f32[136,128]{1,0:T(8,128)S(1)}, f32[136,128]{1,0:T(8,128)S(1)}, u32[]{:S(2)}, u32[]{:S(2)}) %collective-permute-start.3) | collective-permute-done | bytes 69664 | tf_op jit(solution)/shard_map/ppermute | solution.py:647
  48.1 1.8 %step.1 = (f32[2,24,32,128]{3,2,1,0:T(8,128)}, f32[32,128]{1,0:T(8,128)}, f32[2,32,128]{2,1,0:T(8,128)}) custom-call(f32[136,128]{1,0:T(8,128)S(1)} %collective-permute-done.2.second_ref, f32[136,128]{1,0:T(8,128)S(1)} %collective-permute-done.3.first_ref, f32[32,128]{1,0:T(8,128)S(1)} %copy-done.2, f32[2,32,128]{2,1,0:T(8,128)S(1)} %copy-done, ...), custom_call_target="tpu_custom_call" | custom-call | tf_op jit(solution)/shard_map/step/pallas_call | solution.py:659
Async XLA Ops:
  0.6 18.4 %copy-start.5 = (s32[4,32,128]{2,1,0:T(8,128)S(1)}, s32[4,32,128]{2,1,0:T(8,128)}, u32[]{:S(2)}) copy-start(s32[4,32,128]{2,1,0:T(8,128)} %slot_ref.1) | copy-start | bytes 196612
  0.6 18.4 %copy-start.6 = (f32[4,32,128]{2,1,0:T(8,128)S(1)}, f32[4,32,128]{2,1,0:T(8,128)}, u32[]{:S(2)}) copy-start(f32[4,32,128]{2,1,0:T(8,128)} %weight_ref.1) | copy-start | bytes 196612
  2.6 16.4 %copy-start = (f32[2,32,128]{2,1,0:T(8,128)S(1)}, f32[2,32,128]{2,1,0:T(8,128)}, u32[]{:S(2)}) copy-start(f32[2,32,128]{2,1,0:T(8,128)} %transport_ref.5) | copy-start | bytes 98308
  2.6 16.4 %copy-start.1 = (s32[32,128]{1,0:T(8,128)S(1)}, s32[32,128]{1,0:T(8,128)}, u32[]{:S(2)}) copy-start(s32[32,128]{1,0:T(8,128)} %level_ref.7) | copy-start | bytes 49156
  2.7 16.4 %copy-start.2 = (f32[32,128]{1,0:T(8,128)S(1)}, f32[32,128]{1,0:T(8,128)}, u32[]{:S(2)}) copy-start(f32[32,128]{1,0:T(8,128)} %height_ref.5) | copy-start | bytes 49156
  2.7 16.4 %copy-start.4 = (s32[4,32,128]{2,1,0:T(8,128)S(1)}, s32[4,32,128]{2,1,0:T(8,128)}, u32[]{:S(2)}) copy-start(s32[4,32,128]{2,1,0:T(8,128)} %owner_ref.1) | copy-start | bytes 196612
  2.7 16.4 %copy-start.7 = (s32[32,128]{1,0:T(8,128)S(1)}, s32[32,128]{1,0:T(8,128)}, u32[]{:S(2)}) copy-start(s32[32,128]{1,0:T(8,128)} %count_ref.1) | copy-start | bytes 49156
  2.7 33.2 %all-to-all-start = ((f32[32,1,640]{2,1,0:T(1,128)}), f32[32,1,640]{2,1,0:T(1,128)S(1)}, u32[]{:S(2)}, u32[]{:S(2)}) async-start(f32[32,1,640]{2,1,0:T(1,128)} %get-tuple-element.24.picked_ref), calls=%async_computation | async-start | bytes 163840 | tf_op jit(solution)/shard_map/all_to_all | solution.py:579
  20.4 11.5 %collective-permute-start = (f32[64,128]{1,0:T(8,128)S(1)}, f32[64,128]{1,0:T(8,128)S(1)}, u32[]{:S(2)}, u32[]{:S(2)}) collective-permute-start(f32[64,128]{1,0:T(8,128)S(1)} %get-tuple-element.27), channel_id=1, source_target_pairs={{1,2},{2,1},{3,4},{4,3},{5,6},{6,5},{7,8},{8,7},{9,10},{10,9},{11,... | collective-permute-start | bytes 98312 | tf_op jit(solution)/shard_map/ppermute | solution.py:604
  30.0 3.1 %collective-permute-start.1 = (f32[64,128]{1,0:T(8,128)S(1)}, f32[64,128]{1,0:T(8,128)S(1)}, u32[]{:S(2)}, u32[]{:S(2)}) collective-permute-start(f32[64,128]{1,0:T(8,128)S(1)} %get-tuple-element.28), channel_id=1, source_target_pairs={{0,1},{1,0},{2,3},{3,2},{4,5},{5,4},{6,7},{7,6},{8,9},{9,8},{10,11... | collective-permute-start | bytes 98312 | tf_op jit(solution)/shard_map/ppermute | solution.py:605
  35.9 8.0 %copy-start.3 = (f32[32,128]{1,0:T(8,128)S(1)}, f32[32,128]{1,0:T(8,128)}, u32[]{:S(2)}) copy-start(f32[32,128]{1,0:T(8,128)} %diff_ref.3) | copy-start | bytes 49156
  36.7 10.2 %collective-permute-start.2 = (f32[136,128]{1,0:T(8,128)S(1)}, f32[136,128]{1,0:T(8,128)S(1)}, u32[]{:S(2)}, u32[]{:S(2)}) collective-permute-start(f32[136,128]{1,0:T(8,128)S(1)} %get-tuple-element.33), channel_id=1, source_target_pairs={{32,64},{64,32},{96,128},{128,96},{160,192},{192,160},{224,256},{2... | collective-permute-start | bytes 208904 | tf_op jit(solution)/shard_map/ppermute | solution.py:646
  41.9 6.2 %collective-permute-start.3 = (f32[136,128]{1,0:T(8,128)S(1)}, f32[136,128]{1,0:T(8,128)S(1)}, u32[]{:S(2)}, u32[]{:S(2)}) collective-permute-start(f32[136,128]{1,0:T(8,128)S(1)} %get-tuple-element.34), channel_id=1, source_target_pairs={{0,32},{32,0},{64,96},{96,64},{128,160},{160,128},{192,224},{224,1... | collective-permute-start | bytes 208904 | tf_op jit(solution)/shard_map/ppermute | solution.py:647

commit v9 on v8

--- a/solution.py
+++ b/solution.py
@@ -48,13 +48,15 @@
 
 
 def pick_kernel(
-    atm_hbm, rows_hbm, t_hbm, v_hbm, out_ref, t_ref, u_ref, atm_ref, rows_ref, sems,
+    atm_hbm, rows_hbm, t_hbm, v_hbm, out_hbm, t_ref, u_ref, v_rows, atm_ref, rows_ref, out_ref, sems,
 ):
+    last = t_ref.shape[2] - HALO
     copies = [
         pltpu.make_async_copy(atm_hbm, atm_ref, sems.at[0]),
         pltpu.make_async_copy(rows_hbm, rows_ref, sems.at[1]),
         pltpu.make_async_copy(t_hbm, t_ref, sems.at[2]),
         pltpu.make_async_copy(v_hbm.at[0], u_ref, sems.at[3]),
+        pltpu.make_async_copy(v_hbm.at[1, :, last:], v_rows, sems.at[4]),
     ]
     for copy in copies:
         copy.start()
@@ -78,17 +80,17 @@
     for f in range(1, 4):
         at = 128 + f * 128
         out_ref[:, 0, at : at + 128] = jnp.where(low, turn(values[f], -1, 0), turn(values[f], 1, 0))
+    copies.append(pltpu.make_async_copy(out_ref, out_hbm, sems.at[5]))
+    copies[-1].start()
     for copy in copies[2:]:
         copy.wait()
 
 
 def edge_kernel(
-    picked_ref, v_hbm, t_ref, u_ref, level_ref, height_ref, transport_ref, owner_ref, slot_ref, weight_ref, count_ref,
-    two_ref, one_ref, t_0_ref, rows_ref, pick_row_ref, pick_lane_ref, used_ref, v_rows, sem,
+    picked_ref, v_rows, t_ref, u_ref, level_ref, height_ref, transport_ref, owner_ref, slot_ref, weight_ref, count_ref,
+    two_ref, one_ref, t_0_ref, rows_ref, pick_row_ref, pick_lane_ref, used_ref,
 ):
     depth, rows, cols = t_ref.shape[1:]
-    copy = pltpu.make_async_copy(v_hbm.at[1, :, rows - HALO : rows], v_rows, sem)
-    copy.start()
     shape = (rows, cols)
     lane = lanes(shape)
     level = level_ref[...]
@@ -132,7 +134,6 @@
             at = c * depth + l
             rows_ref[0, at : at + 1] = t_ref[c, l, rows - 1 : rows]
             rows_ref[1, at : at + 1] = t_ref[c, l, 0:1]
-    copy.wait()
     for l in range(depth):
         at = 2 * depth + l
         rows_ref[0, at : at + 1] = v_rows[l, HALO - 1 : HALO]
@@ -278,7 +279,7 @@
 
 def tracer_kernel(
     two_ref, one_ref, t_0_ref, level_ref, diff_ref, t_ref, u_ref, v_hbm, x_ref, unit_ref, inv_rows_ref, gain_ref,
-    parts, rims, net_x, v_ref, inv_ref, sem,
+    parts, rims, net_x, v_ref, sem,
 ):
     depth, rows, cols = t_ref.shape[1:]
     copy = pltpu.make_async_copy(v_hbm.at[1], v_ref, sem)
@@ -325,45 +326,41 @@
             t_east = jnp.where(lane == last, rims[at], turn(t, -1, 1))
             flux_e = jnp.where(mask_e, u_l * (t + t_east), 0.0)
             net_x[at] = flux_e - jnp.where(lane == 0, rims[at], turn(flux_e, 1, 1))
+    copy.wait()
     diff = diff_ref[...]
     above = jnp.zeros(shape, F32)
-    inv = unit = None
+    inv = None
+    right = [None, None, None]
     for l in range(depth):
         below = jnp.where(level > l + 1, diff, 0.0) if l < depth - 1 else jnp.zeros(shape, F32)
         pivot = 1.0 + above + below
         if l > 0:
             pivot = pivot - above * above * inv
         inv = 1.0 / pivot
-        inv_ref[l] = inv
         inv_rows_ref[0, l : l + 1] = inv[rows - 1 : rows]
         inv_rows_ref[1, l : l + 1] = inv[0:1]
         gain_ref[l] = below * inv
-        unit = inv if l == 0 else above * unit * inv
-        unit_ref[l] = unit
-        above = below
-    for l in range(depth - 2, -1, -1):
-        unit = unit_ref[l] + gain_ref[l] * unit
-        unit_ref[l] = unit
-    copy.wait()
-    right = [None, None]
-    for l in range(depth):
-        above = jnp.where(level > l, diff, 0.0)
-        inv = inv_ref[l]
         mask_n = face_n > l
         v_l = v_ref[l] * 0.5
         for c in range(2):
             f = c * depth + l
+            at = slice(f * rows, (f + 1) * rows)
             t = t_ref[c, l]
             flux_n = jnp.where(mask_n, v_l * (t + turn(t, -1, 0)), 0.0)
             flux_s = turn(flux_n, 1, 0)
-            forced = t - adv_rate * (net_x[f * rows : (f + 1) * rows] + (flux_n - flux_s))
+            forced = t - adv_rate * (net_x[at] + (flux_n - flux_s))
             right[c] = forced * inv if l == 0 else (forced + above * right[c]) * inv
             x_ref[c, l] = right[c]
+        right[2] = inv if l == 0 else above * right[2] * inv
+        unit_ref[l] = right[2]
+        above = below
     for l in range(depth - 2, -1, -1):
         gain = gain_ref[l]
         for c in range(2):
             right[c] = x_ref[c, l] + gain * right[c]
             x_ref[c, l] = right[c]
+        right[2] = unit_ref[l] + gain * right[2]
+        unit_ref[l] = right[2]
 
 
 def step_kernel(
@@ -558,19 +555,21 @@
     depth, rows, cols = tracers.shape[1:]
     slots = send_rows.shape[3]
     block = (rows, cols)
-    picked, t_near, u_near = pl.pallas_call(
+    picked, t_near, u_near, v_rows = pl.pallas_call(
         pick_kernel,
         out_shape=(
             shape_of(n_lon, 1, 10 * slots),
             shape_of(2, depth, *block),
             shape_of(depth, *block),
+            shape_of(depth, HALO, cols),
         ),
         in_specs=[pl.BlockSpec(memory_space=pltpu.HBM)] * 4,
-        out_specs=vmem(3),
+        out_specs=[pl.BlockSpec(memory_space=pltpu.HBM)] + vmem(3),
         scratch_shapes=[
             pltpu.VMEM(atm_flux.shape, F32),
             pltpu.VMEM(send_rows.shape, jnp.int32),
-            pltpu.SemaphoreType.DMA((4,)),
+            pltpu.VMEM((n_lon, 1, 10 * slots), F32),
+            pltpu.SemaphoreType.DMA((6,)),
         ],
         compiler_params=params(24),
         cost_estimate=work(40),
@@ -590,14 +589,13 @@
             jax.ShapeDtypeStruct((4, *block), jnp.int32),
             shape_of(4, *block),
         ),
-        in_specs=[pl.BlockSpec(memory_space=pl.ANY), pl.BlockSpec(memory_space=pltpu.HBM)] + vmem(9),
+        in_specs=[pl.BlockSpec(memory_space=pl.ANY)] + vmem(10),
         out_specs=vmem(7),
-        scratch_shapes=[pltpu.VMEM((depth, HALO, cols), F32), pltpu.SemaphoreType.DMA],
         compiler_params=params(),
         cost_estimate=work(2),
         name="edges",
     )(
-        picked, in_hbm(velocity), t_near, u_near, ocean_levels, surface_height, transport, src_owner, src_slot,
+        picked, v_rows, t_near, u_near, ocean_levels, surface_height, transport, src_owner, src_slot,
         xgrid_weights, xgrid_count,
     )
     pairs = lon_pairs(n_lon)
@@ -614,7 +612,6 @@
             pltpu.VMEM((2 * depth * rows, 2 * cols), jnp.bfloat16),
             pltpu.VMEM((2 * depth * rows, cols), F32),
             pltpu.VMEM((2 * depth * rows, cols), F32),
-            pltpu.VMEM((depth, *block), F32),
             pltpu.VMEM((depth, *block), F32),
             pltpu.SemaphoreType.DMA,
         ],

time: 50.3 us -> 50.1 us (level)
  Pallas kernels: 9.06 us -> 7.72 us
  waiting for transfers between devices: 5.13 us -> 6.29 us
    all_to_all x1, waiting for transfers between devices: 2.77 us -> 3.61 us  [per_device(): lax.all_to_all(picked, 'lon', split_axis=0, concat_axis=0, tiled=True)]
    pallas_call x1, Pallas kernels: 1.36 us -> 0.53 us  [per_device(): pl.pallas_call(edge_kernel, out_shape=(shape_of(2 * rows, cols), shape_of...]
  transfers between devices with their start and end apart: 5 -> 5, of which waited for: 3 -> 3; matrix products, arithmetic and copies ran while one was open for 0% -> 0% of each run, Pallas kernels for 9% -> 7%
where the time goes in v9:
time: 50.1 us; the launch traced here: 49.7 us
  starting transfers between devices  34.8 us (69%)
  Pallas kernels  7.72 us (15%)
  waiting for transfers between devices  6.29 us (13%)
  between operations  0.84 us (2%)
    all_to_all x1, starting transfers between devices, per_device(): lax.all_to_all(picked, 'lon', split_axis=0, concat_axis=0, tiled=True)  16.3 us
    ppermute x1, starting transfers between devices, per_device(): two = lax.ppermute(two, 'lon', pairs[1])  9.55 us
    ppermute x1, starting transfers between devices, per_device(): second = lax.ppermute(second, ('lat', 'lon'), pairs[1])  5.15 us
    all_to_all x1, waiting for transfers between devices, per_device(): lax.all_to_all(picked, 'lon', split_axis=0, concat_axis=0, tiled=True)  3.61 us
    ppermute x1, starting transfers between devices, per_device(): one = lax.ppermute(one, 'lon', pairs[0])  1.92 us
    ppermute x1, starting transfers between devices, per_device(): first = lax.ppermute(first, ('lat', 'lon'), pairs[0])  1.92 us
    pallas_call x1, Pallas kernels, per_device(): pl.pallas_call(step_kernel, out_shape=(shape_of(2, depth, rows, cols), sh...  1.82 us
    pallas_call x1, Pallas kernels, per_device(): pl.pallas_call(pick_kernel, out_shape=(shape_of(n_lon, 1, 10 * slots), sh...  1.79 us
  transfers between devices with their start and end apart: 5, of which 3 were waited for; matrix products, arithmetic and copies ran while one was open for 0% of the time, Pallas kernels for 7%

profile of v9, /device:TPU:64, one launch (start us, length us, event | category | flops | bytes accessed | tf_op | source)
XLA Modules:
  0.0 49.7 jit_solution(18035091331506042359)
XLA Ops:
  0.6 0.0 copy-start.5
  0.6 0.0 copy-start.6
  0.7 1.8 %pick.1 = (f32[32,1,640]{2,1,0:T(1,128)}, f32[2,24,32,128]{3,2,1,0:T(8,128)S(1)}, f32[24,32,128]{2,1,0:T(8,128)S(1)}, f32[24,8,128]{2,1,0:T(8,128)S(1)}) custom-call(f32[1,4,512]{2,1,0:T(4,128)} %atm_hbm.1, s32[1,1,32,64]{3,2,1,0:T(8,128)} %rows_hbm.1, f32[2,24,32,128]{3,2,1,0:T(8,128)} %t_hbm.1, f32[2,24,32,128]{3,2,1,0:T(8,128)} %v_hbm.3), custom_call_target="tpu_custom_call" | custom-call | flops 40000000 | bytes 40000000 | tf_op jit(solution)/shard_map/pick/pallas_call | solution.py:558
  2.5 0.0 copy-start
  2.5 0.0 copy-start.1
  2.5 0.0 copy-start.2
  2.5 0.0 copy-start.4
  2.5 0.0 copy-start.7
  2.5 16.3 %all-to-all-start = ((f32[32,1,640]{2,1,0:T(1,128)}), f32[32,1,640]{2,1,0:T(1,128)S(1)}, u32[]{:S(2)}, u32[]{:S(2)}) async-start(f32[32,1,640]{2,1,0:T(1,128)} %get-tuple-element.25.picked_ref), calls=%async_computation | async-start | bytes 163840 | tf_op jit(solution)/shard_map/all_to_all | solution.py:578
  18.8 0.0 copy-done.5
  18.8 0.0 copy-done.6
  18.8 0.0 copy-done
  18.8 0.0 copy-done.1
  18.8 0.0 copy-done.2
  18.9 0.0 copy-done.4
  18.9 0.0 copy-done.7
  18.9 0.5 %edges.1 = (f32[64,128]{1,0:T(8,128)S(1)}, f32[64,128]{1,0:T(8,128)S(1)}, f32[32,128]{1,0:T(8,128)S(1)}, f32[2,72,128]{2,1,0:T(8,128)S(1)}, s32[4,32,128]{2,1,0:...) custom-call(f32[32,1,640]{2,1,0:T(1,128)} %get-tuple-element.25.picked_ref, ...), custom_call_target="tpu_custom_call" | custom-call | flops 2000000 | bytes 2000000 | tf_op jit(solution)/shard_map/edges/pallas_call | solution.py:581
  19.4 9.6 %collective-permute-start = (f32[64,128]{1,0:T(8,128)S(1)}, f32[64,128]{1,0:T(8,128)S(1)}, u32[]{:S(2)}, u32[]{:S(2)}) collective-permute-start(f32[64,128]{1,0:T(8,128)S(1)} %get-tuple-element.29), channel_id=1, source_target_pairs={{1,2},{2,1},{3,4},{4,3},{5,6},{6,5},{7,8},{8,7},{9,10},{10,9},{11,... | collective-permute-start | bytes 98312 | tf_op jit(solution)/shard_map/ppermute | solution.py:602
  29.0 1.9 %collective-permute-start.1 = (f32[64,128]{1,0:T(8,128)S(1)}, f32[64,128]{1,0:T(8,128)S(1)}, u32[]{:S(2)}, u32[]{:S(2)}) collective-permute-start(f32[64,128]{1,0:T(8,128)S(1)} %get-tuple-element.30), channel_id=1, source_target_pairs={{0,1},{1,0},{2,3},{3,2},{4,5},{5,4},{6,7},{7,6},{8,9},{9,8},{10,11... | collective-permute-start | bytes 98312 | tf_op jit(solution)/shard_map/ppermute | solution.py:603
  30.9 0.0 collective-permute-done.two_ref
  30.9 1.2 %collective-permute-done.1.one_ref = f32[64,128]{1,0:T(8,128)S(1)} collective-permute-done((f32[64,128]{1,0:T(8,128)S(1)}, f32[64,128]{1,0:T(8,128)S(1)}, u32[]{:S(2)}, u32[]{:S(2)}) %collective-permute-start.1) | collective-permute-done | bytes 32800 | tf_op jit(solution)/shard_map/ppermute | solution.py:603
  32.1 3.6 %all-to-all-done.table_ref = f32[32,1,640]{2,1,0:T(1,128)S(1)} async-done(((f32[32,1,640]{2,1,0:T(1,128)}), f32[32,1,640]{2,1,0:T(1,128)S(1)}, u32[]{:S(2)}, u32[]{:S(2)}) %all-to-all-start) | async-done | bytes 81952 | tf_op jit(solution)/shard_map/all_to_all | solution.py:578
  35.7 0.0 copy-start.3
  35.7 0.9 %rim_lookup.1 = (f32[136,128]{1,0:T(8,128)S(1)}, f32[136,128]{1,0:T(8,128)S(1)}, f32[2,3,8,128]{3,2,1,0:T(8,128)S(1)}, f32[2,3,8,128]{3,2,1,0:T(8,128)S(1)}, f32...) custom-call(f32[32,1,640]{2,1,0:T(1,128)S(1)} %all-to-all-done.table_ref, f32[64,128]{1,0:T(8,128)S(1)} %collective-permute-done.two_ref, ...), custom_call_target="tpu_custom_call" | custom-call | flops 8000000 | bytes 8000000 | tf_op jit(solution)/shard_map/rim_lookup/pallas_call | solution.py:623
  36.6 5.2 %collective-permute-start.2 = (f32[136,128]{1,0:T(8,128)S(1)}, f32[136,128]{1,0:T(8,128)S(1)}, u32[]{:S(2)}, u32[]{:S(2)}) collective-permute-start(f32[136,128]{1,0:T(8,128)S(1)} %get-tuple-element.35), channel_id=1, source_target_pairs={{32,64},{64,32},{96,128},{128,96},{160,192},{192,160},{224,256},{2... | collective-permute-start | bytes 208904 | tf_op jit(solution)/shard_map/ppermute | solution.py:643
  41.7 1.9 %collective-permute-start.3 = (f32[136,128]{1,0:T(8,128)S(1)}, f32[136,128]{1,0:T(8,128)S(1)}, u32[]{:S(2)}, u32[]{:S(2)}) collective-permute-start(f32[136,128]{1,0:T(8,128)S(1)} %get-tuple-element.36), channel_id=1, source_target_pairs={{0,32},{32,0},{64,96},{96,64},{128,160},{160,128},{192,224},{224,1... | collective-permute-start | bytes 208904 | tf_op jit(solution)/shard_map/ppermute | solution.py:644
  43.6 0.0 copy-done.3
  43.7 1.7 %tracers.1 = (f32[2,24,32,128]{3,2,1,0:T(8,128)S(1)}, f32[24,32,128]{2,1,0:T(8,128)S(1)}, f32[2,24,128]{2,1,0:T(8,128)S(1)}) custom-call(f32[64,128]{1,0:T(8,128)S(1)} %collective-permute-done.two_ref, f32[64,128]{1,0:T(8,128)S(1)} %collective-permute-done.1.one_ref, f32[32,128]{1,0:T(8,128)S(1)} %get-tuple-element.43.t_0_ref, s32[32,128]{1,0:T(8,128)S(1)} %copy-done.1, ...), custom_call_target="tpu_custom_call" | custom-call | flops 8000000 | bytes 8000000 | tf_op jit(solution)/shard_map/tracers/pallas_call | solution.py:605
  45.3 1.1 %lookup.1 = (f32[4,32,128]{2,1,0:T(8,128)S(1)}, f32[7,32,128]{2,1,0:T(8,128)S(1)}) custom-call(f32[2,3,8,128]{3,2,1,0:T(8,128)S(1)} %get-tuple-element.37.edge_flux_ref, f32[2,3,8,128]{3,2,1,0:T(8,128)S(1)} %get-tuple-element.38.edge_rim_ref, f32[4,16,128]{2,1,0:T(8,128)S(1)} %get-tuple-element.39.tab, f32[3,32,128]{2,1,0:T(8,128)S(1)} %get-tuple-element.40.side, ...), custom_call_target="tpu_custom_call" | custom-call | flops 8000000 | bytes 8000000 | tf_op jit(solution)/shard_map/lookup/pallas_call | solution.py:646
  46.4 0.0 collective-permute-done.2.second_ref
  46.4 1.5 %collective-permute-done.3.first_ref = f32[136,128]{1,0:T(8,128)S(1)} collective-permute-done((f32[136,128]{1,0:T(8,128)S(1)}, f32[136,128]{1,0:T(8,128)S(1)}, u32[]{:S(2)}, u32[]{:S(2)}) %collective-permute-start.3) | collective-permute-done | bytes 69664 | tf_op jit(solution)/shard_map/ppermute | solution.py:644
  47.9 1.8 %step.1 = (f32[2,24,32,128]{3,2,1,0:T(8,128)}, f32[32,128]{1,0:T(8,128)}, f32[2,32,128]{2,1,0:T(8,128)}) custom-call(f32[136,128]{1,0:T(8,128)S(1)} %collective-permute-done.2.second_ref, f32[136,128]{1,0:T(8,128)S(1)} %collective-permute-done.3.first_ref, f32[32,128]{1,0:T(8,128)S(1)} %copy-done.2, f32[2,32,128]{2,1,0:T(8,128)S(1)} %copy-done, ...), custom_call_target="tpu_custom_call" | custom-call | tf_op jit(solution)/shard_map/step/pallas_call | solution.py:656
Async XLA Ops:
  0.6 18.2 %copy-start.5 = (s32[4,32,128]{2,1,0:T(8,128)S(1)}, s32[4,32,128]{2,1,0:T(8,128)}, u32[]{:S(2)}) copy-start(s32[4,32,128]{2,1,0:T(8,128)} %slot_ref.1) | copy-start | bytes 196612
  0.6 18.2 %copy-start.6 = (f32[4,32,128]{2,1,0:T(8,128)S(1)}, f32[4,32,128]{2,1,0:T(8,128)}, u32[]{:S(2)}) copy-start(f32[4,32,128]{2,1,0:T(8,128)} %weight_ref.1) | copy-start | bytes 196612
  2.5 16.4 %copy-start = (f32[2,32,128]{2,1,0:T(8,128)S(1)}, f32[2,32,128]{2,1,0:T(8,128)}, u32[]{:S(2)}) copy-start(f32[2,32,128]{2,1,0:T(8,128)} %transport_ref.5) | copy-start | bytes 98308
  2.5 16.4 %copy-start.1 = (s32[32,128]{1,0:T(8,128)S(1)}, s32[32,128]{1,0:T(8,128)}, u32[]{:S(2)}) copy-start(s32[32,128]{1,0:T(8,128)} %level_ref.7) | copy-start | bytes 49156
  2.5 16.4 %copy-start.2 = (f32[32,128]{1,0:T(8,128)S(1)}, f32[32,128]{1,0:T(8,128)}, u32[]{:S(2)}) copy-start(f32[32,128]{1,0:T(8,128)} %height_ref.5) | copy-start | bytes 49156
  2.5 16.4 %copy-start.4 = (s32[4,32,128]{2,1,0:T(8,128)S(1)}, s32[4,32,128]{2,1,0:T(8,128)}, u32[]{:S(2)}) copy-start(s32[4,32,128]{2,1,0:T(8,128)} %owner_ref.1) | copy-start | bytes 196612
  2.5 16.4 %copy-start.7 = (s32[32,128]{1,0:T(8,128)S(1)}, s32[32,128]{1,0:T(8,128)}, u32[]{:S(2)}) copy-start(s32[32,128]{1,0:T(8,128)} %count_ref.1) | copy-start | bytes 49156
  2.5 33.2 %all-to-all-start = ((f32[32,1,640]{2,1,0:T(1,128)}), f32[32,1,640]{2,1,0:T(1,128)S(1)}, u32[]{:S(2)}, u32[]{:S(2)}) async-start(f32[32,1,640]{2,1,0:T(1,128)} %get-tuple-element.25.picked_ref), calls=%async_computation | async-start | bytes 163840 | tf_op jit(solution)/shard_map/all_to_all | solution.py:578
  19.4 11.5 %collective-permute-start = (f32[64,128]{1,0:T(8,128)S(1)}, f32[64,128]{1,0:T(8,128)S(1)}, u32[]{:S(2)}, u32[]{:S(2)}) collective-permute-start(f32[64,128]{1,0:T(8,128)S(1)} %get-tuple-element.29), channel_id=1, source_target_pairs={{1,2},{2,1},{3,4},{4,3},{5,6},{6,5},{7,8},{8,7},{9,10},{10,9},{11,... | collective-permute-start | bytes 98312 | tf_op jit(solution)/shard_map/ppermute | solution.py:602
  29.0 3.1 %collective-permute-start.1 = (f32[64,128]{1,0:T(8,128)S(1)}, f32[64,128]{1,0:T(8,128)S(1)}, u32[]{:S(2)}, u32[]{:S(2)}) collective-permute-start(f32[64,128]{1,0:T(8,128)S(1)} %get-tuple-element.30), channel_id=1, source_target_pairs={{0,1},{1,0},{2,3},{3,2},{4,5},{5,4},{6,7},{7,6},{8,9},{9,8},{10,11... | collective-permute-start | bytes 98312 | tf_op jit(solution)/shard_map/ppermute | solution.py:603
  35.7 8.0 %copy-start.3 = (f32[32,128]{1,0:T(8,128)S(1)}, f32[32,128]{1,0:T(8,128)}, u32[]{:S(2)}) copy-start(f32[32,128]{1,0:T(8,128)} %diff_ref.3) | copy-start | bytes 49156
  36.6 9.8 %collective-permute-start.2 = (f32[136,128]{1,0:T(8,128)S(1)}, f32[136,128]{1,0:T(8,128)S(1)}, u32[]{:S(2)}, u32[]{:S(2)}) collective-permute-start(f32[136,128]{1,0:T(8,128)S(1)} %get-tuple-element.35), channel_id=1, source_target_pairs={{32,64},{64,32},{96,128},{128,96},{160,192},{192,160},{224,256},{2... | collective-permute-start | bytes 208904 | tf_op jit(solution)/shard_map/ppermute | solution.py:643
  41.7 6.2 %collective-permute-start.3 = (f32[136,128]{1,0:T(8,128)S(1)}, f32[136,128]{1,0:T(8,128)S(1)}, u32[]{:S(2)}, u32[]{:S(2)}) collective-permute-start(f32[136,128]{1,0:T(8,128)S(1)} %get-tuple-element.36), channel_id=1, source_target_pairs={{0,32},{32,0},{64,96},{96,64},{128,160},{160,128},{192,224},{224,1... | collective-permute-start | bytes 208904 | tf_op jit(solution)/shard_map/ppermute | solution.py:644

commit v10 on v9

--- a/solution.py
+++ b/solution.py
@@ -206,7 +206,7 @@
 
 def rim_lookup_kernel(
     table_ref, two_ref, one_ref, pick_row_ref, pick_lane_ref, used_ref, rows_ref, level_ref, height_ref,
-    transport_ref, second_ref, first_ref, flux_ref, rim_ref, tab, side, pack,
+    transport_ref, after_ref, first_ref, second_ref, flux_ref, rim_ref, tab, side, pack,
 ):
     n_lon = table_ref.shape[0]
     half = n_lon // 2
@@ -243,15 +243,21 @@
         pack[s, ROW_T:] = rows_ref[s]
     even = is_even("lat")
     north_going, south_going = pack[0], pack[1]
+    first_ref[...] = jnp.where(even, north_going, south_going)
     second_ref[...] = jnp.where(even, south_going, north_going)
-    first_ref[...] = jnp.where(even, north_going, south_going)
+
+
+def sources(flux_ref, level_ref, cut):
+    wet = (level_ref[cut] > 0).astype(F32)
+    return heat_gain * flux_ref[0, cut] * wet, -salt_gain * flux_ref[1, cut] * wet
 
 
 def lookup_kernel(
     edge_flux_ref, edge_rim_ref, tab, side, two_ref, one_ref, pick_row_ref, pick_lane_ref, used_ref,
-    flux_ref, rim_ref,
+    level_ref, x_ref, unit_ref, flux_ref, rim_ref, t_out, fixed, sems,
 ):
     rows = used_ref.shape[1]
+    depth = x_ref.shape[1]
     cuts = [slice(at, at + HALO) for at in range(0, rows, HALO)]
     sides = [from_lon(one_ref, two_ref, cut) for cut in cuts]
     for at in range(1, len(cuts) - 1, 2):
@@ -263,6 +269,14 @@
                 flux_ref[f, cut] = found[f]
             for g, rim in enumerate(state_rims(*sides[at + i]) + side_rims[i]):
                 rim_ref[g, cut] = rim
+    mid = slice(HALO, rows - HALO)
+    source = sources(flux_ref, level_ref, mid)
+    copies = []
+    for c in range(2):
+        for l in range(depth):
+            fixed[c, l] = x_ref[c, l, mid] + unit_ref[l, mid] * source[c]
+        copies.append(pltpu.make_async_copy(fixed.at[c], t_out.at[c, :, mid], sems.at[c]))
+        copies[c].start()
     for s, at in ((0, len(cuts) - 1), (1, 0)):
         cut = cuts[at]
         flux_ref[0, cut] = own_lookup(tab, pick_row_ref, pick_lane_ref, used_ref, cut, (0,))[0]
@@ -270,6 +284,8 @@
             flux_ref[f + 1, cut] = edge_flux_ref[s, f]
         for g, rim in enumerate(state_rims(*sides[at]) + [edge_rim_ref[s, f] for f in range(3)]):
             rim_ref[g, cut] = rim
+    for copy in copies:
+        copy.wait()
 
 
 def split(x):
@@ -364,28 +380,21 @@
 
 
 def step_kernel(
-    second_ref, first_ref, height_ref, transport_ref, level_ref, diff_ref, flux_ref, rim_ref, rows_ref, inv_rows_ref,
-    x_ref, unit_ref, t_out, height_out, transport_out, north_ref, shift, fixed, result, sems,
+    first_ref, second_ref, height_ref, transport_ref, level_ref, diff_ref, flux_ref, rim_ref, rows_ref, inv_rows_ref,
+    x_ref, unit_ref, t_middle, t_out, height_out, transport_out, north_ref, shift, fixed, result, sems,
 ):
     top = is_top()
     level = level_ref[...]
     level_f = level.astype(F32)
     rows, cols = level.shape
     depth = x_ref.shape[1]
-    wet_0 = (level > 0).astype(F32)
-    source = (heat_gain * flux_ref[0] * wet_0, -salt_gain * flux_ref[1] * wet_0)
     lo, hi = slice(0, HALO), slice(rows - HALO, rows)
-    mid = slice(HALO, rows - HALO)
     copies = []
 
     def send(value, out):
         copies.append(pltpu.make_async_copy(value, out, sems.at[len(copies)]))
         copies[-1].start()
 
-    for c in range(2):
-        for l in range(depth):
-            fixed[c, l, mid] = x_ref[c, l, mid] + unit_ref[l, mid] * source[c][mid]
-        send(fixed.at[c, :, mid], t_out.at[c, :, mid])
     even = is_even("lat")
     a, b = first_ref[...], second_ref[...]
     south = jnp.where(even, b, a)
@@ -465,16 +474,17 @@
     across = (row_h == last) & top
     p_last = rows_of(p_h.shape) == HALO - 1
     for step in range(SUBSTEPS):
-        if step == 4:
+        if step == 3:
             row = rows_of((HALO, cols))
             for s, cut, at_row in ((0, hi, HALO - 1), (1, lo, 0)):
+                source = sources(flux_ref, level_ref, cut)
                 for c in range(2):
                     for l in range(depth):
                         at = c * depth + l
                         add = jnp.broadcast_to(shift[s, at : at + 1], (HALO, cols))
-                        x = x_ref[c, l, cut] + unit_ref[l, cut] * source[c][cut]
-                        fixed[c, l, cut] = x + jnp.where(row == at_row, add, 0.0)
-                send(fixed.at[:, :, cut], t_out.at[:, :, cut])
+                        x = x_ref[c, l, cut] + unit_ref[l, cut] * source[c]
+                        fixed[s, c, l] = x + jnp.where(row == at_row, add, 0.0)
+                send(fixed.at[s], t_out.at[:, :, cut])
         h = (h - wave_div * ((e - turn(e, 1, 1)) + (n - turn(n, 1, 0)))) * wet + fresh
         p_h = (p_h - wave_div * ((p_e - turn(p_e, -1, 1)) + (p_n - turn(p_n, 1, 0)))) * p_wet + p_fresh
         h_n = jnp.where(across, jnp.broadcast_to(p_h[HALO - 1 :], h.shape), turn(h, -1, 0))
@@ -620,7 +630,7 @@
         name="tracers",
     )(two, one, t_0, ocean_levels, diffusivity, t_near, u_near, in_hbm(velocity))
 
-    second, first, edge_flux, edge_rim, tab, side = pl.pallas_call(
+    first, second, edge_flux, edge_rim, tab, side = pl.pallas_call(
         rim_lookup_kernel,
         out_shape=(
             shape_of(lat_rows, cols),
@@ -630,7 +640,7 @@
             shape_of(4, n_lon // 2, 128),
             shape_of(3, n_lon, 128),
         ),
-        in_specs=vmem(10),
+        in_specs=vmem(10) + [pl.BlockSpec(memory_space=pl.ANY)],
         out_specs=vmem(6),
         scratch_shapes=[pltpu.VMEM((2, lat_rows, cols), F32)],
         compiler_params=params(),
@@ -638,38 +648,43 @@
         name="rim_lookup",
     )(
         table, two, one, pick_row, pick_lane, used, edge_rows, ocean_levels, surface_height, transport,
+        inv_rows,
     )
     pairs = lat_pairs(n_lat, n_lon)
+    first = lax.ppermute(first, ("lat", "lon"), pairs[0])
     second = lax.ppermute(second, ("lat", "lon"), pairs[1])
-    first = lax.ppermute(first, ("lat", "lon"), pairs[0])
-
-    flux, rim = pl.pallas_call(
+
+    flux, rim, t_middle = pl.pallas_call(
         lookup_kernel,
-        out_shape=(shape_of(4, *block), shape_of(FIELDS, *block)),
-        in_specs=vmem(9),
-        out_specs=vmem(2),
+        out_shape=(shape_of(4, *block), shape_of(FIELDS, *block), shape_of(2, depth, *block)),
+        in_specs=vmem(12),
+        out_specs=vmem(2) + [pl.BlockSpec(memory_space=pltpu.HBM)],
+        scratch_shapes=[pltpu.VMEM((2, depth, rows - 2 * HALO, cols), F32), pltpu.SemaphoreType.DMA((2,))],
         compiler_params=params(),
         cost_estimate=work(8),
         name="lookup",
-    )(edge_flux, edge_rim, tab, side, two, one, pick_row, pick_lane, used)
+    )(
+        edge_flux, edge_rim, tab, side, two, one, pick_row, pick_lane, used, ocean_levels, solved, unit,
+    )
 
     return pl.pallas_call(
         step_kernel,
         out_shape=(shape_of(2, depth, rows, cols), shape_of(rows, cols), shape_of(2, rows, cols)),
-        in_specs=vmem(12),
-        out_specs=(pl.BlockSpec(memory_space=pl.ANY),) * 3,
+        in_specs=vmem(12) + [pl.BlockSpec(memory_space=pltpu.HBM)],
+        out_specs=(pl.BlockSpec(memory_space=pltpu.HBM),) * 3,
+        input_output_aliases={12: 0},
         scratch_shapes=[
             pltpu.VMEM((lat_rows, cols), F32),
             pltpu.VMEM((2, 2 * depth, cols), F32),
-            pltpu.VMEM((2, depth, rows, cols), F32),
+            pltpu.VMEM((2, 2, depth, HALO, cols), F32),
             pltpu.VMEM((3, rows, cols), F32),
-            pltpu.SemaphoreType.DMA((6,)),
+            pltpu.SemaphoreType.DMA((4,)),
         ],
         compiler_params=params(),
         name="step",
     )(
-        second, first, surface_height, transport, ocean_levels, diffusivity, flux, rim, edge_rows, inv_rows,
-        solved, unit,
+        first, second, surface_height, transport, ocean_levels, diffusivity, flux, rim, edge_rows, inv_rows,
+        solved, unit, t_middle,
     )
 
 

time: 50.1 us -> 51.5 us (1.028)
  the two profiles are of different devices: /device:TPU:64 before, /device:TPU:120 now
where the time goes in v10:
time: 51.5 us; the launch traced here: 50.9 us
  starting transfers between devices  37.1 us (72%)
  Pallas kernels  8.28 us (16%)
  waiting for transfers between devices  4.6 us (9%)
  between operations  0.83 us (2%)
    all_to_all x1, starting transfers between devices, per_device(): lax.all_to_all(picked, 'lon', split_axis=0, concat_axis=0, tiled=True)  15.4 us
    ppermute x1, starting transfers between devices, per_device(): two = lax.ppermute(two, 'lon', pairs[1])  9.55 us
    ppermute x1, starting transfers between devices, per_device(): second = lax.ppermute(second, ('lat', 'lon'), pairs[1])  7.59 us
    ppermute x1, waiting for transfers between devices, per_device(): second = lax.ppermute(second, ('lat', 'lon'), pairs[1])  2.98 us
    ppermute x1, starting transfers between devices, per_device(): first = lax.ppermute(first, ('lat', 'lon'), pairs[0])  2.65 us
    ppermute x1, starting transfers between devices, per_device(): one = lax.ppermute(one, 'lon', pairs[0])  1.92 us
    pallas_call x1, Pallas kernels, per_device(): pl.pallas_call(pick_kernel, out_shape=(shape_of(n_lon, 1, 10 * slots), sh...  1.79 us
    pallas_call x1, Pallas kernels, per_device(): pl.pallas_call(step_kernel, out_shape=(shape_of(2, depth, rows, cols), sh...  1.75 us
  transfers between devices with their start and end apart: 5, of which 3 were waited for; matrix products, arithmetic and copies ran while one was open for 0% of the time, Pallas kernels for 8%

profile of v10, /device:TPU:120, one launch (start us, length us, event | category | flops | bytes accessed | tf_op | source)
XLA Modules:
  0.0 50.9 jit_solution(10905183159499023368)
XLA Ops:
  0.6 0.0 copy-start.5
  0.6 0.0 copy-start.6
  0.7 1.8 %pick.1 = (f32[32,1,640]{2,1,0:T(1,128)}, f32[2,24,32,128]{3,2,1,0:T(8,128)S(1)}, f32[24,32,128]{2,1,0:T(8,128)S(1)}, f32[24,8,128]{2,1,0:T(8,128)S(1)}) custom-call(f32[1,4,512]{2,1,0:T(4,128)} %atm_hbm.1, s32[1,1,32,64]{3,2,1,0:T(8,128)} %rows_hbm.1, f32[2,24,32,128]{3,2,1,0:T(8,128)} %t_hbm.1, f32[2,24,32,128]{3,2,1,0:T(8,128)} %v_hbm.3), custom_call_target="tpu_custom_call" | custom-call | flops 40000000 | bytes 40000000 | tf_op jit(solution)/shard_map/pick/pallas_call | solution.py:568
  2.5 0.0 copy-start
  2.5 0.0 copy-start.1
  2.5 0.0 copy-start.2
  2.5 0.0 copy-start.4
  2.5 0.0 copy-start.7
  2.5 15.4 %all-to-all-start = ((f32[32,1,640]{2,1,0:T(1,128)}), f32[32,1,640]{2,1,0:T(1,128)S(1)}, u32[]{:S(2)}, u32[]{:S(2)}) async-start(f32[32,1,640]{2,1,0:T(1,128)} %get-tuple-element.26.picked_ref), calls=%async_computation | async-start | bytes 163840 | tf_op jit(solution)/shard_map/all_to_all | solution.py:588
  17.9 0.0 copy-done.5
  17.9 0.0 copy-done.6
  17.9 0.0 copy-done
  17.9 0.0 copy-done.1
  17.9 0.0 copy-done.2
  18.0 0.0 copy-done.4
  18.0 0.0 copy-done.7
  18.0 0.0 copy-start.3
  18.0 0.5 %edges.1 = (f32[64,128]{1,0:T(8,128)S(1)}, f32[64,128]{1,0:T(8,128)S(1)}, f32[32,128]{1,0:T(8,128)S(1)}, f32[2,72,128]{2,1,0:T(8,128)S(1)}, s32[4,32,128]{2,1,0:...) custom-call(f32[32,1,640]{2,1,0:T(1,128)} %get-tuple-element.26.picked_ref, ...), custom_call_target="tpu_custom_call" | custom-call | flops 2000000 | bytes 2000000 | tf_op jit(solution)/shard_map/edges/pallas_call | solution.py:591
  18.5 9.6 %collective-permute-start = (f32[64,128]{1,0:T(8,128)S(1)}, f32[64,128]{1,0:T(8,128)S(1)}, u32[]{:S(2)}, u32[]{:S(2)}) collective-permute-start(f32[64,128]{1,0:T(8,128)S(1)} %get-tuple-element.30), channel_id=1, source_target_pairs={{1,2},{2,1},{3,4},{4,3},{5,6},{6,5},{7,8},{8,7},{9,10},{10,9},{11,... | collective-permute-start | bytes 98312 | tf_op jit(solution)/shard_map/ppermute | solution.py:612
  28.1 1.9 %collective-permute-start.1 = (f32[64,128]{1,0:T(8,128)S(1)}, f32[64,128]{1,0:T(8,128)S(1)}, u32[]{:S(2)}, u32[]{:S(2)}) collective-permute-start(f32[64,128]{1,0:T(8,128)S(1)} %get-tuple-element.31), channel_id=1, source_target_pairs={{0,1},{1,0},{2,3},{3,2},{4,5},{5,4},{6,7},{7,6},{8,9},{9,8},{10,11... | collective-permute-start | bytes 98312 | tf_op jit(solution)/shard_map/ppermute | solution.py:613
  30.0 1.2 %collective-permute-done.two_ref = f32[64,128]{1,0:T(8,128)S(1)} collective-permute-done((f32[64,128]{1,0:T(8,128)S(1)}, f32[64,128]{1,0:T(8,128)S(1)}, u32[]{:S(2)}, u32[]{:S(2)}) %collective-permute-start) | collective-permute-done | bytes 32800 | tf_op jit(solution)/shard_map/ppermute | solution.py:612
  31.3 0.0 collective-permute-done.1.one_ref
  31.3 0.0 copy-done.3
  31.3 1.6 %tracers.1 = (f32[2,24,32,128]{3,2,1,0:T(8,128)S(1)}, f32[24,32,128]{2,1,0:T(8,128)S(1)}, f32[2,24,128]{2,1,0:T(8,128)S(1)}) custom-call(f32[64,128]{1,0:T(8,128)S(1)} %collective-permute-done.two_ref, f32[64,128]{1,0:T(8,128)S(1)} %collective-permute-done.1.one_ref, f32[32,128]{1,0:T(8,128)S(1)} %get-tuple-element.36.t_0_ref, s32[32,128]{1,0:T(8,128)S(1)} %copy-done, ...), custom_call_target="tpu_custom_call" | custom-call | flops 8000000 | bytes 8000000 | tf_op jit(solution)/shard_map/tracers/pallas_call | solution.py:615
  32.9 0.4 all-to-all-done.table_ref
  33.3 0.9 %rim_lookup.1 = (f32[136,128]{1,0:T(8,128)S(1)}, f32[136,128]{1,0:T(8,128)S(1)}, f32[2,3,8,128]{3,2,1,0:T(8,128)S(1)}, f32[2,3,8,128]{3,2,1,0:T(8,128)S(1)}, f32...) custom-call(f32[32,1,640]{2,1,0:T(1,128)S(1)} %all-to-all-done.table_ref, f32[64,128]{1,0:T(8,128)S(1)} %collective-permute-done.two_ref, ...), custom_call_target="tpu_custom_call" | custom-call | flops 8000000 | bytes 8000000 | tf_op jit(solution)/shard_map/rim_lookup/pallas_call | solution.py:633
  34.2 2.7 %collective-permute-start.2 = (f32[136,128]{1,0:T(8,128)S(1)}, f32[136,128]{1,0:T(8,128)S(1)}, u32[]{:S(2)}, u32[]{:S(2)}) collective-permute-start(f32[136,128]{1,0:T(8,128)S(1)} %get-tuple-element.38), channel_id=1, source_target_pairs={{0,32},{32,0},{64,96},{96,64},{128,160},{160,128},{192,224},{224,1... | collective-permute-start | bytes 208904 | tf_op jit(solution)/shard_map/ppermute | solution.py:654
  36.8 7.6 %collective-permute-start.3 = (f32[136,128]{1,0:T(8,128)S(1)}, f32[136,128]{1,0:T(8,128)S(1)}, u32[]{:S(2)}, u32[]{:S(2)}) collective-permute-start(f32[136,128]{1,0:T(8,128)S(1)} %get-tuple-element.39), channel_id=1, source_target_pairs={{32,64},{64,32},{96,128},{128,96},{160,192},{192,160},{224,256},{2... | collective-permute-start | bytes 208904 | tf_op jit(solution)/shard_map/ppermute | solution.py:655
  44.4 1.7 %lookup.1 = (f32[4,32,128]{2,1,0:T(8,128)S(1)}, f32[7,32,128]{2,1,0:T(8,128)S(1)}, f32[2,24,32,128]{3,2,1,0:T(8,128)}) custom-call(f32[2,3,8,128]{3,2,1,0:T(8,128)S(1)} %get-tuple-element.40.edge_flux_ref, f32[2,3,8,128]{3,2,1,0:T(8,128)S(1)} %get-tuple-element.41.edge_rim_ref, f32[4,16,128]{2,1,0:T(8,128)S(1)} %get-tuple-element.42.tab, ...), custom_call_target="tpu_custom_call" | custom-call | flops 8000000 | bytes 8000000 | tf_op jit(solution)/shard_map/lookup/pallas_call | solution.py:657
  46.1 0.0 collective-permute-done.2.first_ref
  46.1 3.0 %collective-permute-done.3.second_ref = f32[136,128]{1,0:T(8,128)S(1)} collective-permute-done((f32[136,128]{1,0:T(8,128)S(1)}, f32[136,128]{1,0:T(8,128)S(1)}, u32[]{:S(2)}, u32[]{:S(2)}) %collective-permute-start.3) | collective-permute-done | bytes 69664 | tf_op jit(solution)/shard_map/ppermute | solution.py:655
  49.1 1.8 %step.1 = (f32[2,24,32,128]{3,2,1,0:T(8,128)}, f32[32,128]{1,0:T(8,128)}, f32[2,32,128]{2,1,0:T(8,128)}) custom-call(f32[136,128]{1,0:T(8,128)S(1)} %collective-permute-done.2.first_ref, f32[136,128]{1,0:T(8,128)S(1)} %collective-permute-done.3.second_ref, f32[32,128]{1,0:T(8,128)S(1)} %copy-done.2, ...), custom_call_target="tpu_custom_call", output_to_operand_aliasing={{0}: (12, {})} | custom-call | tf_op jit(solution)/shard_map/step/pallas_call | solution.py:670
Async XLA Ops:
  0.6 17.3 %copy-start.5 = (s32[4,32,128]{2,1,0:T(8,128)S(1)}, s32[4,32,128]{2,1,0:T(8,128)}, u32[]{:S(2)}) copy-start(s32[4,32,128]{2,1,0:T(8,128)} %slot_ref.1) | copy-start | bytes 196612
  0.6 17.3 %copy-start.6 = (f32[4,32,128]{2,1,0:T(8,128)S(1)}, f32[4,32,128]{2,1,0:T(8,128)}, u32[]{:S(2)}) copy-start(f32[4,32,128]{2,1,0:T(8,128)} %weight_ref.1) | copy-start | bytes 196612
  2.5 15.5 %copy-start = (s32[32,128]{1,0:T(8,128)S(1)}, s32[32,128]{1,0:T(8,128)}, u32[]{:S(2)}) copy-start(s32[32,128]{1,0:T(8,128)} %level_ref.9) | copy-start | bytes 49156
  2.5 15.5 %copy-start.1 = (f32[2,32,128]{2,1,0:T(8,128)S(1)}, f32[2,32,128]{2,1,0:T(8,128)}, u32[]{:S(2)}) copy-start(f32[2,32,128]{2,1,0:T(8,128)} %transport_ref.5) | copy-start | bytes 98308
  2.5 15.5 %copy-start.2 = (f32[32,128]{1,0:T(8,128)S(1)}, f32[32,128]{1,0:T(8,128)}, u32[]{:S(2)}) copy-start(f32[32,128]{1,0:T(8,128)} %height_ref.5) | copy-start | bytes 49156
  2.5 15.5 %copy-start.4 = (s32[4,32,128]{2,1,0:T(8,128)S(1)}, s32[4,32,128]{2,1,0:T(8,128)}, u32[]{:S(2)}) copy-start(s32[4,32,128]{2,1,0:T(8,128)} %owner_ref.1) | copy-start | bytes 196612
  2.5 15.5 %copy-start.7 = (s32[32,128]{1,0:T(8,128)S(1)}, s32[32,128]{1,0:T(8,128)}, u32[]{:S(2)}) copy-start(s32[32,128]{1,0:T(8,128)} %count_ref.1) | copy-start | bytes 49156
  2.5 30.8 %all-to-all-start = ((f32[32,1,640]{2,1,0:T(1,128)}), f32[32,1,640]{2,1,0:T(1,128)S(1)}, u32[]{:S(2)}, u32[]{:S(2)}) async-start(f32[32,1,640]{2,1,0:T(1,128)} %get-tuple-element.26.picked_ref), calls=%async_computation | async-start | bytes 163840 | tf_op jit(solution)/shard_map/all_to_all | solution.py:588
  18.0 13.3 %copy-start.3 = (f32[32,128]{1,0:T(8,128)S(1)}, f32[32,128]{1,0:T(8,128)}, u32[]{:S(2)}) copy-start(f32[32,128]{1,0:T(8,128)} %diff_ref.3) | copy-start | bytes 49156
  18.5 12.7 %collective-permute-start = (f32[64,128]{1,0:T(8,128)S(1)}, f32[64,128]{1,0:T(8,128)S(1)}, u32[]{:S(2)}, u32[]{:S(2)}) collective-permute-start(f32[64,128]{1,0:T(8,128)S(1)} %get-tuple-element.30), channel_id=1, source_target_pairs={{1,2},{2,1},{3,4},{4,3},{5,6},{6,5},{7,8},{8,7},{9,10},{10,9},{11,... | collective-permute-start | bytes 98312 | tf_op jit(solution)/shard_map/ppermute | solution.py:612
  28.1 3.2 %collective-permute-start.1 = (f32[64,128]{1,0:T(8,128)S(1)}, f32[64,128]{1,0:T(8,128)S(1)}, u32[]{:S(2)}, u32[]{:S(2)}) collective-permute-start(f32[64,128]{1,0:T(8,128)S(1)} %get-tuple-element.31), channel_id=1, source_target_pairs={{0,1},{1,0},{2,3},{3,2},{4,5},{5,4},{6,7},{7,6},{8,9},{9,8},{10,11... | collective-permute-start | bytes 98312 | tf_op jit(solution)/shard_map/ppermute | solution.py:613
  34.2 12.0 %collective-permute-start.2 = (f32[136,128]{1,0:T(8,128)S(1)}, f32[136,128]{1,0:T(8,128)S(1)}, u32[]{:S(2)}, u32[]{:S(2)}) collective-permute-start(f32[136,128]{1,0:T(8,128)S(1)} %get-tuple-element.38), channel_id=1, source_target_pairs={{0,32},{32,0},{64,96},{96,64},{128,160},{160,128},{192,224},{224,1... | collective-permute-start | bytes 208904 | tf_op jit(solution)/shard_map/ppermute | solution.py:654
  36.8 12.3 %collective-permute-start.3 = (f32[136,128]{1,0:T(8,128)S(1)}, f32[136,128]{1,0:T(8,128)S(1)}, u32[]{:S(2)}, u32[]{:S(2)}) collective-permute-start(f32[136,128]{1,0:T(8,128)S(1)} %get-tuple-element.39), channel_id=1, source_target_pairs={{32,64},{64,32},{96,128},{128,96},{160,192},{192,160},{224,256},{2... | collective-permute-start | bytes 208904 | tf_op jit(solution)/shard_map/ppermute | solution.py:655

commit v11 on v9

--- a/solution.py
+++ b/solution.py
@@ -460,6 +460,8 @@
     p_wet, p_grad, p_fresh, p_wind_e, p_wind_n = coefficients(fold)
     h, e, n = mine[HEIGHT], mine[EAST], mine[NORTH]
     p_h, p_e, p_n = fold[HEIGHT], fold[EAST], fold[NORTH]
+    e_w, grad_w, wet_w, wind_w = (turn(x, 1, 1) for x in (e, grad, wet, wind_e))
+    p_e_w, p_grad_w, p_wet_w, p_wind_w = (turn(x, -1, 1) for x in (p_e, p_grad, p_wet, p_wind_e))
     row_h = rows_of(h.shape)
     last = HALO + rows - 1
     across = (row_h == last) & top
@@ -475,14 +477,16 @@
                         x = x_ref[c, l, cut] + unit_ref[l, cut] * source[c][cut]
                         fixed[c, l, cut] = x + jnp.where(row == at_row, add, 0.0)
                 send(fixed.at[:, :, cut], t_out.at[:, :, cut])
-        h = (h - wave_div * ((e - turn(e, 1, 1)) + (n - turn(n, 1, 0)))) * wet + fresh
-        p_h = (p_h - wave_div * ((p_e - turn(p_e, -1, 1)) + (p_n - turn(p_n, 1, 0)))) * p_wet + p_fresh
+        h = (h - wave_div * ((e - e_w) + (n - turn(n, 1, 0)))) * wet + fresh
+        p_h = (p_h - wave_div * ((p_e - p_e_w) + (p_n - turn(p_n, 1, 0)))) * p_wet + p_fresh
         h_n = jnp.where(across, jnp.broadcast_to(p_h[HALO - 1 :], h.shape), turn(h, -1, 0))
         p_h_n = jnp.where(p_last, jnp.broadcast_to(h[last : last + 1], p_h.shape), turn(p_h, -1, 0))
         e = (e - grad * (turn(h, -1, 1) - h)) * wet + wind_e
         n = (n - grad * (h_n - h)) * wet + wind_n
         p_e = (p_e - p_grad * (turn(p_h, 1, 1) - p_h)) * p_wet + p_wind_e
         p_n = (p_n - p_grad * (p_h_n - p_h)) * p_wet + p_wind_n
+        e_w = (e_w - grad_w * (h - turn(h, 1, 1))) * wet_w + wind_w
+        p_e_w = (p_e_w - p_grad_w * (p_h - turn(p_h, -1, 1))) * p_wet_w + p_wind_w
     inside = slice(HALO, HALO + rows)
     result[0] = h[inside, :cols]
     result[1] = e[inside, :cols]

time: 50.1 us -> 49.9 us (level)
  no operation moved by 1% of the time
where the time goes in v11:
time: 49.9 us; the launch traced here: 49.5 us
  starting transfers between devices  34.8 us (70%)
  Pallas kernels  7.5 us (15%)
  waiting for transfers between devices  6.29 us (13%)
  between operations  0.84 us (2%)
    all_to_all x1, starting transfers between devices, per_device(): lax.all_to_all(picked, 'lon', split_axis=0, concat_axis=0, tiled=True)  16.3 us
    ppermute x1, starting transfers between devices, per_device(): two = lax.ppermute(two, 'lon', pairs[1])  9.55 us
    ppermute x1, starting transfers between devices, per_device(): second = lax.ppermute(second, ('lat', 'lon'), pairs[1])  5.15 us
    all_to_all x1, waiting for transfers between devices, per_device(): lax.all_to_all(picked, 'lon', split_axis=0, concat_axis=0, tiled=True)  3.61 us
    ppermute x1, starting transfers between devices, per_device(): one = lax.ppermute(one, 'lon', pairs[0])  1.92 us
    ppermute x1, starting transfers between devices, per_device(): first = lax.ppermute(first, ('lat', 'lon'), pairs[0])  1.92 us
    pallas_call x1, Pallas kernels, per_device(): pl.pallas_call(pick_kernel, out_shape=(shape_of(n_lon, 1, 10 * slots), sh...  1.79 us
    pallas_call x1, Pallas kernels, per_device(): pl.pallas_call(tracer_kernel, out_shape=(shape_of(2, depth, *block), shap...  1.66 us
  transfers between devices with their start and end apart: 5, of which 3 were waited for; matrix products, arithmetic and copies ran while one was open for 0% of the time, Pallas kernels for 7%

profile of v11, /device:TPU:64, one launch (start us, length us, event | category | flops | bytes accessed | tf_op | source)
XLA Modules:
  0.0 49.5 jit_solution(13914424273863831646)
XLA Ops:
  0.6 0.0 copy-start.5
  0.6 0.0 copy-start.6
  0.7 1.8 %pick.1 = (f32[32,1,640]{2,1,0:T(1,128)}, f32[2,24,32,128]{3,2,1,0:T(8,128)S(1)}, f32[24,32,128]{2,1,0:T(8,128)S(1)}, f32[24,8,128]{2,1,0:T(8,128)S(1)}) custom-call(f32[1,4,512]{2,1,0:T(4,128)} %atm_hbm.1, s32[1,1,32,64]{3,2,1,0:T(8,128)} %rows_hbm.1, f32[2,24,32,128]{3,2,1,0:T(8,128)} %t_hbm.1, f32[2,24,32,128]{3,2,1,0:T(8,128)} %v_hbm.3), custom_call_target="tpu_custom_call" | custom-call | flops 40000000 | bytes 40000000 | tf_op jit(solution)/shard_map/pick/pallas_call | solution.py:562
  2.5 0.0 copy-start
  2.5 0.0 copy-start.1
  2.5 0.0 copy-start.2
  2.5 0.0 copy-start.4
  2.5 0.0 copy-start.7
  2.5 16.3 %all-to-all-start = ((f32[32,1,640]{2,1,0:T(1,128)}), f32[32,1,640]{2,1,0:T(1,128)S(1)}, u32[]{:S(2)}, u32[]{:S(2)}) async-start(f32[32,1,640]{2,1,0:T(1,128)} %get-tuple-element.25.picked_ref), calls=%async_computation | async-start | bytes 163840 | tf_op jit(solution)/shard_map/all_to_all | solution.py:582
  18.8 0.0 copy-done.5
  18.8 0.0 copy-done.6
  18.8 0.0 copy-done
  18.8 0.0 copy-done.1
  18.8 0.0 copy-done.2
  18.9 0.0 copy-done.4
  18.9 0.0 copy-done.7
  18.9 0.5 %edges.1 = (f32[64,128]{1,0:T(8,128)S(1)}, f32[64,128]{1,0:T(8,128)S(1)}, f32[32,128]{1,0:T(8,128)S(1)}, f32[2,72,128]{2,1,0:T(8,128)S(1)}, s32[4,32,128]{2,1,0:...) custom-call(f32[32,1,640]{2,1,0:T(1,128)} %get-tuple-element.25.picked_ref, ...), custom_call_target="tpu_custom_call" | custom-call | flops 2000000 | bytes 2000000 | tf_op jit(solution)/shard_map/edges/pallas_call | solution.py:585
  19.4 9.6 %collective-permute-start = (f32[64,128]{1,0:T(8,128)S(1)}, f32[64,128]{1,0:T(8,128)S(1)}, u32[]{:S(2)}, u32[]{:S(2)}) collective-permute-start(f32[64,128]{1,0:T(8,128)S(1)} %get-tuple-element.29), channel_id=1, source_target_pairs={{1,2},{2,1},{3,4},{4,3},{5,6},{6,5},{7,8},{8,7},{9,10},{10,9},{11,... | collective-permute-start | bytes 98312 | tf_op jit(solution)/shard_map/ppermute | solution.py:606
  29.0 1.9 %collective-permute-start.1 = (f32[64,128]{1,0:T(8,128)S(1)}, f32[64,128]{1,0:T(8,128)S(1)}, u32[]{:S(2)}, u32[]{:S(2)}) collective-permute-start(f32[64,128]{1,0:T(8,128)S(1)} %get-tuple-element.30), channel_id=1, source_target_pairs={{0,1},{1,0},{2,3},{3,2},{4,5},{5,4},{6,7},{7,6},{8,9},{9,8},{10,11... | collective-permute-start | bytes 98312 | tf_op jit(solution)/shard_map/ppermute | solution.py:607
  30.9 0.0 collective-permute-done.two_ref
  30.9 1.2 %collective-permute-done.1.one_ref = f32[64,128]{1,0:T(8,128)S(1)} collective-permute-done((f32[64,128]{1,0:T(8,128)S(1)}, f32[64,128]{1,0:T(8,128)S(1)}, u32[]{:S(2)}, u32[]{:S(2)}) %collective-permute-start.1) | collective-permute-done | bytes 32800 | tf_op jit(solution)/shard_map/ppermute | solution.py:607
  32.1 3.6 %all-to-all-done.table_ref = f32[32,1,640]{2,1,0:T(1,128)S(1)} async-done(((f32[32,1,640]{2,1,0:T(1,128)}), f32[32,1,640]{2,1,0:T(1,128)S(1)}, u32[]{:S(2)}, u32[]{:S(2)}) %all-to-all-start) | async-done | bytes 81952 | tf_op jit(solution)/shard_map/all_to_all | solution.py:582
  35.7 0.0 copy-start.3
  35.7 0.9 %rim_lookup.1 = (f32[136,128]{1,0:T(8,128)S(1)}, f32[136,128]{1,0:T(8,128)S(1)}, f32[2,3,8,128]{3,2,1,0:T(8,128)S(1)}, f32[2,3,8,128]{3,2,1,0:T(8,128)S(1)}, f32...) custom-call(f32[32,1,640]{2,1,0:T(1,128)S(1)} %all-to-all-done.table_ref, f32[64,128]{1,0:T(8,128)S(1)} %collective-permute-done.two_ref, ...), custom_call_target="tpu_custom_call" | custom-call | flops 8000000 | bytes 8000000 | tf_op jit(solution)/shard_map/rim_lookup/pallas_call | solution.py:627
  36.6 5.2 %collective-permute-start.2 = (f32[136,128]{1,0:T(8,128)S(1)}, f32[136,128]{1,0:T(8,128)S(1)}, u32[]{:S(2)}, u32[]{:S(2)}) collective-permute-start(f32[136,128]{1,0:T(8,128)S(1)} %get-tuple-element.35), channel_id=1, source_target_pairs={{32,64},{64,32},{96,128},{128,96},{160,192},{192,160},{224,256},{2... | collective-permute-start | bytes 208904 | tf_op jit(solution)/shard_map/ppermute | solution.py:647
  41.7 1.9 %collective-permute-start.3 = (f32[136,128]{1,0:T(8,128)S(1)}, f32[136,128]{1,0:T(8,128)S(1)}, u32[]{:S(2)}, u32[]{:S(2)}) collective-permute-start(f32[136,128]{1,0:T(8,128)S(1)} %get-tuple-element.36), channel_id=1, source_target_pairs={{0,32},{32,0},{64,96},{96,64},{128,160},{160,128},{192,224},{224,1... | collective-permute-start | bytes 208904 | tf_op jit(solution)/shard_map/ppermute | solution.py:648
  43.6 0.0 copy-done.3
  43.7 1.7 %tracers.1 = (f32[2,24,32,128]{3,2,1,0:T(8,128)S(1)}, f32[24,32,128]{2,1,0:T(8,128)S(1)}, f32[2,24,128]{2,1,0:T(8,128)S(1)}) custom-call(f32[64,128]{1,0:T(8,128)S(1)} %collective-permute-done.two_ref, f32[64,128]{1,0:T(8,128)S(1)} %collective-permute-done.1.one_ref, f32[32,128]{1,0:T(8,128)S(1)} %get-tuple-element.43.t_0_ref, s32[32,128]{1,0:T(8,128)S(1)} %copy-done.1, ...), custom_call_target="tpu_custom_call" | custom-call | flops 8000000 | bytes 8000000 | tf_op jit(solution)/shard_map/tracers/pallas_call | solution.py:609
  45.3 1.1 %lookup.1 = (f32[4,32,128]{2,1,0:T(8,128)S(1)}, f32[7,32,128]{2,1,0:T(8,128)S(1)}) custom-call(f32[2,3,8,128]{3,2,1,0:T(8,128)S(1)} %get-tuple-element.37.edge_flux_ref, f32[2,3,8,128]{3,2,1,0:T(8,128)S(1)} %get-tuple-element.38.edge_rim_ref, f32[4,16,128]{2,1,0:T(8,128)S(1)} %get-tuple-element.39.tab, f32[3,32,128]{2,1,0:T(8,128)S(1)} %get-tuple-element.40.side, ...), custom_call_target="tpu_custom_call" | custom-call | flops 8000000 | bytes 8000000 | tf_op jit(solution)/shard_map/lookup/pallas_call | solution.py:650
  46.4 0.0 collective-permute-done.2.second_ref
  46.4 1.5 %collective-permute-done.3.first_ref = f32[136,128]{1,0:T(8,128)S(1)} collective-permute-done((f32[136,128]{1,0:T(8,128)S(1)}, f32[136,128]{1,0:T(8,128)S(1)}, u32[]{:S(2)}, u32[]{:S(2)}) %collective-permute-start.3) | collective-permute-done | bytes 69664 | tf_op jit(solution)/shard_map/ppermute | solution.py:648
  47.9 1.6 %step.1 = (f32[2,24,32,128]{3,2,1,0:T(8,128)}, f32[32,128]{1,0:T(8,128)}, f32[2,32,128]{2,1,0:T(8,128)}) custom-call(f32[136,128]{1,0:T(8,128)S(1)} %collective-permute-done.2.second_ref, f32[136,128]{1,0:T(8,128)S(1)} %collective-permute-done.3.first_ref, f32[32,128]{1,0:T(8,128)S(1)} %copy-done.2, f32[2,32,128]{2,1,0:T(8,128)S(1)} %copy-done, ...), custom_call_target="tpu_custom_call" | custom-call | tf_op jit(solution)/shard_map/step/pallas_call | solution.py:660
Async XLA Ops:
  0.6 18.2 %copy-start.5 = (s32[4,32,128]{2,1,0:T(8,128)S(1)}, s32[4,32,128]{2,1,0:T(8,128)}, u32[]{:S(2)}) copy-start(s32[4,32,128]{2,1,0:T(8,128)} %slot_ref.1) | copy-start | bytes 196612
  0.6 18.2 %copy-start.6 = (f32[4,32,128]{2,1,0:T(8,128)S(1)}, f32[4,32,128]{2,1,0:T(8,128)}, u32[]{:S(2)}) copy-start(f32[4,32,128]{2,1,0:T(8,128)} %weight_ref.1) | copy-start | bytes 196612
  2.5 16.4 %copy-start = (f32[2,32,128]{2,1,0:T(8,128)S(1)}, f32[2,32,128]{2,1,0:T(8,128)}, u32[]{:S(2)}) copy-start(f32[2,32,128]{2,1,0:T(8,128)} %transport_ref.5) | copy-start | bytes 98308
  2.5 16.4 %copy-start.1 = (s32[32,128]{1,0:T(8,128)S(1)}, s32[32,128]{1,0:T(8,128)}, u32[]{:S(2)}) copy-start(s32[32,128]{1,0:T(8,128)} %level_ref.7) | copy-start | bytes 49156
  2.5 16.4 %copy-start.2 = (f32[32,128]{1,0:T(8,128)S(1)}, f32[32,128]{1,0:T(8,128)}, u32[]{:S(2)}) copy-start(f32[32,128]{1,0:T(8,128)} %height_ref.5) | copy-start | bytes 49156
  2.5 16.4 %copy-start.4 = (s32[4,32,128]{2,1,0:T(8,128)S(1)}, s32[4,32,128]{2,1,0:T(8,128)}, u32[]{:S(2)}) copy-start(s32[4,32,128]{2,1,0:T(8,128)} %owner_ref.1) | copy-start | bytes 196612
  2.5 16.4 %copy-start.7 = (s32[32,128]{1,0:T(8,128)S(1)}, s32[32,128]{1,0:T(8,128)}, u32[]{:S(2)}) copy-start(s32[32,128]{1,0:T(8,128)} %count_ref.1) | copy-start | bytes 49156
  2.5 33.2 %all-to-all-start = ((f32[32,1,640]{2,1,0:T(1,128)}), f32[32,1,640]{2,1,0:T(1,128)S(1)}, u32[]{:S(2)}, u32[]{:S(2)}) async-start(f32[32,1,640]{2,1,0:T(1,128)} %get-tuple-element.25.picked_ref), calls=%async_computation | async-start | bytes 163840 | tf_op jit(solution)/shard_map/all_to_all | solution.py:582
  19.4 11.5 %collective-permute-start = (f32[64,128]{1,0:T(8,128)S(1)}, f32[64,128]{1,0:T(8,128)S(1)}, u32[]{:S(2)}, u32[]{:S(2)}) collective-permute-start(f32[64,128]{1,0:T(8,128)S(1)} %get-tuple-element.29), channel_id=1, source_target_pairs={{1,2},{2,1},{3,4},{4,3},{5,6},{6,5},{7,8},{8,7},{9,10},{10,9},{11,... | collective-permute-start | bytes 98312 | tf_op jit(solution)/shard_map/ppermute | solution.py:606
  29.0 3.1 %collective-permute-start.1 = (f32[64,128]{1,0:T(8,128)S(1)}, f32[64,128]{1,0:T(8,128)S(1)}, u32[]{:S(2)}, u32[]{:S(2)}) collective-permute-start(f32[64,128]{1,0:T(8,128)S(1)} %get-tuple-element.30), channel_id=1, source_target_pairs={{0,1},{1,0},{2,3},{3,2},{4,5},{5,4},{6,7},{7,6},{8,9},{9,8},{10,11... | collective-permute-start | bytes 98312 | tf_op jit(solution)/shard_map/ppermute | solution.py:607
  35.7 8.0 %copy-start.3 = (f32[32,128]{1,0:T(8,128)S(1)}, f32[32,128]{1,0:T(8,128)}, u32[]{:S(2)}) copy-start(f32[32,128]{1,0:T(8,128)} %diff_ref.3) | copy-start | bytes 49156
  36.6 9.8 %collective-permute-start.2 = (f32[136,128]{1,0:T(8,128)S(1)}, f32[136,128]{1,0:T(8,128)S(1)}, u32[]{:S(2)}, u32[]{:S(2)}) collective-permute-start(f32[136,128]{1,0:T(8,128)S(1)} %get-tuple-element.35), channel_id=1, source_target_pairs={{32,64},{64,32},{96,128},{128,96},{160,192},{192,160},{224,256},{2... | collective-permute-start | bytes 208904 | tf_op jit(solution)/shard_map/ppermute | solution.py:647
  41.7 6.2 %collective-permute-start.3 = (f32[136,128]{1,0:T(8,128)S(1)}, f32[136,128]{1,0:T(8,128)S(1)}, u32[]{:S(2)}, u32[]{:S(2)}) collective-permute-start(f32[136,128]{1,0:T(8,128)S(1)} %get-tuple-element.36), channel_id=1, source_target_pairs={{0,32},{32,0},{64,96},{96,64},{128,160},{160,128},{192,224},{224,1... | collective-permute-start | bytes 208904 | tf_op jit(solution)/shard_map/ppermute | solution.py:648

commit v12 on v11

--- a/solution.py
+++ b/solution.py
@@ -365,7 +365,7 @@
 
 def step_kernel(
     second_ref, first_ref, height_ref, transport_ref, level_ref, diff_ref, flux_ref, rim_ref, rows_ref, inv_rows_ref,
-    x_ref, unit_ref, t_out, height_out, transport_out, north_ref, shift, fixed, result, sems,
+    x_ref, unit_ref, t_out, height_out, transport_out, shift, fixed, result, sems,
 ):
     top = is_top()
     level = level_ref[...]
@@ -390,9 +390,9 @@
     a, b = first_ref[...], second_ref[...]
     south = jnp.where(even, b, a)
     north = jnp.where(even, a, b)
-    mirrored = jnp.take_along_axis(north, 127 - lanes(north.shape), axis=1)
-    north = jnp.where(top, mirrored, north)
-    north_ref[...] = north
+    used = ROW_T + 2 * depth
+    mirrored = jnp.take_along_axis(north[:used], 127 - lanes((used, cols)), axis=1)
+    north = jnp.where(top, mirrored, north[:used])
 
     first = LEVELS * HALO
     level_n = jnp.where(top, north[first + HALO - 1 : first + HALO], north[first : first + 1])
@@ -663,7 +663,6 @@
         in_specs=vmem(12),
         out_specs=(pl.BlockSpec(memory_space=pl.ANY),) * 3,
         scratch_shapes=[
-            pltpu.VMEM((lat_rows, cols), F32),
             pltpu.VMEM((2, 2 * depth, cols), F32),
             pltpu.VMEM((2, depth, rows, cols), F32),
             pltpu.VMEM((3, rows, cols), F32),

time: 49.9 us -> 49.9 us (level)
  no operation moved by 1% of the time
where the time goes in v12:
time: 49.9 us; the launch traced here: 49.5 us
  starting transfers between devices  34.8 us (70%)
  Pallas kernels  7.5 us (15%)
  waiting for transfers between devices  6.29 us (13%)
  between operations  0.84 us (2%)
    all_to_all x1, starting transfers between devices, per_device(): lax.all_to_all(picked, 'lon', split_axis=0, concat_axis=0, tiled=True)  16.3 us
    ppermute x1, starting transfers between devices, per_device(): two = lax.ppermute(two, 'lon', pairs[1])  9.55 us
    ppermute x1, starting transfers between devices, per_device(): second = lax.ppermute(second, ('lat', 'lon'), pairs[1])  5.15 us
    all_to_all x1, waiting for transfers between devices, per_device(): lax.all_to_all(picked, 'lon', split_axis=0, concat_axis=0, tiled=True)  3.61 us
    ppermute x1, starting transfers between devices, per_device(): one = lax.ppermute(one, 'lon', pairs[0])  1.92 us
    ppermute x1, starting transfers between devices, per_device(): first = lax.ppermute(first, ('lat', 'lon'), pairs[0])  1.92 us
    pallas_call x1, Pallas kernels, per_device(): pl.pallas_call(pick_kernel, out_shape=(shape_of(n_lon, 1, 10 * slots), sh...  1.79 us
    pallas_call x1, Pallas kernels, per_device(): pl.pallas_call(tracer_kernel, out_shape=(shape_of(2, depth, *block), shap...  1.66 us
  transfers between devices with their start and end apart: 5, of which 3 were waited for; matrix products, arithmetic and copies ran while one was open for 0% of the time, Pallas kernels for 7%

profile of v12, /device:TPU:64, one launch (start us, length us, event | category | flops | bytes accessed | tf_op | source)
XLA Modules:
  0.0 49.5 jit_solution(13914424273863831646)
XLA Ops:
  0.6 0.0 copy-start.5
  0.6 0.0 copy-start.6
  0.7 1.8 %pick.1 = (f32[32,1,640]{2,1,0:T(1,128)}, f32[2,24,32,128]{3,2,1,0:T(8,128)S(1)}, f32[24,32,128]{2,1,0:T(8,128)S(1)}, f32[24,8,128]{2,1,0:T(8,128)S(1)}) custom-call(f32[1,4,512]{2,1,0:T(4,128)} %atm_hbm.1, s32[1,1,32,64]{3,2,1,0:T(8,128)} %rows_hbm.1, f32[2,24,32,128]{3,2,1,0:T(8,128)} %t_hbm.1, f32[2,24,32,128]{3,2,1,0:T(8,128)} %v_hbm.3), custom_call_target="tpu_custom_call" | custom-call | flops 40000000 | bytes 40000000 | tf_op jit(solution)/shard_map/pick/pallas_call | solution.py:562
  2.5 0.0 copy-start
  2.5 0.0 copy-start.1
  2.5 0.0 copy-start.2
  2.5 0.0 copy-start.4
  2.5 0.0 copy-start.7
  2.5 16.3 %all-to-all-start = ((f32[32,1,640]{2,1,0:T(1,128)}), f32[32,1,640]{2,1,0:T(1,128)S(1)}, u32[]{:S(2)}, u32[]{:S(2)}) async-start(f32[32,1,640]{2,1,0:T(1,128)} %get-tuple-element.25.picked_ref), calls=%async_computation | async-start | bytes 163840 | tf_op jit(solution)/shard_map/all_to_all | solution.py:582
  18.8 0.0 copy-done.5
  18.8 0.0 copy-done.6
  18.8 0.0 copy-done
  18.8 0.0 copy-done.1
  18.8 0.0 copy-done.2
  18.9 0.0 copy-done.4
  18.9 0.0 copy-done.7
  18.9 0.5 %edges.1 = (f32[64,128]{1,0:T(8,128)S(1)}, f32[64,128]{1,0:T(8,128)S(1)}, f32[32,128]{1,0:T(8,128)S(1)}, f32[2,72,128]{2,1,0:T(8,128)S(1)}, s32[4,32,128]{2,1,0:...) custom-call(f32[32,1,640]{2,1,0:T(1,128)} %get-tuple-element.25.picked_ref, ...), custom_call_target="tpu_custom_call" | custom-call | flops 2000000 | bytes 2000000 | tf_op jit(solution)/shard_map/edges/pallas_call | solution.py:585
  19.4 9.6 %collective-permute-start = (f32[64,128]{1,0:T(8,128)S(1)}, f32[64,128]{1,0:T(8,128)S(1)}, u32[]{:S(2)}, u32[]{:S(2)}) collective-permute-start(f32[64,128]{1,0:T(8,128)S(1)} %get-tuple-element.29), channel_id=1, source_target_pairs={{1,2},{2,1},{3,4},{4,3},{5,6},{6,5},{7,8},{8,7},{9,10},{10,9},{11,... | collective-permute-start | bytes 98312 | tf_op jit(solution)/shard_map/ppermute | solution.py:606
  29.0 1.9 %collective-permute-start.1 = (f32[64,128]{1,0:T(8,128)S(1)}, f32[64,128]{1,0:T(8,128)S(1)}, u32[]{:S(2)}, u32[]{:S(2)}) collective-permute-start(f32[64,128]{1,0:T(8,128)S(1)} %get-tuple-element.30), channel_id=1, source_target_pairs={{0,1},{1,0},{2,3},{3,2},{4,5},{5,4},{6,7},{7,6},{8,9},{9,8},{10,11... | collective-permute-start | bytes 98312 | tf_op jit(solution)/shard_map/ppermute | solution.py:607
  30.9 0.0 collective-permute-done.two_ref
  30.9 1.2 %collective-permute-done.1.one_ref = f32[64,128]{1,0:T(8,128)S(1)} collective-permute-done((f32[64,128]{1,0:T(8,128)S(1)}, f32[64,128]{1,0:T(8,128)S(1)}, u32[]{:S(2)}, u32[]{:S(2)}) %collective-permute-start.1) | collective-permute-done | bytes 32800 | tf_op jit(solution)/shard_map/ppermute | solution.py:607
  32.1 3.6 %all-to-all-done.table_ref = f32[32,1,640]{2,1,0:T(1,128)S(1)} async-done(((f32[32,1,640]{2,1,0:T(1,128)}), f32[32,1,640]{2,1,0:T(1,128)S(1)}, u32[]{:S(2)}, u32[]{:S(2)}) %all-to-all-start) | async-done | bytes 81952 | tf_op jit(solution)/shard_map/all_to_all | solution.py:582
  35.7 0.0 copy-start.3
  35.7 0.9 %rim_lookup.1 = (f32[136,128]{1,0:T(8,128)S(1)}, f32[136,128]{1,0:T(8,128)S(1)}, f32[2,3,8,128]{3,2,1,0:T(8,128)S(1)}, f32[2,3,8,128]{3,2,1,0:T(8,128)S(1)}, f32...) custom-call(f32[32,1,640]{2,1,0:T(1,128)S(1)} %all-to-all-done.table_ref, f32[64,128]{1,0:T(8,128)S(1)} %collective-permute-done.two_ref, ...), custom_call_target="tpu_custom_call" | custom-call | flops 8000000 | bytes 8000000 | tf_op jit(solution)/shard_map/rim_lookup/pallas_call | solution.py:627
  36.6 5.2 %collective-permute-start.2 = (f32[136,128]{1,0:T(8,128)S(1)}, f32[136,128]{1,0:T(8,128)S(1)}, u32[]{:S(2)}, u32[]{:S(2)}) collective-permute-start(f32[136,128]{1,0:T(8,128)S(1)} %get-tuple-element.35), channel_id=1, source_target_pairs={{32,64},{64,32},{96,128},{128,96},{160,192},{192,160},{224,256},{2... | collective-permute-start | bytes 208904 | tf_op jit(solution)/shard_map/ppermute | solution.py:647
  41.7 1.9 %collective-permute-start.3 = (f32[136,128]{1,0:T(8,128)S(1)}, f32[136,128]{1,0:T(8,128)S(1)}, u32[]{:S(2)}, u32[]{:S(2)}) collective-permute-start(f32[136,128]{1,0:T(8,128)S(1)} %get-tuple-element.36), channel_id=1, source_target_pairs={{0,32},{32,0},{64,96},{96,64},{128,160},{160,128},{192,224},{224,1... | collective-permute-start | bytes 208904 | tf_op jit(solution)/shard_map/ppermute | solution.py:648
  43.6 0.0 copy-done.3
  43.7 1.7 %tracers.1 = (f32[2,24,32,128]{3,2,1,0:T(8,128)S(1)}, f32[24,32,128]{2,1,0:T(8,128)S(1)}, f32[2,24,128]{2,1,0:T(8,128)S(1)}) custom-call(f32[64,128]{1,0:T(8,128)S(1)} %collective-permute-done.two_ref, f32[64,128]{1,0:T(8,128)S(1)} %collective-permute-done.1.one_ref, f32[32,128]{1,0:T(8,128)S(1)} %get-tuple-element.43.t_0_ref, s32[32,128]{1,0:T(8,128)S(1)} %copy-done.1, ...), custom_call_target="tpu_custom_call" | custom-call | flops 8000000 | bytes 8000000 | tf_op jit(solution)/shard_map/tracers/pallas_call | solution.py:609
  45.3 1.1 %lookup.1 = (f32[4,32,128]{2,1,0:T(8,128)S(1)}, f32[7,32,128]{2,1,0:T(8,128)S(1)}) custom-call(f32[2,3,8,128]{3,2,1,0:T(8,128)S(1)} %get-tuple-element.37.edge_flux_ref, f32[2,3,8,128]{3,2,1,0:T(8,128)S(1)} %get-tuple-element.38.edge_rim_ref, f32[4,16,128]{2,1,0:T(8,128)S(1)} %get-tuple-element.39.tab, f32[3,32,128]{2,1,0:T(8,128)S(1)} %get-tuple-element.40.side, ...), custom_call_target="tpu_custom_call" | custom-call | flops 8000000 | bytes 8000000 | tf_op jit(solution)/shard_map/lookup/pallas_call | solution.py:650
  46.4 0.0 collective-permute-done.2.second_ref
  46.4 1.5 %collective-permute-done.3.first_ref = f32[136,128]{1,0:T(8,128)S(1)} collective-permute-done((f32[136,128]{1,0:T(8,128)S(1)}, f32[136,128]{1,0:T(8,128)S(1)}, u32[]{:S(2)}, u32[]{:S(2)}) %collective-permute-start.3) | collective-permute-done | bytes 69664 | tf_op jit(solution)/shard_map/ppermute | solution.py:648
  47.9 1.6 %step.1 = (f32[2,24,32,128]{3,2,1,0:T(8,128)}, f32[32,128]{1,0:T(8,128)}, f32[2,32,128]{2,1,0:T(8,128)}) custom-call(f32[136,128]{1,0:T(8,128)S(1)} %collective-permute-done.2.second_ref, f32[136,128]{1,0:T(8,128)S(1)} %collective-permute-done.3.first_ref, f32[32,128]{1,0:T(8,128)S(1)} %copy-done.2, f32[2,32,128]{2,1,0:T(8,128)S(1)} %copy-done, ...), custom_call_target="tpu_custom_call" | custom-call | tf_op jit(solution)/shard_map/step/pallas_call | solution.py:660
Async XLA Ops:
  0.6 18.2 %copy-start.5 = (s32[4,32,128]{2,1,0:T(8,128)S(1)}, s32[4,32,128]{2,1,0:T(8,128)}, u32[]{:S(2)}) copy-start(s32[4,32,128]{2,1,0:T(8,128)} %slot_ref.1) | copy-start | bytes 196612
  0.6 18.2 %copy-start.6 = (f32[4,32,128]{2,1,0:T(8,128)S(1)}, f32[4,32,128]{2,1,0:T(8,128)}, u32[]{:S(2)}) copy-start(f32[4,32,128]{2,1,0:T(8,128)} %weight_ref.1) | copy-start | bytes 196612
  2.5 16.4 %copy-start = (f32[2,32,128]{2,1,0:T(8,128)S(1)}, f32[2,32,128]{2,1,0:T(8,128)}, u32[]{:S(2)}) copy-start(f32[2,32,128]{2,1,0:T(8,128)} %transport_ref.5) | copy-start | bytes 98308
  2.5 16.4 %copy-start.1 = (s32[32,128]{1,0:T(8,128)S(1)}, s32[32,128]{1,0:T(8,128)}, u32[]{:S(2)}) copy-start(s32[32,128]{1,0:T(8,128)} %level_ref.7) | copy-start | bytes 49156
  2.5 16.4 %copy-start.2 = (f32[32,128]{1,0:T(8,128)S(1)}, f32[32,128]{1,0:T(8,128)}, u32[]{:S(2)}) copy-start(f32[32,128]{1,0:T(8,128)} %height_ref.5) | copy-start | bytes 49156
  2.5 16.4 %copy-start.4 = (s32[4,32,128]{2,1,0:T(8,128)S(1)}, s32[4,32,128]{2,1,0:T(8,128)}, u32[]{:S(2)}) copy-start(s32[4,32,128]{2,1,0:T(8,128)} %owner_ref.1) | copy-start | bytes 196612
  2.5 16.4 %copy-start.7 = (s32[32,128]{1,0:T(8,128)S(1)}, s32[32,128]{1,0:T(8,128)}, u32[]{:S(2)}) copy-start(s32[32,128]{1,0:T(8,128)} %count_ref.1) | copy-start | bytes 49156
  2.5 33.2 %all-to-all-start = ((f32[32,1,640]{2,1,0:T(1,128)}), f32[32,1,640]{2,1,0:T(1,128)S(1)}, u32[]{:S(2)}, u32[]{:S(2)}) async-start(f32[32,1,640]{2,1,0:T(1,128)} %get-tuple-element.25.picked_ref), calls=%async_computation | async-start | bytes 163840 | tf_op jit(solution)/shard_map/all_to_all | solution.py:582
  19.4 11.5 %collective-permute-start = (f32[64,128]{1,0:T(8,128)S(1)}, f32[64,128]{1,0:T(8,128)S(1)}, u32[]{:S(2)}, u32[]{:S(2)}) collective-permute-start(f32[64,128]{1,0:T(8,128)S(1)} %get-tuple-element.29), channel_id=1, source_target_pairs={{1,2},{2,1},{3,4},{4,3},{5,6},{6,5},{7,8},{8,7},{9,10},{10,9},{11,... | collective-permute-start | bytes 98312 | tf_op jit(solution)/shard_map/ppermute | solution.py:606
  29.0 3.1 %collective-permute-start.1 = (f32[64,128]{1,0:T(8,128)S(1)}, f32[64,128]{1,0:T(8,128)S(1)}, u32[]{:S(2)}, u32[]{:S(2)}) collective-permute-start(f32[64,128]{1,0:T(8,128)S(1)} %get-tuple-element.30), channel_id=1, source_target_pairs={{0,1},{1,0},{2,3},{3,2},{4,5},{5,4},{6,7},{7,6},{8,9},{9,8},{10,11... | collective-permute-start | bytes 98312 | tf_op jit(solution)/shard_map/ppermute | solution.py:607
  35.7 8.0 %copy-start.3 = (f32[32,128]{1,0:T(8,128)S(1)}, f32[32,128]{1,0:T(8,128)}, u32[]{:S(2)}) copy-start(f32[32,128]{1,0:T(8,128)} %diff_ref.3) | copy-start | bytes 49156
  36.6 9.8 %collective-permute-start.2 = (f32[136,128]{1,0:T(8,128)S(1)}, f32[136,128]{1,0:T(8,128)S(1)}, u32[]{:S(2)}, u32[]{:S(2)}) collective-permute-start(f32[136,128]{1,0:T(8,128)S(1)} %get-tuple-element.35), channel_id=1, source_target_pairs={{32,64},{64,32},{96,128},{128,96},{160,192},{192,160},{224,256},{2... | collective-permute-start | bytes 208904 | tf_op jit(solution)/shard_map/ppermute | solution.py:647
  41.7 6.2 %collective-permute-start.3 = (f32[136,128]{1,0:T(8,128)S(1)}, f32[136,128]{1,0:T(8,128)S(1)}, u32[]{:S(2)}, u32[]{:S(2)}) collective-permute-start(f32[136,128]{1,0:T(8,128)S(1)} %get-tuple-element.36), channel_id=1, source_target_pairs={{0,32},{32,0},{64,96},{96,64},{128,160},{160,128},{192,224},{224,1... | collective-permute-start | bytes 208904 | tf_op jit(solution)/shard_map/ppermute | solution.py:648
